TPU v7x, 256 devices: a whole 4x4x8 slice. The times are simulated.
256 devices in a mesh: frame: 4 (over x), cuts: 64 (over y, z, core).
Axes of the slice: x: 4, y: 4, z: 8, core: 2. Of those that a mesh axis runs over, the one named last changes fastest.
Arguments:
- measured: float32 [64, 64, 20, 8, 512], P('frame', 'cuts'), may hold values from -6 to 6
- coil_maps: float32 [64, 20, 8, 512], P('cuts'), may hold values from -2 to 2
- sampling: int32 [64, 256], P('frame'), may hold values from 0 to 1, as said below
Outputs:
- image: float32 [64, 64, 8, 512], P('frame', 'cuts')
Inputs may be any that keep to these rules, and one draw needn't show every extreme that they name: `sampling`: each frame samples between 32 and 64 of the 256 lines, always the 16 central ones; some frame samples exactly 64.
All inputs are finite; a program needn't handle non-finite values.
Results may differ from a plain program's by a relative error of at most 0.0003.
Values sent between devices are 32-bit elements; how exact they have to be, the bound alone decides.
No kernel may reach another device: no remote copies, remote signals or barrier semaphores. Data moves between devices by JAX's collectives and lax.ppermute only.
A program may use at most 128 MiB of HBM per device.

v0:
```python
import math

import jax
import jax.numpy as jnp
import numpy as np
from jax import lax
from jax.experimental import pallas as pl
from jax.experimental.pallas import tpu as pltpu
from jax.sharding import PartitionSpec as P

ITERS = 2


TAU = 0.25
SIGMA = 0.25
LAM_TIME = 0.2
LAM_SPACE = 0.1
EPSILON = 1e-06
KEEP = 1.0 / (1.0 + SIGMA)
TAKE = SIGMA / (1.0 + SIGMA)
AXES = ("frame", "cuts")
STEP = 4
VMEM_BYTES = 56 * 1024 * 1024
BF16 = jnp.bfloat16
F32 = jnp.float32


def split_table(table):
    high = table.astype(np.float32).astype(BF16)
    low = (table - high.astype(np.float64)).astype(np.float32).astype(BF16)
    return high, low


def block_table(cosine, sine):
    return np.concatenate(
        [np.concatenate([cosine, sine], 1), np.concatenate([-sine, cosine], 1)], 0
    )


def line_tables(positions):
    half = positions // 2
    lines = np.arange(half)[:, None]
    tables = {}
    for name, places in (("even", 2 * np.arange(half)), ("odd", 2 * np.arange(half) + 1)):
        angles = 2.0 * math.pi / positions * (lines * places[None, :] % positions)
        back = block_table(np.cos(angles), np.sin(angles)) / math.sqrt(positions)
        for key, table in (("back_" + name, back), ("fore_" + name, back.T)):
            high, low = split_table(table)
            tables[key] = np.concatenate([high, high, low], 0)
    return tables


def time_tables(frames_all, frames_here):
    index = np.arange(frames_all)
    angles = 2.0 * math.pi / frames_all * (index[:, None] * index[None, :] % frames_all)
    fore = block_table(np.cos(angles), np.sin(angles)) / math.sqrt(frames_all)
    rows = np.concatenate([np.arange(frames_here), frames_all + np.arange(frames_here)])
    back = fore.T[rows]
    out = []
    for table in (fore, back):
        high, low = split_table(table)
        out.append(np.concatenate([high, high, low], 1))
    return out


def parting_table(positions):
    table = np.zeros((positions, positions), np.float32)
    half = positions // 2
    table[2 * np.arange(half), np.arange(half)] = 1.0
    table[2 * np.arange(half) + 1, half + np.arange(half)] = 1.0
    return table


def parted(value):
    high = value.astype(BF16)
    return high, (value - high.astype(F32)).astype(BF16)


def product(value, table):
    high, low = parted(value)
    return jnp.dot(
        jnp.concatenate([high, low, high], -1), table, preferred_element_type=F32
    )


def left_product(table, value):
    high, low = parted(value)
    return jnp.dot(
        table, jnp.concatenate([high, low, high], 0), preferred_element_type=F32
    )


def moved(value, table):
    first = value.astype(BF16)
    rest = value - first.astype(F32)
    second = rest.astype(BF16)
    third = (rest - second.astype(F32)).astype(BF16)
    return sum(
        jnp.dot(piece, table, preferred_element_type=F32) for piece in (first, second, third)
    )


def quarters(value):
    size = value.shape[-1] // 4
    return [value[..., index * size : (index + 1) * size] for index in range(4)]


def cat(*pieces):
    return jnp.concatenate(pieces, -1)


def combine_coils(coil_fields, maps):
    re, im = coil_fields[..., :128], coil_fields[..., 128:]
    map_re, map_im = maps[..., :128], maps[..., 128:]
    return cat(
        jnp.sum(map_re * re + map_im * im, axis=0), jnp.sum(map_re * im - map_im * re, axis=0)
    )


def initial_kernel(
    measured_ref, maps_ref, sampling_ref, even_ref, odd_ref, part_ref,
    image_ref, image_x_ref, energy_ref, parted_ref, total_ref,
):
    step = pl.program_id(0)
    frames = measured_ref.shape[0]
    coils, readout, doubled = maps_ref.shape[1:]
    half, quarter = doubled // 2, doubled // 4
    rows = coils * readout

    @pl.when(step == 0)
    def _():
        maps = maps_ref[0].reshape(rows, doubled)
        re = moved(maps[:, :half], part_ref[...])
        im = moved(maps[:, half:], part_ref[...])
        parted_ref[...] = cat(
            re[:, :quarter], im[:, :quarter], re[:, quarter:], im[:, quarter:]
        ).reshape(coils, readout, doubled)
        total_ref[...] = jnp.zeros_like(total_ref)

    evens, odds = [], []
    for index in range(frames):
        data = measured_ref[index, 0].reshape(rows, doubled)
        weight = sampling_ref[pl.ds(step * frames + index, 1), :].astype(F32)
        low, high = weight[:, :quarter], weight[:, quarter:]
        re_low, re_high, im_low, im_high = quarters(data)
        re_low, re_high = re_low * low, re_high * high
        im_low, im_high = im_low * low, im_high * high
        evens.append(cat(re_low + re_high, im_low + im_high))
        odds.append(cat(re_low - re_high, im_low - im_high))
    evens = product(jnp.concatenate(evens, 0), even_ref[...])
    odds = product(jnp.concatenate(odds, 0), odd_ref[...])
    evens = evens.reshape(frames, coils, readout, half)
    odds = odds.reshape(frames, coils, readout, half)
    energy = total_ref[...]
    for index in range(frames):
        image = cat(
            combine_coils(evens[index], parted_ref[:, :, :half]),
            combine_coils(odds[index], parted_ref[:, :, half:]),
        )
        image_ref[step * frames + index] = image
        energy = energy + sum(piece * piece for piece in quarters(image))
    total_ref[...] = energy

    @pl.when(step == pl.num_programs(0) - 1)
    def _():
        energy_ref[...] = jnp.broadcast_to(jnp.sum(total_ref[...]), energy_ref.shape)
        image_x_ref[...] = jnp.swapaxes(image_ref[...], 0, 1)


def normal_kernel(
    image_ref, maps_ref, sampling_ref, fore_even_ref, fore_odd_ref, even_ref, odd_ref,
    out_ref,
):
    step = pl.program_id(0)
    frames = image_ref.shape[0]
    coils, readout, doubled = maps_ref.shape
    half, quarter = doubled // 2, doubled // 4
    rows = coils * readout

    def lines(offset, table_ref):
        pieces = []
        for index in range(frames):
            re = image_ref[index, :, offset : offset + quarter][None]
            im = image_ref[index, :, offset + quarter : offset + half][None]
            map_re = maps_ref[:, :, offset : offset + quarter]
            map_im = maps_ref[:, :, offset + quarter : offset + half]
            pieces.append(
                cat(map_re * re - map_im * im, map_re * im + map_im * re).reshape(rows, half)
            )
        return product(jnp.concatenate(pieces, 0), table_ref[...])

    from_even = lines(0, fore_even_ref)
    from_odd = lines(half, fore_odd_ref)
    low = from_even + from_odd
    high = from_even - from_odd
    evens, odds = [], []
    for index in range(frames):
        weight = sampling_ref[pl.ds(step * frames + index, 1), :].astype(F32)
        weight_low = cat(weight[:, :quarter], weight[:, :quarter])
        weight_high = cat(weight[:, quarter:], weight[:, quarter:])
        kept_low = low[index * rows : (index + 1) * rows] * weight_low
        kept_high = high[index * rows : (index + 1) * rows] * weight_high
        evens.append(kept_low + kept_high)
        odds.append(kept_low - kept_high)
    evens = product(jnp.concatenate(evens, 0), even_ref[...])
    odds = product(jnp.concatenate(odds, 0), odd_ref[...])
    evens = evens.reshape(frames, coils, readout, half)
    odds = odds.reshape(frames, coils, readout, half)
    for index in range(frames):
        out_ref[index] = cat(
            combine_coils(evens[index], maps_ref[:, :, :half]),
            combine_coils(odds[index], maps_ref[:, :, half:]),
        )


def frequencies(blocks, x, table):
    parts = [quarters(block[x]) for block in blocks]
    re = jnp.concatenate([cat(part[0], part[2]) for part in parts], 0)
    im = jnp.concatenate([cat(part[1], part[3]) for part in parts], 0)
    return left_product(table, jnp.concatenate([re, im], 0))


def frequency_kernel(own_ref, one_ref, two_ref, three_ref, table_ref, out_ref):
    for x in range(own_ref.shape[0]):
        out_ref[x] = frequencies((own_ref, one_ref, two_ref, three_ref), x, table_ref[...])


def level(energy_ref, cells):
    total = jnp.sum(energy_ref[...], axis=0, keepdims=True)
    return jnp.sqrt(total / cells + EPSILON)


def clip_time(dual, limit):
    size = dual.shape[0] // 2
    re, im = dual[:size], dual[size:]
    scale = jnp.minimum(1.0, limit * lax.rsqrt(re * re + im * im))
    return jnp.concatenate([re * scale, im * scale], 0)


def frames_of(dual, table):
    field = left_product(table, dual)
    size, half = field.shape[0] // 2, field.shape[1] // 2
    re, im = field[:size], field[size:]
    return cat(re[:, :half], im[:, :half], re[:, half:], im[:, half:])


def later_lines(field):
    re_even, im_even, re_odd, im_odd = quarters(field)
    size = re_even.shape[-1]
    last = lax.broadcasted_iota(jnp.int32, re_even.shape, 1) == size - 1

    def rolled(piece):
        return jnp.where(last, 0.0, pltpu.roll(piece, size - 1, 1))

    return cat(re_odd, im_odd, rolled(re_even), rolled(im_even))


def earlier_lines(field):
    re_even, im_even, re_odd, im_odd = quarters(field)
    first = lax.broadcasted_iota(jnp.int32, re_even.shape, 1) == 0

    def rolled(piece):
        return jnp.where(first, 0.0, pltpu.roll(piece, 1, 1))

    return cat(rolled(re_odd), rolled(im_odd), re_even, im_even)


def clip_space(components, limit):
    re_even, im_even, re_odd, im_odd = (
        sum(piece * piece for piece in pieces)
        for pieces in zip(*(quarters(component) for component in components))
    )
    even = jnp.minimum(1.0, limit * lax.rsqrt(re_even + im_even))
    odd = jnp.minimum(1.0, limit * lax.rsqrt(re_odd + im_odd))
    scale = cat(even, even, odd, odd)
    return [component * scale for component in components]


def space_step(field, above, x, old, limit):
    readout = field.shape[0]
    here = field[x]
    further = field[x + 1] if x + 1 < readout else jnp.zeros_like(here)
    increments = (above[x] - here, further - here, later_lines(here) - here)
    if old is None:
        duals = [SIGMA * increment for increment in increments]
    else:
        duals = [
            old[index, x] + SIGMA * increment for index, increment in enumerate(increments)
        ]
    return clip_space(duals, limit)


def space_part(own, above, below, x, rows_before, has_below, old, old_below, limit):
    duals = space_step(own, above, x, old, limit)
    duals_below = space_step(below, own, x, old_below, limit)
    total = has_below * duals_below[0] - duals[0]
    total = total + (rows_before - duals[1])
    total = total + (earlier_lines(duals[2]) - duals[2])
    return total, duals, duals_below


def first_kernel(
    cells, energy_ref, flag_ref, own_ref, above_ref, below_ref, normal_ref, frequency_ref,
    table_ref,
    base_ref, bar_x_ref, bar_ref, time_ref, space_ref, space_below_ref,
):
    rms_level = level(energy_ref, cells)
    limit_time, limit_space = LAM_TIME * rms_level, LAM_SPACE * rms_level
    limit_wide = cat(limit_time, limit_time)
    has_below = flag_ref[0, 0]
    normal = jnp.swapaxes(normal_ref[...], 0, 1)
    rows_before = jnp.zeros(own_ref.shape[1:], F32)
    bars = []
    for x in range(own_ref.shape[0]):
        dual = clip_time(SIGMA * frequency_ref[x], limit_wide)
        time_ref[x] = dual
        total, duals, duals_below = space_part(
            own_ref, above_ref, below_ref, x, rows_before, has_below, None, None, limit_space
        )
        rows_before = duals[1]
        for index in range(3):
            space_ref[index, x] = duals[index]
            space_below_ref[index, x] = duals_below[index]
        initial = own_ref[x]
        data_part = TAKE * (normal[x] - initial)
        updated = initial - TAU * (data_part + frames_of(dual, table_ref[...]) + total)
        base_ref[x] = updated - TAU * (KEEP * data_part - TAKE * initial)
        bar = 2.0 * updated - initial
        bar_x_ref[x] = bar
        bars.append(bar)
    bar_ref[...] = jnp.swapaxes(jnp.stack(bars, 0), 0, 1)


def space_kernel(
    cells, energy_ref, flag_ref, own_ref, above_ref, below_ref, normal_ref, base_ref,
    space_ref, space_below_ref,
    out_ref,
):
    limit_space = LAM_SPACE * level(energy_ref, cells)
    has_below = flag_ref[0, 0]
    normal = jnp.swapaxes(normal_ref[...], 0, 1)
    rows_before = jnp.zeros(own_ref.shape[1:], F32)
    for x in range(own_ref.shape[0]):
        total, duals, _ = space_part(
            own_ref, above_ref, below_ref, x, rows_before, has_below,
            space_ref, space_below_ref, limit_space,
        )
        rows_before = duals[1]
        out_ref[x] = base_ref[x] - TAU * (TAKE * normal[x] + total)


def last_kernel(
    cells, energy_ref, own_ref, one_ref, two_ref, three_ref, time_ref, base_ref,
    fore_ref, back_ref, part_ref,
    out_ref,
):
    limit_time = LAM_TIME * level(energy_ref, cells)
    limit_wide = cat(limit_time, limit_time)
    blocks = (own_ref, one_ref, two_ref, three_ref)
    images = []
    for x in range(own_ref.shape[0]):
        dual = time_ref[x] + SIGMA * frequencies(blocks, x, fore_ref[...])
        field = frames_of(clip_time(dual, limit_wide), back_ref[...])
        images.append(base_ref[x] - TAU * field)
    count, size = len(images), images[0].shape[0]
    image = jnp.concatenate(images, 0)
    re_even, im_even, re_odd, im_odd = quarters(image)
    image = cat(
        moved(cat(re_even, re_odd), part_ref[...]), moved(cat(im_even, im_odd), part_ref[...])
    )
    out_ref[:, 0] = jnp.swapaxes(image.reshape(count, size, image.shape[-1]), 0, 1)


def params():
    return pltpu.CompilerParams(vmem_limit_bytes=VMEM_BYTES)


def cost(flops, moved_bytes):
    return pl.CostEstimate(flops=flops, bytes_accessed=moved_bytes, transcendentals=0)


def whole(array):
    return pl.BlockSpec(array.shape, lambda step: (0,) * array.ndim)


def struct(*shape):
    return jax.ShapeDtypeStruct(shape, F32)


def shards(measured, coil_maps, sampling):
    frames_here, slices_here, coils, readout, doubled = measured.shape
    positions = doubled // 2
    blocks = lax.axis_size("frame")
    slices_all = slices_here * lax.axis_size("cuts")
    frames_all = frames_here * blocks
    devices = blocks * lax.axis_size("cuts")
    cells = float(frames_all * slices_all * readout * positions)
    lines = {key: jnp.asarray(table) for key, table in line_tables(positions).items()}
    time_fore, time_back = (jnp.asarray(table) for table in time_tables(frames_all, frames_here))
    parting = parting_table(positions)
    part, unpart = jnp.asarray(parting, BF16), jnp.asarray(parting.T, BF16)
    plane = (readout, frames_here, doubled)
    turned = (frames_here, readout, doubled)
    rows = frames_here * coils * readout

    even, odd = lines["back_even"], lines["back_odd"]
    initial, initial_x, energy, maps = pl.pallas_call(
        initial_kernel,
        grid=(frames_here // STEP,),
        in_specs=[
            pl.BlockSpec((STEP,) + measured.shape[1:], lambda step: (step, 0, 0, 0, 0)),
            whole(coil_maps), whole(sampling), whole(even), whole(odd), whole(part),
        ],
        out_specs=[
            whole(struct(*turned)), whole(struct(*plane)), whole(struct(devices, 128)),
            whole(struct(coils, readout, doubled)),
        ],
        out_shape=[
            struct(*turned), struct(*plane), struct(devices, 128),
            struct(coils, readout, doubled),
        ],
        scratch_shapes=[pltpu.VMEM((readout, 128), F32)],
        compiler_params=params(),
        cost_estimate=cost(6 * rows * doubled * positions, measured.size * 4),
    )(measured, coil_maps, sampling, even, odd, part)

    energies = lax.all_to_all(energy, AXES, 0, 0, tiled=True)

    def normal(image):
        tables = [lines[key] for key in ("fore_even", "fore_odd", "back_even", "back_odd")]
        return pl.pallas_call(
            normal_kernel,
            grid=(frames_here // STEP,),
            in_specs=[
                pl.BlockSpec((STEP, readout, doubled), lambda step: (step, 0, 0)),
                whole(maps), whole(sampling),
            ] + [whole(table) for table in tables],
            out_specs=pl.BlockSpec((STEP, readout, doubled), lambda step: (step, 0, 0)),
            out_shape=struct(*turned),
            compiler_params=params(),
            cost_estimate=cost(12 * rows * doubled * positions, image.size * 8),
        )(image, maps, sampling, *tables)

    def gathered(image):
        others = [
            lax.ppermute(
                image, "frame", [((index + by) % blocks, index) for index in range(blocks)]
            )
            for by in range(1, blocks)
        ]
        return [image] + others

    def neighbours(image):
        count = lax.axis_size("cuts")
        above = lax.ppermute(image, "cuts", [(i + 1, i) for i in range(count - 1)])
        below = lax.ppermute(image, "cuts", [(i, i + 1) for i in range(count - 1)])
        return above, below

    flag = (lax.axis_index("cuts") > 0).astype(F32).reshape(1, 1)
    smem = pl.BlockSpec(memory_space=pltpu.SMEM)
    vmem = pl.BlockSpec(memory_space=pltpu.VMEM)

    def call(kernel, args, out_shape, flops):
        specs = [smem if arg is flag else vmem for arg in args]
        return pl.pallas_call(
            kernel,
            in_specs=specs,
            out_specs=jax.tree.map(lambda _: vmem, out_shape),
            out_shape=out_shape,
            compiler_params=params(),
            cost_estimate=cost(flops, sum(arg.size * 4 for arg in args)),
        )(*args)

    time_flops = 6 * (2 * frames_all) ** 2 * readout * positions
    all_blocks = gathered(initial_x)
    above, below = neighbours(initial_x)
    normal_initial = normal(initial)
    frequency_shape = struct(readout, 2 * frames_all, positions)
    frequency = call(frequency_kernel, all_blocks + [time_fore], frequency_shape, time_flops)
    duals_shape = struct(3, *plane)

    def first(*refs):
        first_kernel(cells, *refs)

    def space(*refs):
        space_kernel(cells, *refs)

    def last(*refs):
        last_kernel(cells, *refs)

    base, bar_x, bar, time_dual, space_dual, space_below = call(
        first,
        [energies, flag, initial_x, above, below, normal_initial, frequency, time_back],
        [struct(*plane), struct(*plane), struct(*turned), frequency_shape, duals_shape, duals_shape],
        time_flops // 4,
    )
    all_blocks = gathered(bar_x)
    above, below = neighbours(bar_x)
    normal_bar = normal(bar)
    base = call(
        space,
        [energies, flag, bar_x, above, below, normal_bar, base, space_dual, space_below],
        struct(*plane),
        1000000,
    )
    return call(
        last,
        [energies] + all_blocks + [time_dual, base, time_fore, time_back, unpart],
        struct(frames_here, slices_here, readout, doubled),
        time_flops,
    )


def solution(mesh):
    placed = (P("frame", "cuts", None, None, None), P("cuts", None, None, None), P("frame", None))
    return jax.shard_map(
        shards,
        mesh=mesh,
        in_specs=placed,
        out_specs=P("frame", "cuts", None, None),
        check_vma=False,
    )
```

profile of v0, /device:TPU:24, one launch (start us, length us, event | category | flops | bytes accessed | tf_op | source)
XLA Modules:
  0.0 77.9 jit_solution(17251226130089792741)
XLA Ops:
  0.0 6.6 %shard_map.109 = (f32[16,8,512]{2,1,0:T(8,128)}, f32[8,16,512]{2,1,0:T(8,128)}, f32[256,128]{1,0:T(8,128)}, f32[20,8,512]{2,1,0:T(8,128)}) custom-call(f32[16,1,20,8,512]{4,3,2,1,0:T(8,128)} %measured_ref.1, f32[1,20,8,512]{3,2,1,0:T(8,128)} %maps_ref.1, s32[16,256]{1,0:T(8,128)} %sampling_ref.5, bf16[768,256]{1,0:T(8,128)(2,1)} %constant.22.clone.even_ref, ...), custom_call_target="tpu_custom_call" | custom-call | flops 2013265920 | bytes 5242880 | tf_op jit(solution)/shard_map/pallas_call | solution.py:407
  6.6 1.5 %collective-permute-start.4 = (f32[8,16,512]{2,1,0:T(8,128)}, f32[8,16,512]{2,1,0:T(8,128)S(1)}, u32[]{:S(2)}, u32[]{:S(2)}) collective-permute-start(f32[8,16,512]{2,1,0:T(8,128)} %get-tuple-element.16.own_ref.refs_2_), channel_id=1, source_target_pairs={{192,0},{0,64},{64,128},{128,192},{193,1},{1,65},{65,129},{129,193... | collective-permute-start | bytes 786440 | tf_op jit(solution)/shard_map/ppermute | solution.py:446
  8.1 2.7 %collective-permute-start.3 = (f32[8,16,512]{2,1,0:T(8,128)}, f32[8,16,512]{2,1,0:T(8,128)S(1)}, u32[]{:S(2)}, u32[]{:S(2)}) collective-permute-start(f32[8,16,512]{2,1,0:T(8,128)} %get-tuple-element.16.own_ref.refs_2_), channel_id=1, source_target_pairs={{128,0},{192,64},{0,128},{64,192},{129,1},{193,65},{1,129},{65,193... | collective-permute-start | bytes 786440 | tf_op jit(solution)/shard_map/ppermute | solution.py:446
  10.8 1.4 %collective-permute-start.2 = (f32[8,16,512]{2,1,0:T(8,128)}, f32[8,16,512]{2,1,0:T(8,128)S(1)}, u32[]{:S(2)}, u32[]{:S(2)}) collective-permute-start(f32[8,16,512]{2,1,0:T(8,128)} %get-tuple-element.16.own_ref.refs_2_), channel_id=1, source_target_pairs={{64,0},{128,64},{192,128},{0,192},{65,1},{129,65},{193,129},{1,193... | collective-permute-start | bytes 786440 | tf_op jit(solution)/shard_map/ppermute | solution.py:446
  12.2 1.9 %collective-permute-start.1 = (f32[8,16,512]{2,1,0:T(8,128)}, f32[8,16,512]{2,1,0:T(8,128)S(1)}, u32[]{:S(2)}, u32[]{:S(2)}) collective-permute-start(f32[8,16,512]{2,1,0:T(8,128)} %get-tuple-element.16.own_ref.refs_2_), channel_id=1, source_target_pairs={{0,1},{1,2},{2,3},{3,4},{4,5},{5,6},{6,7},{7,8},{8,9},{9,10},{10,1... | collective-permute-start | bytes 786440 | tf_op jit(solution)/shard_map/ppermute | solution.py:456
  14.1 6.5 %collective-permute-start = (f32[8,16,512]{2,1,0:T(8,128)}, f32[8,16,512]{2,1,0:T(8,128)S(1)}, u32[]{:S(2)}, u32[]{:S(2)}) collective-permute-start(f32[8,16,512]{2,1,0:T(8,128)} %get-tuple-element.16.own_ref.refs_2_), channel_id=1, source_target_pairs={{1,0},{2,1},{3,2},{4,3},{5,4},{6,5},{7,6},{8,7},{9,8},{10,9},{11,1... | collective-permute-start | bytes 786440 | tf_op jit(solution)/shard_map/ppermute | solution.py:455
  20.7 10.3 %all-to-all-start = ((f32[256,1,128]{2,1,0:T(1,128)}), f32[256,1,128]{2,1,0:T(1,128)S(1)}, u32[]{:S(2)}, u32[]{:S(2)}) async-start(f32[256,1,128]{2,1,0:T(1,128)} %bitcast.8), calls=%async_computation | async-start | bytes 262144 | tf_op jit(solution)/shard_map/all_to_all | solution.py:427
  31.0 7.2 %shard_map.110.refs_5_ = f32[16,8,512]{2,1,0:T(8,128)} custom-call(f32[16,8,512]{2,1,0:T(8,128)} %get-tuple-element.17.image_ref, f32[20,8,512]{2,1,0:T(8,128)} %get-tuple-element.18.maps_ref, s32[16,256]{1,0:T(8,128)} %sampling_ref.5, bf16[768,256]{1,0:T(8,128)(2,1)} %constant.23.clone.fore_even_ref, bf16[768,256]{1,0:T(8,128)(2,1)} %constant.25.clone.fore_odd_ref, ...), custom_call_target="tpu_custom_call" | custom-call | flops 4026531840 | bytes 524288 | tf_op jit(solution)/shard_map/pallas_call | solution.py:431
  38.2 0.7 copy-done.4
  38.9 0.1 copy-done.6
  39.0 0.7 copy-done.8
  39.7 2.6 %shard_map.111.refs_6_ = f32[8,128,256]{2,1,0:T(8,128)} custom-call(f32[8,16,512]{2,1,0:T(8,128)} %get-tuple-element.16.own_ref.refs_2_, f32[8,16,512]{2,1,0:T(8,128)} %copy-done.8, f32[8,16,512]{2,1,0:T(8,128)} %copy-done.6, f32[8,16,512]{2,1,0:T(8,128)} %copy-done.4, bf16[128,384]{1,0:T(8,128)(2,1)} %constant.26.clone.table_ref.refs_7_), custom_call_target="tpu_custom_call" | custom-call | flops 201326592 | bytes 1245184 | tf_op jit(solution)/shard_map/pallas_call | solution.py:465
  42.3 0.1 all-to-all-done
  42.5 0.0 copy-start.2
  42.5 0.6 copy-done
  43.1 0.1 copy-done.1
  43.2 0.1 copy-done.2
  43.3 3.9 %shard_map.112 = (f32[8,16,512]{2,1,0:T(8,128)}, f32[8,16,512]{2,1,0:T(8,128)}, f32[16,8,512]{2,1,0:T(8,128)}, f32[8,128,256]{2,1,0:T(8,128)}, f32[3,8,16,512]{3,2,1,0:T(8,128)}, /*index=5*/f32[3,8,16,512]{3,2,1,0:T(8,128)}) custom-call(f32[256,128]{1,0:T(8,128)} %bitcast.5, f32[1,1]{1,0:T(1,128)} %bitcast.3.refs_1_, ...), custom_call_target="tpu_custom_call" | custom-call | flops 50331648 | bytes 2277380 | tf_op jit(solution)/shard_map/pallas_call | solution.py:465
  47.2 1.9 %collective-permute-start.9 = (f32[8,16,512]{2,1,0:T(8,128)}, f32[8,16,512]{2,1,0:T(8,128)S(1)}, u32[]{:S(2)}, u32[]{:S(2)}) collective-permute-start(f32[8,16,512]{2,1,0:T(8,128)} %get-tuple-element.19.refs_2_.refs_1_), channel_id=1, source_target_pairs={{0,1},{1,2},{2,3},{3,4},{4,5},{5,6},{6,7},{7,8},{8,9},{9,10},{10,1... | collective-permute-start | bytes 786440 | tf_op jit(solution)/shard_map/ppermute | solution.py:456
  49.1 6.3 %collective-permute-start.8 = (f32[8,16,512]{2,1,0:T(8,128)}, f32[8,16,512]{2,1,0:T(8,128)S(1)}, u32[]{:S(2)}, u32[]{:S(2)}) collective-permute-start(f32[8,16,512]{2,1,0:T(8,128)} %get-tuple-element.19.refs_2_.refs_1_), channel_id=1, source_target_pairs={{1,0},{2,1},{3,2},{4,3},{5,4},{6,5},{7,6},{8,7},{9,8},{10,9},{11,1... | collective-permute-start | bytes 786440 | tf_op jit(solution)/shard_map/ppermute | solution.py:455
  55.4 1.6 %collective-permute-start.7 = (f32[8,16,512]{2,1,0:T(8,128)}, f32[8,16,512]{2,1,0:T(8,128)S(1)}, u32[]{:S(2)}, u32[]{:S(2)}) collective-permute-start(f32[8,16,512]{2,1,0:T(8,128)} %get-tuple-element.19.refs_2_.refs_1_), channel_id=1, source_target_pairs={{192,0},{0,64},{64,128},{128,192},{193,1},{1,65},{65,129},{129,193... | collective-permute-start | bytes 786440 | tf_op jit(solution)/shard_map/ppermute | solution.py:446
  57.0 2.7 %collective-permute-start.6 = (f32[8,16,512]{2,1,0:T(8,128)}, f32[8,16,512]{2,1,0:T(8,128)S(1)}, u32[]{:S(2)}, u32[]{:S(2)}) collective-permute-start(f32[8,16,512]{2,1,0:T(8,128)} %get-tuple-element.19.refs_2_.refs_1_), channel_id=1, source_target_pairs={{128,0},{192,64},{0,128},{64,192},{129,1},{193,65},{1,129},{65,193... | collective-permute-start | bytes 786440 | tf_op jit(solution)/shard_map/ppermute | solution.py:446
  59.7 1.4 %collective-permute-start.5 = (f32[8,16,512]{2,1,0:T(8,128)}, f32[8,16,512]{2,1,0:T(8,128)S(1)}, u32[]{:S(2)}, u32[]{:S(2)}) collective-permute-start(f32[8,16,512]{2,1,0:T(8,128)} %get-tuple-element.19.refs_2_.refs_1_), channel_id=1, source_target_pairs={{64,0},{128,64},{192,128},{0,192},{65,1},{129,65},{193,129},{1,193... | collective-permute-start | bytes 786440 | tf_op jit(solution)/shard_map/ppermute | solution.py:446
  61.1 7.1 %shard_map.113.refs_5_ = f32[16,8,512]{2,1,0:T(8,128)} custom-call(f32[16,8,512]{2,1,0:T(8,128)} %get-tuple-element.21.image_ref, f32[20,8,512]{2,1,0:T(8,128)} %get-tuple-element.18.maps_ref, s32[16,256]{1,0:T(8,128)} %sampling_ref.5, bf16[768,256]{1,0:T(8,128)(2,1)} %constant.23.clone.fore_even_ref, bf16[768,256]{1,0:T(8,128)(2,1)} %constant.25.clone.fore_odd_ref, ...), custom_call_target="tpu_custom_call" | custom-call | flops 4026531840 | bytes 524288 | tf_op jit(solution)/shard_map/pallas_call | solution.py:431
  68.3 0.0 copy-start.10
  68.3 0.7 copy-done.9
  69.0 0.1 copy-done.10
  69.1 3.0 %shard_map.114.refs_6_ = f32[8,16,512]{2,1,0:T(8,128)} custom-call(f32[256,128]{1,0:T(8,128)} %bitcast.6, f32[1,1]{1,0:T(1,128)} %bitcast.3.refs_1_, f32[8,16,512]{2,1,0:T(8,128)} %get-tuple-element.19.refs_2_.refs_1_, f32[8,16,512]{2,1,0:T(8,128)} %copy-done.10, f32[8,16,512]{2,1,0:T(8,128)} %copy-done.9, f32[16,8,512]{2,1,0:T(8,128)} %shard_map.113.refs_5_, ...), custom_call_target="tpu_custom_call" | custom-call | flops 1000000 | bytes 3014660 | tf_op jit(solution)/shard_map/pallas_call | solution.py:465
  72.1 0.7 copy-done.3
  72.8 0.1 copy-done.5
  72.8 0.1 copy-done.7
  73.0 5.0 %shard_map.115 = f32[16,1,8,512]{3,2,1,0:T(8,128)} custom-call(f32[256,128]{1,0:T(8,128)} %bitcast.7, f32[8,16,512]{2,1,0:T(8,128)} %get-tuple-element.19.refs_2_.refs_1_, f32[8,16,512]{2,1,0:T(8,128)} %copy-done.7, f32[8,16,512]{2,1,0:T(8,128)} %copy-done.5, f32[8,16,512]{2,1,0:T(8,128)} %copy-done.3, f32[8,128,256]{2,1,0:T(8,128)} %get-tuple-element.20.refs_5_, ...), custom_call_target="tpu_custom_call" | custom-call | flops 201326592 | bytes 2998272 | tf_op jit(solution)/shard_map/pallas_call | solution.py:465
  (19 shorter events, 0.0 us)
Async XLA Ops:
  6.6 31.6 %collective-permute-start.4 = (f32[8,16,512]{2,1,0:T(8,128)}, f32[8,16,512]{2,1,0:T(8,128)S(1)}, u32[]{:S(2)}, u32[]{:S(2)}) collective-permute-start(f32[8,16,512]{2,1,0:T(8,128)} %get-tuple-element.16.own_ref.refs_2_), channel_id=1, source_target_pairs={{192,0},{0,64},{64,128},{128,192},{193,1},{1,65},{65,129},{129,193... | collective-permute-start | bytes 786440 | tf_op jit(solution)/shard_map/ppermute | solution.py:446
  8.1 30.2 %collective-permute-start.3 = (f32[8,16,512]{2,1,0:T(8,128)}, f32[8,16,512]{2,1,0:T(8,128)S(1)}, u32[]{:S(2)}, u32[]{:S(2)}) collective-permute-start(f32[8,16,512]{2,1,0:T(8,128)} %get-tuple-element.16.own_ref.refs_2_), channel_id=1, source_target_pairs={{128,0},{192,64},{0,128},{64,192},{129,1},{193,65},{1,129},{65,193... | collective-permute-start | bytes 786440 | tf_op jit(solution)/shard_map/ppermute | solution.py:446
  10.8 27.5 %collective-permute-start.2 = (f32[8,16,512]{2,1,0:T(8,128)}, f32[8,16,512]{2,1,0:T(8,128)S(1)}, u32[]{:S(2)}, u32[]{:S(2)}) collective-permute-start(f32[8,16,512]{2,1,0:T(8,128)} %get-tuple-element.16.own_ref.refs_2_), channel_id=1, source_target_pairs={{64,0},{128,64},{192,128},{0,192},{65,1},{129,65},{193,129},{1,193... | collective-permute-start | bytes 786440 | tf_op jit(solution)/shard_map/ppermute | solution.py:446
  12.2 30.2 %collective-permute-start.1 = (f32[8,16,512]{2,1,0:T(8,128)}, f32[8,16,512]{2,1,0:T(8,128)S(1)}, u32[]{:S(2)}, u32[]{:S(2)}) collective-permute-start(f32[8,16,512]{2,1,0:T(8,128)} %get-tuple-element.16.own_ref.refs_2_), channel_id=1, source_target_pairs={{0,1},{1,2},{2,3},{3,4},{4,5},{5,6},{6,7},{7,8},{8,9},{9,10},{10,1... | collective-permute-start | bytes 786440 | tf_op jit(solution)/shard_map/ppermute | solution.py:456
  14.1 28.3 %collective-permute-start = (f32[8,16,512]{2,1,0:T(8,128)}, f32[8,16,512]{2,1,0:T(8,128)S(1)}, u32[]{:S(2)}, u32[]{:S(2)}) collective-permute-start(f32[8,16,512]{2,1,0:T(8,128)} %get-tuple-element.16.own_ref.refs_2_), channel_id=1, source_target_pairs={{1,0},{2,1},{3,2},{4,3},{5,4},{6,5},{7,6},{8,7},{9,8},{10,9},{11,1... | collective-permute-start | bytes 786440 | tf_op jit(solution)/shard_map/ppermute | solution.py:455
  20.7 21.8 %all-to-all-start = ((f32[256,1,128]{2,1,0:T(1,128)}), f32[256,1,128]{2,1,0:T(1,128)S(1)}, u32[]{:S(2)}, u32[]{:S(2)}) async-start(f32[256,1,128]{2,1,0:T(1,128)} %bitcast.8), calls=%async_computation | async-start | bytes 262144 | tf_op jit(solution)/shard_map/all_to_all | solution.py:427
  38.2 0.7 copy-start.4
  38.2 0.8 copy-start.6
  39.0 0.7 copy-start.8
  42.5 0.7 copy-start
  42.5 0.8 copy-start.1
  42.5 0.8 %copy-start.2 = (f32[8,16,512]{2,1,0:T(8,128)}, f32[8,16,512]{2,1,0:T(8,128)S(1)}, u32[]{:S(2)}) copy-start(f32[8,16,512]{2,1,0:T(8,128)S(1)} %collective-permute-done.refs_3_) | copy-start | bytes 786436
  47.2 21.1 %collective-permute-start.9 = (f32[8,16,512]{2,1,0:T(8,128)}, f32[8,16,512]{2,1,0:T(8,128)S(1)}, u32[]{:S(2)}, u32[]{:S(2)}) collective-permute-start(f32[8,16,512]{2,1,0:T(8,128)} %get-tuple-element.19.refs_2_.refs_1_), channel_id=1, source_target_pairs={{0,1},{1,2},{2,3},{3,4},{4,5},{5,6},{6,7},{7,8},{8,9},{9,10},{10,1... | collective-permute-start | bytes 786440 | tf_op jit(solution)/shard_map/ppermute | solution.py:456
  49.1 19.2 %collective-permute-start.8 = (f32[8,16,512]{2,1,0:T(8,128)}, f32[8,16,512]{2,1,0:T(8,128)S(1)}, u32[]{:S(2)}, u32[]{:S(2)}) collective-permute-start(f32[8,16,512]{2,1,0:T(8,128)} %get-tuple-element.19.refs_2_.refs_1_), channel_id=1, source_target_pairs={{1,0},{2,1},{3,2},{4,3},{5,4},{6,5},{7,6},{8,7},{9,8},{10,9},{11,1... | collective-permute-start | bytes 786440 | tf_op jit(solution)/shard_map/ppermute | solution.py:455
  55.4 16.6 %collective-permute-start.7 = (f32[8,16,512]{2,1,0:T(8,128)}, f32[8,16,512]{2,1,0:T(8,128)S(1)}, u32[]{:S(2)}, u32[]{:S(2)}) collective-permute-start(f32[8,16,512]{2,1,0:T(8,128)} %get-tuple-element.19.refs_2_.refs_1_), channel_id=1, source_target_pairs={{192,0},{0,64},{64,128},{128,192},{193,1},{1,65},{65,129},{129,193... | collective-permute-start | bytes 786440 | tf_op jit(solution)/shard_map/ppermute | solution.py:446
  57.0 15.1 %collective-permute-start.6 = (f32[8,16,512]{2,1,0:T(8,128)}, f32[8,16,512]{2,1,0:T(8,128)S(1)}, u32[]{:S(2)}, u32[]{:S(2)}) collective-permute-start(f32[8,16,512]{2,1,0:T(8,128)} %get-tuple-element.19.refs_2_.refs_1_), channel_id=1, source_target_pairs={{128,0},{192,64},{0,128},{64,192},{129,1},{193,65},{1,129},{65,193... | collective-permute-start | bytes 786440 | tf_op jit(solution)/shard_map/ppermute | solution.py:446
  59.7 12.4 %collective-permute-start.5 = (f32[8,16,512]{2,1,0:T(8,128)}, f32[8,16,512]{2,1,0:T(8,128)S(1)}, u32[]{:S(2)}, u32[]{:S(2)}) collective-permute-start(f32[8,16,512]{2,1,0:T(8,128)} %get-tuple-element.19.refs_2_.refs_1_), channel_id=1, source_target_pairs={{64,0},{128,64},{192,128},{0,192},{65,1},{129,65},{193,129},{1,193... | collective-permute-start | bytes 786440 | tf_op jit(solution)/shard_map/ppermute | solution.py:446
  68.3 0.7 copy-start.9
  68.3 0.8 copy-start.10
  72.1 0.7 copy-start.3
  72.1 0.8 copy-start.5
  72.1 0.9 %copy-start.7 = (f32[8,16,512]{2,1,0:T(8,128)}, f32[8,16,512]{2,1,0:T(8,128)S(1)}, u32[]{:S(2)}) copy-start(f32[8,16,512]{2,1,0:T(8,128)S(1)} %collective-permute-done.5.refs_2_) | copy-start | bytes 786436
where the time goes:
time: 78.4 us; the launch traced here: 77.9 us
  starting transfers between devices  38.3 us (49%)
  Pallas kernels  35.4 us (45%)
  local copies, waits for them, and re-layouts  3.89 us (5%)
    pallas_call x4, Pallas kernels, call(): pl.pallas_call(kernel, in_specs=specs, out_specs=jax.tree.map(lambda _: v...  14.5 us
    pallas_call x2, Pallas kernels, normal(): pl.pallas_call(normal_kernel, grid=(frames_here // STEP,), in_specs=[pl.B...  14.3 us
    ppermute x2, starting transfers between devices, neighbours(): above = lax.ppermute(image, 'cuts', [(i + 1, i) for i in range(count - 1)])  12.8 us
    ppermute x6, starting transfers between devices, gathered(): lax.ppermute(image, 'frame', [((index + by) % blocks, index) for index in...  11.4 us
    all_to_all x1, starting transfers between devices, shards(): energies = lax.all_to_all(energy, AXES, 0, 0, tiled=True)  10.3 us
    pallas_call x1, Pallas kernels, shards(): pl.pallas_call(initial_kernel, grid=(frames_here // STEP,), in_specs=[pl....  6.57 us
    unnamed x22, local copies, waits for them, and re-layouts  3.89 us
    ppermute x2, starting transfers between devices, neighbours(): below = lax.ppermute(image, 'cuts', [(i, i + 1) for i in range(count - 1)])  3.82 us
  transfers between devices with their start and end apart: 11, of which 1 were waited for; matrix products, arithmetic and copies ran while one was open for 0% of the time, Pallas kernels for 26%

commit v1 on v0

--- a/solution.py
+++ b/solution.py
@@ -19,8 +19,8 @@
 KEEP = 1.0 / (1.0 + SIGMA)
 TAKE = SIGMA / (1.0 + SIGMA)
 AXES = ("frame", "cuts")
-STEP = 4
-VMEM_BYTES = 56 * 1024 * 1024
+STEP = 8
+VMEM_BYTES = 24 * 1024 * 1024
 BF16 = jnp.bfloat16
 F32 = jnp.float32
 
@@ -40,14 +40,12 @@
 def line_tables(positions):
     half = positions // 2
     lines = np.arange(half)[:, None]
-    tables = {}
-    for name, places in (("even", 2 * np.arange(half)), ("odd", 2 * np.arange(half) + 1)):
+    backs = []
+    for places in (2 * np.arange(half), 2 * np.arange(half) + 1):
         angles = 2.0 * math.pi / positions * (lines * places[None, :] % positions)
         back = block_table(np.cos(angles), np.sin(angles)) / math.sqrt(positions)
-        for key, table in (("back_" + name, back), ("fore_" + name, back.T)):
-            high, low = split_table(table)
-            tables[key] = np.concatenate([high, high, low], 0)
-    return tables
+        backs.extend(split_table(back))
+    return np.stack(backs, 0)
 
 
 def time_tables(frames_all, frames_here):
@@ -76,10 +74,24 @@
     return high, (value - high.astype(F32)).astype(BF16)
 
 
-def product(value, table):
+def product(value, tables_ref, index):
     high, low = parted(value)
+    table_high, table_low = tables_ref[index], tables_ref[index + 1]
     return jnp.dot(
-        jnp.concatenate([high, low, high], -1), table, preferred_element_type=F32
+        jnp.concatenate([high, low, high], -1),
+        jnp.concatenate([table_high, table_high, table_low], 0),
+        preferred_element_type=F32,
+    )
+
+
+def turned_product(value, tables_ref, index):
+    high, low = parted(value)
+    table_high, table_low = tables_ref[index], tables_ref[index + 1]
+    return lax.dot_general(
+        jnp.concatenate([high, low, high], -1),
+        jnp.concatenate([table_high, table_high, table_low], -1),
+        (((1,), (1,)), ((), ())),
+        preferred_element_type=F32,
     )
 
 
@@ -118,99 +130,114 @@
 
 
 def initial_kernel(
-    measured_ref, maps_ref, sampling_ref, even_ref, odd_ref, part_ref,
-    image_ref, image_x_ref, energy_ref, parted_ref, total_ref,
+    measured_hbm, maps_hbm, sampling_hbm, tables_hbm, part_hbm,
+    image_ref, image_x_ref, energy_ref, parted_ref, tables_ref, sampling_ref,
+    data_ref, maps_ref, part_ref, data_sem, sems,
 ):
-    step = pl.program_id(0)
-    frames = measured_ref.shape[0]
-    coils, readout, doubled = maps_ref.shape[1:]
+    frames_here, coils, readout, doubled = data_ref.shape
     half, quarter = doubled // 2, doubled // 4
     rows = coils * readout
-
-    @pl.when(step == 0)
-    def _():
-        maps = maps_ref[0].reshape(rows, doubled)
-        re = moved(maps[:, :half], part_ref[...])
-        im = moved(maps[:, half:], part_ref[...])
-        parted_ref[...] = cat(
-            re[:, :quarter], im[:, :quarter], re[:, quarter:], im[:, quarter:]
-        ).reshape(coils, readout, doubled)
-        total_ref[...] = jnp.zeros_like(total_ref)
-
-    evens, odds = [], []
-    for index in range(frames):
-        data = measured_ref[index, 0].reshape(rows, doubled)
-        weight = sampling_ref[pl.ds(step * frames + index, 1), :].astype(F32)
-        low, high = weight[:, :quarter], weight[:, quarter:]
-        re_low, re_high, im_low, im_high = quarters(data)
-        re_low, re_high = re_low * low, re_high * high
-        im_low, im_high = im_low * low, im_high * high
-        evens.append(cat(re_low + re_high, im_low + im_high))
-        odds.append(cat(re_low - re_high, im_low - im_high))
-    evens = product(jnp.concatenate(evens, 0), even_ref[...])
-    odds = product(jnp.concatenate(odds, 0), odd_ref[...])
-    evens = evens.reshape(frames, coils, readout, half)
-    odds = odds.reshape(frames, coils, readout, half)
-    energy = total_ref[...]
-    for index in range(frames):
-        image = cat(
-            combine_coils(evens[index], parted_ref[:, :, :half]),
-            combine_coils(odds[index], parted_ref[:, :, half:]),
+    groups = frames_here // STEP
+
+    def load(group):
+        frames = pl.ds(group * STEP, STEP)
+        return pltpu.make_async_copy(
+            measured_hbm.at[frames, 0], data_ref.at[frames], data_sem.at[group]
         )
-        image_ref[step * frames + index] = image
-        energy = energy + sum(piece * piece for piece in quarters(image))
-    total_ref[...] = energy
-
-    @pl.when(step == pl.num_programs(0) - 1)
-    def _():
-        energy_ref[...] = jnp.broadcast_to(jnp.sum(total_ref[...]), energy_ref.shape)
-        image_x_ref[...] = jnp.swapaxes(image_ref[...], 0, 1)
-
-
-def normal_kernel(
-    image_ref, maps_ref, sampling_ref, fore_even_ref, fore_odd_ref, even_ref, odd_ref,
-    out_ref,
-):
-    step = pl.program_id(0)
-    frames = image_ref.shape[0]
+
+    small = [
+        pltpu.make_async_copy(maps_hbm.at[0], maps_ref, sems.at[0]),
+        pltpu.make_async_copy(part_hbm, part_ref, sems.at[1]),
+        pltpu.make_async_copy(sampling_hbm, sampling_ref, sems.at[2]),
+        pltpu.make_async_copy(tables_hbm, tables_ref, sems.at[3]),
+    ]
+    for copy in small:
+        copy.start()
+    for group in range(groups):
+        load(group).start()
+    small[0].wait()
+    small[1].wait()
+    maps = maps_ref[...].reshape(rows, doubled)
+    re = moved(maps[:, :half], part_ref[...])
+    im = moved(maps[:, half:], part_ref[...])
+    parted_ref[...] = cat(
+        re[:, :quarter], im[:, :quarter], re[:, quarter:], im[:, quarter:]
+    ).reshape(coils, readout, doubled)
+    small[2].wait()
+    small[3].wait()
+    energy = jnp.zeros((readout, quarter), F32)
+    for group in range(groups):
+        load(group).wait()
+        evens, odds = [], []
+        for frame in range(group * STEP, (group + 1) * STEP):
+            data = data_ref[frame].reshape(rows, doubled)
+            weight = sampling_ref[frame : frame + 1, :].astype(F32)
+            low, high = weight[:, :quarter], weight[:, quarter:]
+            re_low, re_high, im_low, im_high = quarters(data)
+            re_low, re_high = re_low * low, re_high * high
+            im_low, im_high = im_low * low, im_high * high
+            evens.append(cat(re_low + re_high, im_low + im_high))
+            odds.append(cat(re_low - re_high, im_low - im_high))
+        evens = product(jnp.concatenate(evens, 0), tables_ref, 0)
+        odds = product(jnp.concatenate(odds, 0), tables_ref, 2)
+        evens = evens.reshape(STEP, coils, readout, half)
+        odds = odds.reshape(STEP, coils, readout, half)
+        for index in range(STEP):
+            image = cat(
+                combine_coils(evens[index], parted_ref[:, :, :half]),
+                combine_coils(odds[index], parted_ref[:, :, half:]),
+            )
+            image_ref[group * STEP + index] = image
+            energy = energy + sum(piece * piece for piece in quarters(image))
+    energy_ref[...] = jnp.broadcast_to(jnp.sum(energy), energy_ref.shape)
+    image_x_ref[...] = jnp.swapaxes(image_ref[...], 0, 1)
+
+
+def normal_kernel(image_ref, maps_ref, sampling_ref, tables_ref, out_ref):
+    frames_here = image_ref.shape[0]
     coils, readout, doubled = maps_ref.shape
     half, quarter = doubled // 2, doubled // 4
     rows = coils * readout
 
-    def lines(offset, table_ref):
+    def lines(group, offset, table):
         pieces = []
-        for index in range(frames):
-            re = image_ref[index, :, offset : offset + quarter][None]
-            im = image_ref[index, :, offset + quarter : offset + half][None]
+        for index in range(STEP):
+            frame = group * STEP + index
+            re = image_ref[frame, :, offset : offset + quarter][None]
+            im = image_ref[frame, :, offset + quarter : offset + half][None]
             map_re = maps_ref[:, :, offset : offset + quarter]
             map_im = maps_ref[:, :, offset + quarter : offset + half]
             pieces.append(
                 cat(map_re * re - map_im * im, map_re * im + map_im * re).reshape(rows, half)
             )
-        return product(jnp.concatenate(pieces, 0), table_ref[...])
-
-    from_even = lines(0, fore_even_ref)
-    from_odd = lines(half, fore_odd_ref)
-    low = from_even + from_odd
-    high = from_even - from_odd
-    evens, odds = [], []
-    for index in range(frames):
-        weight = sampling_ref[pl.ds(step * frames + index, 1), :].astype(F32)
-        weight_low = cat(weight[:, :quarter], weight[:, :quarter])
-        weight_high = cat(weight[:, quarter:], weight[:, quarter:])
-        kept_low = low[index * rows : (index + 1) * rows] * weight_low
-        kept_high = high[index * rows : (index + 1) * rows] * weight_high
-        evens.append(kept_low + kept_high)
-        odds.append(kept_low - kept_high)
-    evens = product(jnp.concatenate(evens, 0), even_ref[...])
-    odds = product(jnp.concatenate(odds, 0), odd_ref[...])
-    evens = evens.reshape(frames, coils, readout, half)
-    odds = odds.reshape(frames, coils, readout, half)
-    for index in range(frames):
-        out_ref[index] = cat(
-            combine_coils(evens[index], maps_ref[:, :, :half]),
-            combine_coils(odds[index], maps_ref[:, :, half:]),
-        )
+        return turned_product(jnp.concatenate(pieces, 0), tables_ref, table)
+
+    def step(group, carry):
+        from_even = lines(group, 0, 0)
+        from_odd = lines(group, half, 2)
+        low = from_even + from_odd
+        high = from_even - from_odd
+        evens, odds = [], []
+        for index in range(STEP):
+            weight = sampling_ref[pl.ds(group * STEP + index, 1), :].astype(F32)
+            weight_low = cat(weight[:, :quarter], weight[:, :quarter])
+            weight_high = cat(weight[:, quarter:], weight[:, quarter:])
+            kept_low = low[index * rows : (index + 1) * rows] * weight_low
+            kept_high = high[index * rows : (index + 1) * rows] * weight_high
+            evens.append(kept_low + kept_high)
+            odds.append(kept_low - kept_high)
+        evens = product(jnp.concatenate(evens, 0), tables_ref, 0)
+        odds = product(jnp.concatenate(odds, 0), tables_ref, 2)
+        evens = evens.reshape(STEP, coils, readout, half)
+        odds = odds.reshape(STEP, coils, readout, half)
+        for index in range(STEP):
+            out_ref[group * STEP + index] = cat(
+                combine_coils(evens[index], maps_ref[:, :, :half]),
+                combine_coils(odds[index], maps_ref[:, :, half:]),
+            )
+        return carry
+
+    lax.fori_loop(0, frames_here // STEP, step, 0)
 
 
 def frequencies(blocks, x, table):
@@ -300,14 +327,14 @@
 
 
 def first_kernel(
-    cells, energy_ref, flag_ref, own_ref, above_ref, below_ref, normal_ref, frequency_ref,
+    cells, energy_ref, own_ref, above_ref, below_ref, normal_ref, frequency_ref,
     table_ref,
     base_ref, bar_x_ref, bar_ref, time_ref, space_ref, space_below_ref,
 ):
     rms_level = level(energy_ref, cells)
     limit_time, limit_space = LAM_TIME * rms_level, LAM_SPACE * rms_level
     limit_wide = cat(limit_time, limit_time)
-    has_below = flag_ref[0, 0]
+    has_below = (lax.axis_index("cuts") > 0).astype(F32)
     normal = jnp.swapaxes(normal_ref[...], 0, 1)
     rows_before = jnp.zeros(own_ref.shape[1:], F32)
     bars = []
@@ -332,12 +359,12 @@
 
 
 def space_kernel(
-    cells, energy_ref, flag_ref, own_ref, above_ref, below_ref, normal_ref, base_ref,
+    cells, energy_ref, own_ref, above_ref, below_ref, normal_ref, base_ref,
     space_ref, space_below_ref,
     out_ref,
 ):
     limit_space = LAM_SPACE * level(energy_ref, cells)
-    has_below = flag_ref[0, 0]
+    has_below = (lax.axis_index("cuts") > 0).astype(F32)
     normal = jnp.swapaxes(normal_ref[...], 0, 1)
     rows_before = jnp.zeros(own_ref.shape[1:], F32)
     for x in range(own_ref.shape[0]):
@@ -357,11 +384,12 @@
     limit_time = LAM_TIME * level(energy_ref, cells)
     limit_wide = cat(limit_time, limit_time)
     blocks = (own_ref, one_ref, two_ref, three_ref)
-    images = []
-    for x in range(own_ref.shape[0]):
-        dual = time_ref[x] + SIGMA * frequencies(blocks, x, fore_ref[...])
-        field = frames_of(clip_time(dual, limit_wide), back_ref[...])
-        images.append(base_ref[x] - TAU * field)
+    places = range(own_ref.shape[0])
+    duals = [
+        time_ref[x] + SIGMA * frequencies(blocks, x, fore_ref[...]) for x in places
+    ]
+    duals = [clip_time(dual, limit_wide) for dual in duals]
+    images = [base_ref[x] - TAU * frames_of(duals[x], back_ref[...]) for x in places]
     count, size = len(images), images[0].shape[0]
     image = jnp.concatenate(images, 0)
     re_even, im_even, re_odd, im_odd = quarters(image)
@@ -377,10 +405,6 @@
 
 def cost(flops, moved_bytes):
     return pl.CostEstimate(flops=flops, bytes_accessed=moved_bytes, transcendentals=0)
-
-
-def whole(array):
-    return pl.BlockSpec(array.shape, lambda step: (0,) * array.ndim)
 
 
 def struct(*shape):
@@ -395,51 +419,54 @@
     frames_all = frames_here * blocks
     devices = blocks * lax.axis_size("cuts")
     cells = float(frames_all * slices_all * readout * positions)
-    lines = {key: jnp.asarray(table) for key, table in line_tables(positions).items()}
+    tables = jnp.asarray(line_tables(positions))
     time_fore, time_back = (jnp.asarray(table) for table in time_tables(frames_all, frames_here))
     parting = parting_table(positions)
     part, unpart = jnp.asarray(parting, BF16), jnp.asarray(parting.T, BF16)
     plane = (readout, frames_here, doubled)
     turned = (frames_here, readout, doubled)
     rows = frames_here * coils * readout
-
-    even, odd = lines["back_even"], lines["back_odd"]
-    initial, initial_x, energy, maps = pl.pallas_call(
+    hbm = pl.BlockSpec(memory_space=pltpu.HBM)
+    vmem = pl.BlockSpec(memory_space=pltpu.VMEM)
+
+    initial, initial_x, energy, maps, tables, sampling = pl.pallas_call(
         initial_kernel,
-        grid=(frames_here // STEP,),
-        in_specs=[
-            pl.BlockSpec((STEP,) + measured.shape[1:], lambda step: (step, 0, 0, 0, 0)),
-            whole(coil_maps), whole(sampling), whole(even), whole(odd), whole(part),
-        ],
-        out_specs=[
-            whole(struct(*turned)), whole(struct(*plane)), whole(struct(devices, 128)),
-            whole(struct(coils, readout, doubled)),
-        ],
+        in_specs=[hbm] * 5,
+        out_specs=[vmem] * 6,
         out_shape=[
             struct(*turned), struct(*plane), struct(devices, 128),
-            struct(coils, readout, doubled),
+            pltpu.VMEM((coils, readout, doubled), F32),
+            pltpu.VMEM(tables.shape, BF16),
+            pltpu.VMEM(sampling.shape, jnp.int32),
         ],
-        scratch_shapes=[pltpu.VMEM((readout, 128), F32)],
+        scratch_shapes=[
+            pltpu.VMEM((frames_here, coils, readout, doubled), F32),
+            pltpu.VMEM((coils, readout, doubled), F32),
+            pltpu.VMEM(part.shape, BF16),
+            pltpu.SemaphoreType.DMA((frames_here // STEP,)),
+            pltpu.SemaphoreType.DMA((4,)),
+        ],
         compiler_params=params(),
         cost_estimate=cost(6 * rows * doubled * positions, measured.size * 4),
-    )(measured, coil_maps, sampling, even, odd, part)
+    )(*(
+        pltpu.with_memory_space_constraint(array, pltpu.HBM)
+        for array in (measured, coil_maps, sampling, tables, part)
+    ))
 
     energies = lax.all_to_all(energy, AXES, 0, 0, tiled=True)
 
     def normal(image):
-        tables = [lines[key] for key in ("fore_even", "fore_odd", "back_even", "back_odd")]
         return pl.pallas_call(
             normal_kernel,
-            grid=(frames_here // STEP,),
-            in_specs=[
-                pl.BlockSpec((STEP, readout, doubled), lambda step: (step, 0, 0)),
-                whole(maps), whole(sampling),
-            ] + [whole(table) for table in tables],
-            out_specs=pl.BlockSpec((STEP, readout, doubled), lambda step: (step, 0, 0)),
+            in_specs=[vmem] * 4,
+            out_specs=vmem,
             out_shape=struct(*turned),
             compiler_params=params(),
             cost_estimate=cost(12 * rows * doubled * positions, image.size * 8),
-        )(image, maps, sampling, *tables)
+        )(image, *(
+            pltpu.with_memory_space_constraint(array, pltpu.VMEM)
+            for array in (maps, sampling, tables)
+        ))
 
     def gathered(image):
         others = [
@@ -456,15 +483,11 @@
         below = lax.ppermute(image, "cuts", [(i, i + 1) for i in range(count - 1)])
         return above, below
 
-    flag = (lax.axis_index("cuts") > 0).astype(F32).reshape(1, 1)
-    smem = pl.BlockSpec(memory_space=pltpu.SMEM)
-    vmem = pl.BlockSpec(memory_space=pltpu.VMEM)
 
     def call(kernel, args, out_shape, flops):
-        specs = [smem if arg is flag else vmem for arg in args]
         return pl.pallas_call(
             kernel,
-            in_specs=specs,
+            in_specs=[vmem] * len(args),
             out_specs=jax.tree.map(lambda _: vmem, out_shape),
             out_shape=out_shape,
             compiler_params=params(),
@@ -490,7 +513,7 @@
 
     base, bar_x, bar, time_dual, space_dual, space_below = call(
         first,
-        [energies, flag, initial_x, above, below, normal_initial, frequency, time_back],
+        [energies, initial_x, above, below, normal_initial, frequency, time_back],
         [struct(*plane), struct(*plane), struct(*turned), frequency_shape, duals_shape, duals_shape],
         time_flops // 4,
     )
@@ -499,7 +522,7 @@
     normal_bar = normal(bar)
     base = call(
         space,
-        [energies, flag, bar_x, above, below, normal_bar, base, space_dual, space_below],
+        [energies, bar_x, above, below, normal_bar, base, space_dual, space_below],
         struct(*plane),
         1000000,
     )

time: 78.4 us -> 67.3 us (0.86)
  the two profiles are of different devices: /device:TPU:24 before, /device:TPU:1 now
where the time goes in v1:
time: 67.3 us; the launch traced here: 67 us
  starting transfers between devices  34 us (51%)
  Pallas kernels  19.5 us (29%)
  waiting for transfers between devices  12.3 us (18%)
  local copies, waits for them, and re-layouts  1.06 us (2%)
    all_to_all x1, starting transfers between devices, shards(): energies = lax.all_to_all(energy, AXES, 0, 0, tiled=True)  13.1 us
    pallas_call x2, Pallas kernels, normal(): pl.pallas_call(normal_kernel, in_specs=[vmem] * 4, out_specs=vmem, out_sh...  10.2 us
    ppermute x6, starting transfers between devices, gathered(): lax.ppermute(image, 'frame', [((index + by) % blocks, index) for index in...  8.59 us
    ppermute x2, starting transfers between devices, neighbours(): below = lax.ppermute(image, 'cuts', [(i, i + 1) for i in range(count - 1)])  8.43 us
    all_to_all x1, waiting for transfers between devices, shards(): energies = lax.all_to_all(energy, AXES, 0, 0, tiled=True)  7.23 us
    pallas_call x1, Pallas kernels, shards(): pl.pallas_call(initial_kernel, in_specs=[hbm] * 5, out_specs=[vmem] * 6,...  5.61 us
    ppermute x6, waiting for transfers between devices, gathered(): lax.ppermute(image, 'frame', [((index + by) % blocks, index) for index in...  5.08 us
    ppermute x2, starting transfers between devices, neighbours(): above = lax.ppermute(image, 'cuts', [(i + 1, i) for i in range(count - 1)])  3.84 us
  transfers between devices with their start and end apart: 11, of which 3 were waited for; matrix products, arithmetic and copies ran while one was open for 0% of the time, Pallas kernels for 17%

profile of v1, /device:TPU:1, one launch (start us, length us, event | category | flops | bytes accessed | tf_op | source)
XLA Modules:
  0.0 67.0 jit_solution(17714409165953415602)
XLA Ops:
  0.0 5.6 %shard_map.82 = (f32[16,8,512]{2,1,0:T(8,128)S(1)}, f32[8,16,512]{2,1,0:T(8,128)S(1)}, f32[256,128]{1,0:T(8,128)}, f32[20,8,512]{2,1,0:T(8,128)S(1)}, bf16[4,256...) custom-call(f32[16,1,20,8,512]{4,3,2,1,0:T(8,128)} %measured_hbm.1, f32[1,20,8,512]{3,2,1,0:T(8,128)} %maps_hbm.1, ...), custom_call_target="tpu_custom_call" | custom-call | flops 2013265920 | bytes 5242880 | tf_op jit(solution)/shard_map/pallas_call | solution.py:432
  5.6 2.1 %collective-permute-start.4 = (f32[8,16,512]{2,1,0:T(8,128)S(1)}, f32[8,16,512]{2,1,0:T(8,128)S(1)}, u32[]{:S(2)}, u32[]{:S(2)}) collective-permute-start(f32[8,16,512]{2,1,0:T(8,128)S(1)} %get-tuple-element.18.own_ref.refs_1_), channel_id=1, source_target_pairs={{192,0},{0,64},{64,128},{128,192},{193,1},{1,65},{65,129},{129,193... | collective-permute-start | bytes 786440 | tf_op jit(solution)/shard_map/ppermute | solution.py:473
  7.7 2.5 %collective-permute-start.3 = (f32[8,16,512]{2,1,0:T(8,128)S(1)}, f32[8,16,512]{2,1,0:T(8,128)S(1)}, u32[]{:S(2)}, u32[]{:S(2)}) collective-permute-start(f32[8,16,512]{2,1,0:T(8,128)S(1)} %get-tuple-element.18.own_ref.refs_1_), channel_id=1, source_target_pairs={{128,0},{192,64},{0,128},{64,192},{129,1},{193,65},{1,129},{65,193... | collective-permute-start | bytes 786440 | tf_op jit(solution)/shard_map/ppermute | solution.py:473
  10.2 1.1 %collective-permute-start.2 = (f32[8,16,512]{2,1,0:T(8,128)S(1)}, f32[8,16,512]{2,1,0:T(8,128)S(1)}, u32[]{:S(2)}, u32[]{:S(2)}) collective-permute-start(f32[8,16,512]{2,1,0:T(8,128)S(1)} %get-tuple-element.18.own_ref.refs_1_), channel_id=1, source_target_pairs={{64,0},{128,64},{192,128},{0,192},{65,1},{129,65},{193,129},{1,193... | collective-permute-start | bytes 786440 | tf_op jit(solution)/shard_map/ppermute | solution.py:473
  11.4 4.9 %collective-permute-start.1 = (f32[8,16,512]{2,1,0:T(8,128)S(1)}, f32[8,16,512]{2,1,0:T(8,128)S(1)}, u32[]{:S(2)}, u32[]{:S(2)}) collective-permute-start(f32[8,16,512]{2,1,0:T(8,128)S(1)} %get-tuple-element.18.own_ref.refs_1_), channel_id=1, source_target_pairs={{0,1},{1,2},{2,3},{3,4},{4,5},{5,6},{6,7},{7,8},{8,9},{9,10},{10,1... | collective-permute-start | bytes 786440 | tf_op jit(solution)/shard_map/ppermute | solution.py:483
  16.3 1.9 %collective-permute-start = (f32[8,16,512]{2,1,0:T(8,128)S(1)}, f32[8,16,512]{2,1,0:T(8,128)S(1)}, u32[]{:S(2)}, u32[]{:S(2)}) collective-permute-start(f32[8,16,512]{2,1,0:T(8,128)S(1)} %get-tuple-element.18.own_ref.refs_1_), channel_id=1, source_target_pairs={{1,0},{2,1},{3,2},{4,3},{5,4},{6,5},{7,6},{8,7},{9,8},{10,9},{11,1... | collective-permute-start | bytes 786440 | tf_op jit(solution)/shard_map/ppermute | solution.py:482
  18.2 13.1 %all-to-all-start = ((f32[256,1,128]{2,1,0:T(1,128)}), f32[256,1,128]{2,1,0:T(1,128)S(1)}, u32[]{:S(2)}, u32[]{:S(2)}) async-start(f32[256,1,128]{2,1,0:T(1,128)} %bitcast.1), calls=%async_computation | async-start | bytes 262144 | tf_op jit(solution)/shard_map/all_to_all | solution.py:456
  31.4 0.0 copy-start
  31.4 0.0 copy-start.2
  31.4 5.1 %shard_map.83.refs_4_ = f32[16,8,512]{2,1,0:T(8,128)S(1)} custom-call(f32[16,8,512]{2,1,0:T(8,128)S(1)} %get-tuple-element.19.image_ref, f32[20,8,512]{2,1,0:T(8,128)S(1)} %get-tuple-element.20.maps_ref, s32[16,256]{1,0:T(8,128)S(1)} %get-tuple-element.21.sampling_ref, bf16[4,256,256]{2,1,0:T(8,128)(2,1)S(1)} %get-tuple-element.22.tables_ref), custom_call_target="tpu_custom_call" | custom-call | flops 4026531840 | bytes 524288 | tf_op jit(solution)/shard_map/pallas_call | solution.py:459
  36.5 0.0 collective-permute-done.4.three_ref
  36.5 0.0 collective-permute-done.3.two_ref
  36.5 0.0 collective-permute-done.2.one_ref
  36.6 0.4 shard_map.84.refs_5_
  37.0 7.2 %all-to-all-done = f32[256,1,128]{2,1,0:T(1,128)S(1)} async-done(((f32[256,1,128]{2,1,0:T(1,128)}), f32[256,1,128]{2,1,0:T(1,128)S(1)}, u32[]{:S(2)}, u32[]{:S(2)}) %all-to-all-start) | async-done | bytes 131104 | tf_op jit(solution)/shard_map/all_to_all | solution.py:456
  44.2 0.0 collective-permute-done.1.refs_3_
  44.2 0.0 collective-permute-done.refs_2_
  44.2 1.0 %shard_map.85 = (f32[8,16,512]{2,1,0:T(8,128)S(1)}, f32[8,16,512]{2,1,0:T(8,128)S(1)}, f32[16,8,512]{2,1,0:T(8,128)S(1)}, f32[8,128,256]{2,1,0:T(8,128)S(1)}, f3...) custom-call(f32[256,128]{1,0:T(8,128)S(1)} %bitcast.4, f32[8,16,512]{2,1,0:T(8,128)S(1)} %get-tuple-element.18.own_ref.refs_1_, ...), custom_call_target="tpu_custom_call" | custom-call | flops 50331648 | bytes 2277376 | tf_op jit(solution)/shard_map/pallas_call | solution.py:488
  45.2 3.5 %collective-permute-start.9 = (f32[8,16,512]{2,1,0:T(8,128)S(1)}, f32[8,16,512]{2,1,0:T(8,128)S(1)}, u32[]{:S(2)}, u32[]{:S(2)}) collective-permute-start(f32[8,16,512]{2,1,0:T(8,128)S(1)} %get-tuple-element.23.refs_1_), channel_id=1, source_target_pairs={{0,1},{1,2},{2,3},{3,4},{4,5},{5,6},{6,7},{7,8},{8,9},{9,10},{10,1... | collective-permute-start | bytes 786440 | tf_op jit(solution)/shard_map/ppermute | solution.py:483
  48.8 1.9 %collective-permute-start.8 = (f32[8,16,512]{2,1,0:T(8,128)S(1)}, f32[8,16,512]{2,1,0:T(8,128)S(1)}, u32[]{:S(2)}, u32[]{:S(2)}) collective-permute-start(f32[8,16,512]{2,1,0:T(8,128)S(1)} %get-tuple-element.23.refs_1_), channel_id=1, source_target_pairs={{1,0},{2,1},{3,2},{4,3},{5,4},{6,5},{7,6},{8,7},{9,8},{10,9},{11,1... | collective-permute-start | bytes 786440 | tf_op jit(solution)/shard_map/ppermute | solution.py:482
  50.7 0.4 collective-permute-start.7
  51.1 1.8 %collective-permute-start.6 = (f32[8,16,512]{2,1,0:T(8,128)S(1)}, f32[8,16,512]{2,1,0:T(8,128)S(1)}, u32[]{:S(2)}, u32[]{:S(2)}) collective-permute-start(f32[8,16,512]{2,1,0:T(8,128)S(1)} %get-tuple-element.23.refs_1_), channel_id=1, source_target_pairs={{128,0},{192,64},{0,128},{64,192},{129,1},{193,65},{1,129},{65,193... | collective-permute-start | bytes 786440 | tf_op jit(solution)/shard_map/ppermute | solution.py:473
  52.8 0.7 %collective-permute-start.5 = (f32[8,16,512]{2,1,0:T(8,128)S(1)}, f32[8,16,512]{2,1,0:T(8,128)S(1)}, u32[]{:S(2)}, u32[]{:S(2)}) collective-permute-start(f32[8,16,512]{2,1,0:T(8,128)S(1)} %get-tuple-element.23.refs_1_), channel_id=1, source_target_pairs={{64,0},{128,64},{192,128},{0,192},{65,1},{129,65},{193,129},{1,193... | collective-permute-start | bytes 786440 | tf_op jit(solution)/shard_map/ppermute | solution.py:473
  53.6 1.0 %copy-done.4 = bf16[4,256,256]{2,1,0:T(8,128)(2,1)S(1)} copy-done((bf16[4,256,256]{2,1,0:T(8,128)(2,1)S(1)}, bf16[4,256,256]{2,1,0:T(8,128)(2,1)}, u32[]{:S(2)}) %copy-start.4) | copy-done | bytes 524312
  54.6 5.1 %shard_map.86.refs_4_ = f32[16,8,512]{2,1,0:T(8,128)S(1)} custom-call(f32[16,8,512]{2,1,0:T(8,128)S(1)} %get-tuple-element.25.image_ref, f32[20,8,512]{2,1,0:T(8,128)S(1)} %get-tuple-element.20.maps_ref, s32[16,256]{1,0:T(8,128)S(1)} %get-tuple-element.21.sampling_ref, bf16[4,256,256]{2,1,0:T(8,128)(2,1)S(1)} %copy-done.4), custom_call_target="tpu_custom_call" | custom-call | flops 4026531840 | bytes 524288 | tf_op jit(solution)/shard_map/pallas_call | solution.py:459
  59.7 0.0 collective-permute-done.9.refs_3_
  59.7 0.0 collective-permute-done.8.refs_2_
  59.7 0.5 shard_map.87.refs_6_
  60.2 4.2 %collective-permute-done.7.refs_4_ = f32[8,16,512]{2,1,0:T(8,128)S(1)} collective-permute-done((f32[8,16,512]{2,1,0:T(8,128)S(1)}, f32[8,16,512]{2,1,0:T(8,128)S(1)}, u32[]{:S(2)}, u32[]{:S(2)}) %collective-permute-start.7) | collective-permute-done | bytes 262176 | tf_op jit(solution)/shard_map/ppermute | solution.py:473
  64.4 0.0 collective-permute-done.6.refs_3_
  64.4 0.9 %collective-permute-done.5.refs_2_ = f32[8,16,512]{2,1,0:T(8,128)S(1)} collective-permute-done((f32[8,16,512]{2,1,0:T(8,128)S(1)}, f32[8,16,512]{2,1,0:T(8,128)S(1)}, u32[]{:S(2)}, u32[]{:S(2)}) %collective-permute-start.5) | collective-permute-done | bytes 262176 | tf_op jit(solution)/shard_map/ppermute | solution.py:473
  65.3 1.8 %shard_map.88 = f32[16,1,8,512]{3,2,1,0:T(8,128)} custom-call(f32[256,128]{1,0:T(8,128)S(1)} %bitcast.6, f32[8,16,512]{2,1,0:T(8,128)S(1)} %get-tuple-element.23.refs_1_, f32[8,16,512]{2,1,0:T(8,128)S(1)} %collective-permute-done.5.refs_2_, f32[8,16,512]{2,1,0:T(8,128)S(1)} %collective-permute-done.6.refs_3_, ...), custom_call_target="tpu_custom_call" | custom-call | flops 201326592 | bytes 2998272 | tf_op jit(solution)/shard_map/pallas_call | solution.py:488
  (7 shorter events, 0.0 us)
Async XLA Ops:
  5.6 30.9 %copy-start.3 = (bf16[4,256,256]{2,1,0:T(8,128)(2,1)}, bf16[4,256,256]{2,1,0:T(8,128)(2,1)S(1)}, u32[]{:S(2)}) copy-start(bf16[4,256,256]{2,1,0:T(8,128)(2,1)S(1)} %get-tuple-element.22.tables_ref) | copy-start | bytes 1572868
  5.6 30.9 %collective-permute-start.4 = (f32[8,16,512]{2,1,0:T(8,128)S(1)}, f32[8,16,512]{2,1,0:T(8,128)S(1)}, u32[]{:S(2)}, u32[]{:S(2)}) collective-permute-start(f32[8,16,512]{2,1,0:T(8,128)S(1)} %get-tuple-element.18.own_ref.refs_1_), channel_id=1, source_target_pairs={{192,0},{0,64},{64,128},{128,192},{193,1},{1,65},{65,129},{129,193... | collective-permute-start | bytes 786440 | tf_op jit(solution)/shard_map/ppermute | solution.py:473
  7.7 28.8 %collective-permute-start.3 = (f32[8,16,512]{2,1,0:T(8,128)S(1)}, f32[8,16,512]{2,1,0:T(8,128)S(1)}, u32[]{:S(2)}, u32[]{:S(2)}) collective-permute-start(f32[8,16,512]{2,1,0:T(8,128)S(1)} %get-tuple-element.18.own_ref.refs_1_), channel_id=1, source_target_pairs={{128,0},{192,64},{0,128},{64,192},{129,1},{193,65},{1,129},{65,193... | collective-permute-start | bytes 786440 | tf_op jit(solution)/shard_map/ppermute | solution.py:473
  10.2 26.3 %collective-permute-start.2 = (f32[8,16,512]{2,1,0:T(8,128)S(1)}, f32[8,16,512]{2,1,0:T(8,128)S(1)}, u32[]{:S(2)}, u32[]{:S(2)}) collective-permute-start(f32[8,16,512]{2,1,0:T(8,128)S(1)} %get-tuple-element.18.own_ref.refs_1_), channel_id=1, source_target_pairs={{64,0},{128,64},{192,128},{0,192},{65,1},{129,65},{193,129},{1,193... | collective-permute-start | bytes 786440 | tf_op jit(solution)/shard_map/ppermute | solution.py:473
  11.4 32.9 %collective-permute-start.1 = (f32[8,16,512]{2,1,0:T(8,128)S(1)}, f32[8,16,512]{2,1,0:T(8,128)S(1)}, u32[]{:S(2)}, u32[]{:S(2)}) collective-permute-start(f32[8,16,512]{2,1,0:T(8,128)S(1)} %get-tuple-element.18.own_ref.refs_1_), channel_id=1, source_target_pairs={{0,1},{1,2},{2,3},{3,4},{4,5},{5,6},{6,7},{7,8},{8,9},{9,10},{10,1... | collective-permute-start | bytes 786440 | tf_op jit(solution)/shard_map/ppermute | solution.py:483
  16.3 28.0 %collective-permute-start = (f32[8,16,512]{2,1,0:T(8,128)S(1)}, f32[8,16,512]{2,1,0:T(8,128)S(1)}, u32[]{:S(2)}, u32[]{:S(2)}) collective-permute-start(f32[8,16,512]{2,1,0:T(8,128)S(1)} %get-tuple-element.18.own_ref.refs_1_), channel_id=1, source_target_pairs={{1,0},{2,1},{3,2},{4,3},{5,4},{6,5},{7,6},{8,7},{9,8},{10,9},{11,1... | collective-permute-start | bytes 786440 | tf_op jit(solution)/shard_map/ppermute | solution.py:482
  18.2 26.0 %all-to-all-start = ((f32[256,1,128]{2,1,0:T(1,128)}), f32[256,1,128]{2,1,0:T(1,128)S(1)}, u32[]{:S(2)}, u32[]{:S(2)}) async-start(f32[256,1,128]{2,1,0:T(1,128)} %bitcast.1), calls=%async_computation | async-start | bytes 262144 | tf_op jit(solution)/shard_map/all_to_all | solution.py:456
  31.4 5.2 %copy-start = (bf16[128,384]{1,0:T(8,128)(2,1)S(1)}, bf16[128,384]{1,0:T(8,128)(2,1)}, u32[]{:S(2)}) copy-start(bf16[128,384]{1,0:T(8,128)(2,1)} %constant.11.clone.table_ref.refs_7_) | copy-start | bytes 294916
  31.4 12.9 %copy-start.2 = (bf16[32,384]{1,0:T(8,128)(2,1)S(1)}, bf16[32,384]{1,0:T(8,128)(2,1)}, u32[]{:S(2)}) copy-start(bf16[32,384]{1,0:T(8,128)(2,1)} %constant.12.clone.refs_6_.refs_8_) | copy-start | bytes 73732
  45.2 14.5 %collective-permute-start.9 = (f32[8,16,512]{2,1,0:T(8,128)S(1)}, f32[8,16,512]{2,1,0:T(8,128)S(1)}, u32[]{:S(2)}, u32[]{:S(2)}) collective-permute-start(f32[8,16,512]{2,1,0:T(8,128)S(1)} %get-tuple-element.23.refs_1_), channel_id=1, source_target_pairs={{0,1},{1,2},{2,3},{3,4},{4,5},{5,6},{6,7},{7,8},{8,9},{9,10},{10,1... | collective-permute-start | bytes 786440 | tf_op jit(solution)/shard_map/ppermute | solution.py:483
  48.8 11.0 %collective-permute-start.8 = (f32[8,16,512]{2,1,0:T(8,128)S(1)}, f32[8,16,512]{2,1,0:T(8,128)S(1)}, u32[]{:S(2)}, u32[]{:S(2)}) collective-permute-start(f32[8,16,512]{2,1,0:T(8,128)S(1)} %get-tuple-element.23.refs_1_), channel_id=1, source_target_pairs={{1,0},{2,1},{3,2},{4,3},{5,4},{6,5},{7,6},{8,7},{9,8},{10,9},{11,1... | collective-permute-start | bytes 786440 | tf_op jit(solution)/shard_map/ppermute | solution.py:482
  50.7 13.7 %collective-permute-start.7 = (f32[8,16,512]{2,1,0:T(8,128)S(1)}, f32[8,16,512]{2,1,0:T(8,128)S(1)}, u32[]{:S(2)}, u32[]{:S(2)}) collective-permute-start(f32[8,16,512]{2,1,0:T(8,128)S(1)} %get-tuple-element.23.refs_1_), channel_id=1, source_target_pairs={{192,0},{0,64},{64,128},{128,192},{193,1},{1,65},{65,129},{129,193... | collective-permute-start | bytes 786440 | tf_op jit(solution)/shard_map/ppermute | solution.py:473
  51.1 13.3 %collective-permute-start.6 = (f32[8,16,512]{2,1,0:T(8,128)S(1)}, f32[8,16,512]{2,1,0:T(8,128)S(1)}, u32[]{:S(2)}, u32[]{:S(2)}) collective-permute-start(f32[8,16,512]{2,1,0:T(8,128)S(1)} %get-tuple-element.23.refs_1_), channel_id=1, source_target_pairs={{128,0},{192,64},{0,128},{64,192},{129,1},{193,65},{1,129},{65,193... | collective-permute-start | bytes 786440 | tf_op jit(solution)/shard_map/ppermute | solution.py:473
  52.8 12.5 %collective-permute-start.5 = (f32[8,16,512]{2,1,0:T(8,128)S(1)}, f32[8,16,512]{2,1,0:T(8,128)S(1)}, u32[]{:S(2)}, u32[]{:S(2)}) collective-permute-start(f32[8,16,512]{2,1,0:T(8,128)S(1)} %get-tuple-element.23.refs_1_), channel_id=1, source_target_pairs={{64,0},{128,64},{192,128},{0,192},{65,1},{129,65},{193,129},{1,193... | collective-permute-start | bytes 786440 | tf_op jit(solution)/shard_map/ppermute | solution.py:473
  53.6 1.0 %copy-start.4 = (bf16[4,256,256]{2,1,0:T(8,128)(2,1)S(1)}, bf16[4,256,256]{2,1,0:T(8,128)(2,1)}, u32[]{:S(2)}) copy-start(bf16[4,256,256]{2,1,0:T(8,128)(2,1)} %copy-done.3) | copy-start | bytes 1572868
  54.6 10.7 %copy-start.1 = (bf16[256,256]{1,0:T(8,128)(2,1)S(1)}, bf16[256,256]{1,0:T(8,128)(2,1)}, u32[]{:S(2)}) copy-start(bf16[256,256]{1,0:T(8,128)(2,1)} %constant.14.clone.refs_9_) | copy-start | bytes 393220

commit v2 on v1

--- a/solution.py
+++ b/solution.py
@@ -247,11 +247,6 @@
     return left_product(table, jnp.concatenate([re, im], 0))
 
 
-def frequency_kernel(own_ref, one_ref, two_ref, three_ref, table_ref, out_ref):
-    for x in range(own_ref.shape[0]):
-        out_ref[x] = frequencies((own_ref, one_ref, two_ref, three_ref), x, table_ref[...])
-
-
 def level(energy_ref, cells):
     total = jnp.sum(energy_ref[...], axis=0, keepdims=True)
     return jnp.sqrt(total / cells + EPSILON)
@@ -317,6 +312,12 @@
     return clip_space(duals, limit)
 
 
+def around(near_ref, far_ref):
+    even = lax.axis_index("cuts") % 2 == 0
+    near, far = near_ref[...], far_ref[...]
+    return jnp.where(even, near, far), jnp.where(even, far, near)
+
+
 def space_part(own, above, below, x, rows_before, has_below, old, old_below, limit):
     duals = space_step(own, above, x, old, limit)
     duals_below = space_step(below, own, x, old_below, limit)
@@ -326,23 +327,56 @@
     return total, duals, duals_below
 
 
-def first_kernel(
-    cells, energy_ref, own_ref, above_ref, below_ref, normal_ref, frequency_ref,
-    table_ref,
-    base_ref, bar_x_ref, bar_ref, time_ref, space_ref, space_below_ref,
+def in_turn(own_ref, one_ref, two_ref, three_ref):
+    even = lax.axis_index("frame") % 2 == 0
+    one, three = one_ref[...], three_ref[...]
+    return own_ref, jnp.where(even, one, three), two_ref, jnp.where(even, three, one)
+
+
+def time_fields(blocks, level, old, fore_ref, back_ref, field_ref):
+    places = range(field_ref.shape[0])
+    limit = LAM_TIME * cat(level, level)
+    duals = [SIGMA * frequencies(blocks, x, fore_ref[...]) for x in places]
+    if old is not None:
+        duals = [old[x] + dual for x, dual in zip(places, duals)]
+    duals = [clip_time(dual, limit) for dual in duals]
+    for x, dual in zip(places, duals):
+        field_ref[x] = frames_of(dual, back_ref[...])
+    return duals
+
+
+def first_time_kernel(
+    cells, energy_ref, own_ref, one_ref, two_ref, three_ref, fore_ref, back_ref,
+    dual_ref, field_ref, level_ref,
 ):
     rms_level = level(energy_ref, cells)
-    limit_time, limit_space = LAM_TIME * rms_level, LAM_SPACE * rms_level
-    limit_wide = cat(limit_time, limit_time)
+    level_ref[...] = jnp.broadcast_to(rms_level, level_ref.shape)
+    blocks = in_turn(own_ref, one_ref, two_ref, three_ref)
+    duals = time_fields(blocks, rms_level, None, fore_ref, back_ref, field_ref)
+    for x, dual in enumerate(duals):
+        dual_ref[x] = dual
+
+
+def last_time_kernel(
+    level_ref, own_ref, one_ref, two_ref, three_ref, dual_ref, fore_ref, back_ref, field_ref
+):
+    blocks = in_turn(own_ref, one_ref, two_ref, three_ref)
+    time_fields(blocks, level_ref[0:1, :], dual_ref, fore_ref, back_ref, field_ref)
+
+
+def first_space_kernel(
+    level_ref, own_ref, near_ref, far_ref, normal_ref, field_ref,
+    base_ref, bar_x_ref, bar_ref, space_ref, space_below_ref,
+):
+    limit_space = LAM_SPACE * level_ref[0:1, :]
     has_below = (lax.axis_index("cuts") > 0).astype(F32)
+    above, below = around(near_ref, far_ref)
     normal = jnp.swapaxes(normal_ref[...], 0, 1)
     rows_before = jnp.zeros(own_ref.shape[1:], F32)
     bars = []
     for x in range(own_ref.shape[0]):
-        dual = clip_time(SIGMA * frequency_ref[x], limit_wide)
-        time_ref[x] = dual
         total, duals, duals_below = space_part(
-            own_ref, above_ref, below_ref, x, rows_before, has_below, None, None, limit_space
+            own_ref, above, below, x, rows_before, has_below, None, None, limit_space
         )
         rows_before = duals[1]
         for index in range(3):
@@ -350,7 +384,7 @@
             space_below_ref[index, x] = duals_below[index]
         initial = own_ref[x]
         data_part = TAKE * (normal[x] - initial)
-        updated = initial - TAU * (data_part + frames_of(dual, table_ref[...]) + total)
+        updated = initial - TAU * (data_part + field_ref[x] + total)
         base_ref[x] = updated - TAU * (KEEP * data_part - TAKE * initial)
         bar = 2.0 * updated - initial
         bar_x_ref[x] = bar
@@ -358,45 +392,36 @@
     bar_ref[...] = jnp.swapaxes(jnp.stack(bars, 0), 0, 1)
 
 
-def space_kernel(
-    cells, energy_ref, own_ref, above_ref, below_ref, normal_ref, base_ref,
-    space_ref, space_below_ref,
+def last_space_kernel(
+    level_ref, own_ref, near_ref, far_ref, normal_ref, field_ref, base_ref,
+    space_ref, space_below_ref, part_ref,
     out_ref,
 ):
-    limit_space = LAM_SPACE * level(energy_ref, cells)
+    limit_space = LAM_SPACE * level_ref[0:1, :]
     has_below = (lax.axis_index("cuts") > 0).astype(F32)
+    above, below = around(near_ref, far_ref)
     normal = jnp.swapaxes(normal_ref[...], 0, 1)
     rows_before = jnp.zeros(own_ref.shape[1:], F32)
+    images = []
     for x in range(own_ref.shape[0]):
         total, duals, _ = space_part(
-            own_ref, above_ref, below_ref, x, rows_before, has_below,
+            own_ref, above, below, x, rows_before, has_below,
             space_ref, space_below_ref, limit_space,
         )
         rows_before = duals[1]
-        out_ref[x] = base_ref[x] - TAU * (TAKE * normal[x] + total)
-
-
-def last_kernel(
-    cells, energy_ref, own_ref, one_ref, two_ref, three_ref, time_ref, base_ref,
-    fore_ref, back_ref, part_ref,
-    out_ref,
-):
-    limit_time = LAM_TIME * level(energy_ref, cells)
-    limit_wide = cat(limit_time, limit_time)
-    blocks = (own_ref, one_ref, two_ref, three_ref)
-    places = range(own_ref.shape[0])
-    duals = [
-        time_ref[x] + SIGMA * frequencies(blocks, x, fore_ref[...]) for x in places
-    ]
-    duals = [clip_time(dual, limit_wide) for dual in duals]
-    images = [base_ref[x] - TAU * frames_of(duals[x], back_ref[...]) for x in places]
-    count, size = len(images), images[0].shape[0]
+        images.append(base_ref[x] - TAU * (TAKE * normal[x] + field_ref[x] + total))
     image = jnp.concatenate(images, 0)
     re_even, im_even, re_odd, im_odd = quarters(image)
     image = cat(
         moved(cat(re_even, re_odd), part_ref[...]), moved(cat(im_even, im_odd), part_ref[...])
     )
-    out_ref[:, 0] = jnp.swapaxes(image.reshape(count, size, image.shape[-1]), 0, 1)
+    out_ref[:, 0] = jnp.swapaxes(image.reshape(own_ref.shape), 0, 1)
+
+
+def stages(blocks, cuts):
+    rows = 4 if cuts % 4 == 0 else 1
+    index = np.arange(blocks * cuts).reshape(blocks * rows, cuts // rows)
+    return index.T.tolist(), index.tolist()
 
 
 def params():
@@ -417,7 +442,7 @@
     blocks = lax.axis_size("frame")
     slices_all = slices_here * lax.axis_size("cuts")
     frames_all = frames_here * blocks
-    devices = blocks * lax.axis_size("cuts")
+    inner, outer = stages(blocks, lax.axis_size("cuts"))
     cells = float(frames_all * slices_all * readout * positions)
     tables = jnp.asarray(line_tables(positions))
     time_fore, time_back = (jnp.asarray(table) for table in time_tables(frames_all, frames_here))
@@ -434,7 +459,7 @@
         in_specs=[hbm] * 5,
         out_specs=[vmem] * 6,
         out_shape=[
-            struct(*turned), struct(*plane), struct(devices, 128),
+            struct(*turned), struct(*plane), struct(len(inner[0]), 128),
             pltpu.VMEM((coils, readout, doubled), F32),
             pltpu.VMEM(tables.shape, BF16),
             pltpu.VMEM(sampling.shape, jnp.int32),
@@ -453,7 +478,9 @@
         for array in (measured, coil_maps, sampling, tables, part)
     ))
 
-    energies = lax.all_to_all(energy, AXES, 0, 0, tiled=True)
+    energies = lax.all_to_all(energy, AXES, 0, 0, tiled=True, axis_index_groups=inner)
+    energies = jnp.broadcast_to(jnp.sum(energies, axis=0, keepdims=True), (len(outer[0]), 128))
+    energies = lax.all_to_all(energies, AXES, 0, 0, tiled=True, axis_index_groups=outer)
 
     def normal(image):
         return pl.pallas_call(
@@ -470,18 +497,15 @@
 
     def gathered(image):
         others = [
-            lax.ppermute(
-                image, "frame", [((index + by) % blocks, index) for index in range(blocks)]
-            )
+            lax.ppermute(image, "frame", [(index, index ^ by) for index in range(blocks)])
             for by in range(1, blocks)
         ]
         return [image] + others
 
     def neighbours(image):
         count = lax.axis_size("cuts")
-        above = lax.ppermute(image, "cuts", [(i + 1, i) for i in range(count - 1)])
-        below = lax.ppermute(image, "cuts", [(i, i + 1) for i in range(count - 1)])
-        return above, below
+        pairs = [[(i, i ^ 1) for i in range(count)], [(i, ((i + 1) ^ 1) - 1) for i in range(1, count - 1)]]
+        return [lax.ppermute(image, "cuts", pair) for pair in pairs]
 
 
     def call(kernel, args, out_shape, flops):
@@ -494,43 +518,42 @@
             cost_estimate=cost(flops, sum(arg.size * 4 for arg in args)),
         )(*args)
 
-    time_flops = 6 * (2 * frames_all) ** 2 * readout * positions
+    time_flops = 7 * (2 * frames_all) ** 2 * readout * positions
+    dual_shape = struct(readout, 2 * frames_all, positions)
+    duals_shape = struct(3, *plane)
+
+    def first_time(*refs):
+        first_time_kernel(cells, *refs)
+
     all_blocks = gathered(initial_x)
-    above, below = neighbours(initial_x)
+    pair_near, pair_far = neighbours(initial_x)
     normal_initial = normal(initial)
-    frequency_shape = struct(readout, 2 * frames_all, positions)
-    frequency = call(frequency_kernel, all_blocks + [time_fore], frequency_shape, time_flops)
-    duals_shape = struct(3, *plane)
-
-    def first(*refs):
-        first_kernel(cells, *refs)
-
-    def space(*refs):
-        space_kernel(cells, *refs)
-
-    def last(*refs):
-        last_kernel(cells, *refs)
-
-    base, bar_x, bar, time_dual, space_dual, space_below = call(
-        first,
-        [energies, initial_x, above, below, normal_initial, frequency, time_back],
-        [struct(*plane), struct(*plane), struct(*turned), frequency_shape, duals_shape, duals_shape],
-        time_flops // 4,
+    time_dual, field, rms_level = call(
+        first_time,
+        [energies] + all_blocks + [time_fore, time_back],
+        [dual_shape, struct(*plane), struct(8, 128)],
+        time_flops,
+    )
+    base, bar_x, bar, space_dual, space_below = call(
+        first_space_kernel,
+        [rms_level, initial_x, pair_near, pair_far, normal_initial, field],
+        [struct(*plane), struct(*plane), struct(*turned), duals_shape, duals_shape],
+        1000000,
     )
     all_blocks = gathered(bar_x)
-    above, below = neighbours(bar_x)
+    pair_near, pair_far = neighbours(bar_x)
     normal_bar = normal(bar)
-    base = call(
-        space,
-        [energies, bar_x, above, below, normal_bar, base, space_dual, space_below],
+    field = call(
+        last_time_kernel,
+        [rms_level] + all_blocks + [time_dual, time_fore, time_back],
         struct(*plane),
+        time_flops,
+    )
+    return call(
+        last_space_kernel,
+        [rms_level, bar_x, pair_near, pair_far, normal_bar, field, base, space_dual, space_below, unpart],
+        struct(frames_here, slices_here, readout, doubled),
         1000000,
-    )
-    return call(
-        last,
-        [energies] + all_blocks + [time_dual, base, time_fore, time_back, unpart],
-        struct(frames_here, slices_here, readout, doubled),
-        time_flops,
     )
 
 

time: 67.3 us -> 56.5 us (0.84)
  waiting for transfers between devices: 12.3 us -> 4.36 us
  starting transfers between devices: 34 us -> 31.6 us
    ppermute x10, starting transfers between devices: 20.9 us -> 15.2 us  [the longest x4 8.27 us: neighbours(): return [lax.ppermute(image, 'cuts', pair) for pair in pairs]]
    all_to_all x1 -> x2, waiting for transfers between devices: 7.23 us -> 1.96 us  [the longest x1 1.96 us: shards(): lax.all_to_all(energies, AXES, 0, 0, tiled=True, axis_index_groups=outer)]
    all_to_all x1 -> x2, starting transfers between devices: 13.1 us -> 16.4 us  [the longest x1 8.8 us: shards(): lax.all_to_all(energies, AXES, 0, 0, tiled=True, axis_index_groups=outer)]
    ppermute x10, waiting for transfers between devices: 5.09 us -> 2.4 us  [the longest x6 2.37 us: gathered(): lax.ppermute(image, 'frame', [(index, index ^ by) for index in range(bloc...]
    unnamed x10 -> x6, local copies, waits for them, and re-layouts: 1.06 us -> 0.02 us
  transfers between devices with their start and end apart: 11 -> 12, of which waited for: 3 -> 3; matrix products, arithmetic and copies ran while one was open for 0% -> 1% of each run, Pallas kernels for 17% -> 21%
where the time goes in v2:
time: 56.5 us; the launch traced here: 55.9 us
  starting transfers between devices  31.6 us (56%)
  Pallas kernels  19.1 us (34%)
  waiting for transfers between devices  4.36 us (8%)
  local copies, waits for them, and re-layouts  0.62 us (1%)
    pallas_call x2, Pallas kernels, normal(): pl.pallas_call(normal_kernel, in_specs=[vmem] * 4, out_specs=vmem, out_sh...  9.91 us
    all_to_all x1, starting transfers between devices, shards(): lax.all_to_all(energies, AXES, 0, 0, tiled=True, axis_index_groups=outer)  8.8 us
    ppermute x4, starting transfers between devices, neighbours(): return [lax.ppermute(image, 'cuts', pair) for pair in pairs]  8.27 us
    all_to_all x1, starting transfers between devices, shards(): lax.all_to_all(energy, AXES, 0, 0, tiled=True, axis_index_groups=inner)  7.6 us
    ppermute x6, starting transfers between devices, gathered(): lax.ppermute(image, 'frame', [(index, index ^ by) for index in range(bloc...  6.98 us
    pallas_call x1, Pallas kernels, shards(): pl.pallas_call(initial_kernel, in_specs=[hbm] * 5, out_specs=[vmem] * 6,...  5.4 us
    pallas_call x4, Pallas kernels, call(): pl.pallas_call(kernel, in_specs=[vmem] * len(args), out_specs=jax.tree.ma...  3.77 us
    ppermute x6, waiting for transfers between devices, gathered(): lax.ppermute(image, 'frame', [(index, index ^ by) for index in range(bloc...  2.37 us
  transfers between devices with their start and end apart: 12, of which 3 were waited for; matrix products, arithmetic and copies ran while one was open for 1% of the time, Pallas kernels for 21%

profile of v2, /device:TPU:1, one launch (start us, length us, event | category | flops | bytes accessed | tf_op | source)
XLA Modules:
  0.0 55.9 jit_solution(9921406191143988428)
XLA Ops:
  0.0 5.4 %shard_map.82 = (f32[16,8,512]{2,1,0:T(8,128)S(1)}, f32[8,16,512]{2,1,0:T(8,128)S(1)}, f32[16,128]{1,0:T(8,128)}, f32[20,8,512]{2,1,0:T(8,128)S(1)}, bf16[4,256,...) custom-call(f32[16,1,20,8,512]{4,3,2,1,0:T(8,128)} %measured_hbm.1, f32[1,20,8,512]{3,2,1,0:T(8,128)} %maps_hbm.1, ...), custom_call_target="tpu_custom_call" | custom-call | flops 2013265920 | bytes 5242880 | tf_op jit(solution)/shard_map/pallas_call | solution.py:457
  5.4 7.6 %all-to-all-start = ((f32[16,1,128]{2,1,0:T(1,128)}), f32[16,1,128]{2,1,0:T(1,128)S(1)}, u32[]{:S(2)}, u32[]{:S(2)}) async-start(f32[16,1,128]{2,1,0:T(1,128)} %bitcast.1), calls=%async_computation | async-start | bytes 16384 | tf_op jit(solution)/shard_map/all_to_all | solution.py:481
  13.0 4.4 %collective-permute-start.4 = (f32[8,16,512]{2,1,0:T(8,128)S(1)}, f32[8,16,512]{2,1,0:T(8,128)S(1)}, u32[]{:S(2)}, u32[]{:S(2)}) collective-permute-start(f32[8,16,512]{2,1,0:T(8,128)S(1)} %get-tuple-element.20.refs_1_.own_ref), channel_id=1, source_target_pairs={{1,2},{2,1},{3,4},{4,3},{5,6},{6,5},{7,8},{8,7},{9,10},{10,9},{11,... | collective-permute-start | bytes 786440 | tf_op jit(solution)/shard_map/ppermute | solution.py:508
  17.4 0.1 collective-permute-start.3
  17.5 2.9 %collective-permute-start.2 = (f32[8,16,512]{2,1,0:T(8,128)S(1)}, f32[8,16,512]{2,1,0:T(8,128)S(1)}, u32[]{:S(2)}, u32[]{:S(2)}) collective-permute-start(f32[8,16,512]{2,1,0:T(8,128)S(1)} %get-tuple-element.20.refs_1_.own_ref), channel_id=1, source_target_pairs={{0,192},{64,128},{128,64},{192,0},{1,193},{65,129},{129,65},{193,1... | collective-permute-start | bytes 786440 | tf_op jit(solution)/shard_map/ppermute | solution.py:500
  20.4 0.6 %collective-permute-start.1 = (f32[8,16,512]{2,1,0:T(8,128)S(1)}, f32[8,16,512]{2,1,0:T(8,128)S(1)}, u32[]{:S(2)}, u32[]{:S(2)}) collective-permute-start(f32[8,16,512]{2,1,0:T(8,128)S(1)} %get-tuple-element.20.refs_1_.own_ref), channel_id=1, source_target_pairs={{0,128},{64,192},{128,0},{192,64},{1,129},{65,193},{129,1},{193,65... | collective-permute-start | bytes 786440 | tf_op jit(solution)/shard_map/ppermute | solution.py:500
  21.0 0.1 collective-permute-start
  21.1 0.0 all-to-all-done
  21.2 0.6 %broadcast_in_dim.2 = f32[16,1,128]{2,1,0:T(1,128)} broadcast(f32[128]{0:T(128)S(1)} %reduce_sum.9), dimensions={2} | broadcast | bytes 8704 | tf_op jit(solution)/shard_map/broadcast_in_dim | solution.py:482
  21.8 8.8 %all-to-all-start.1 = ((f32[16,1,128]{2,1,0:T(1,128)}), f32[16,1,128]{2,1,0:T(1,128)S(1)}, u32[]{:S(2)}, u32[]{:S(2)}) async-start(f32[16,1,128]{2,1,0:T(1,128)} %broadcast_in_dim.2), calls=%async_computation.1 | async-start | bytes 16384 | tf_op jit(solution)/shard_map/all_to_all | solution.py:483
  30.6 0.0 copy-start.2
  30.6 5.0 %shard_map.84.normal_ref = f32[16,8,512]{2,1,0:T(8,128)S(1)} custom-call(f32[16,8,512]{2,1,0:T(8,128)S(1)} %get-tuple-element.22.image_ref, f32[20,8,512]{2,1,0:T(8,128)S(1)} %get-tuple-element.23.maps_ref, s32[16,256]{1,0:T(8,128)S(1)} %get-tuple-element.24.sampling_ref, bf16[4,256,256]{2,1,0:T(8,128)(2,1)S(1)} %get-tuple-element.25.tables_ref), custom_call_target="tpu_custom_call" | custom-call | flops 4026531840 | bytes 524288 | tf_op jit(solution)/shard_map/pallas_call | solution.py:486
  35.5 2.0 %all-to-all-done.1 = f32[16,1,128]{2,1,0:T(1,128)S(1)} async-done(((f32[16,1,128]{2,1,0:T(1,128)}), f32[16,1,128]{2,1,0:T(1,128)S(1)}, u32[]{:S(2)}, u32[]{:S(2)}) %all-to-all-start.1) | async-done | bytes 8224 | tf_op jit(solution)/shard_map/all_to_all | solution.py:483
  37.5 0.0 collective-permute-done.2.refs_4_
  37.5 0.0 collective-permute-done.1.refs_3_
  37.5 0.0 collective-permute-done.refs_2_
  37.5 0.8 %shard_map.83 = (f32[8,128,256]{2,1,0:T(8,128)S(1)}, f32[8,16,512]{2,1,0:T(8,128)S(1)}, f32[8,128]{1,0:T(8,128)S(1)}) custom-call(f32[16,128]{1,0:T(8,128)S(1)} %bitcast.4, f32[8,16,512]{2,1,0:T(8,128)S(1)} %get-tuple-element.20.refs_1_.own_ref, f32[8,16,512]{2,1,0:T(8,128)S(1)} %collective-permute-done.refs_2_, ...), custom_call_target="tpu_custom_call" | custom-call | flops 234881024 | bytes 1302528 | tf_op jit(solution)/shard_map/pallas_call | solution.py:512
  38.3 0.0 collective-permute-done.4.far_ref
  38.4 0.6 %shard_map.85 = (f32[8,16,512]{2,1,0:T(8,128)S(1)}, f32[8,16,512]{2,1,0:T(8,128)S(1)}, f32[16,8,512]{2,1,0:T(8,128)S(1)}, f32[3,8,16,512]{3,2,1,0:T(8,128)S(1)}, f32[3,8,16,512]{3,2,1,0:T(8,128)S(1)}) custom-call(f32[8,128]{1,0:T(8,128)S(1)} %get-tuple-element.21.level_ref, f32[8,16,512]{2,1,0:T(8,128)S(1)} %get-tuple-element.20.refs_1_.own_ref, ...), custom_call_target="tpu_custom_call" | custom-call | flops 1000000 | bytes 1314816 | tf_op jit(solution)/shard_map/pallas_call | solution.py:512
  39.0 2.7 %collective-permute-start.9 = (f32[8,16,512]{2,1,0:T(8,128)S(1)}, f32[8,16,512]{2,1,0:T(8,128)S(1)}, u32[]{:S(2)}, u32[]{:S(2)}) collective-permute-start(f32[8,16,512]{2,1,0:T(8,128)S(1)} %get-tuple-element.27.own_ref), channel_id=1, source_target_pairs={{0,192},{64,128},{128,64},{192,0},{1,193},{65,129},{129,65},{193,1... | collective-permute-start | bytes 786440 | tf_op jit(solution)/shard_map/ppermute | solution.py:500
  41.7 0.6 %collective-permute-start.8 = (f32[8,16,512]{2,1,0:T(8,128)S(1)}, f32[8,16,512]{2,1,0:T(8,128)S(1)}, u32[]{:S(2)}, u32[]{:S(2)}) collective-permute-start(f32[8,16,512]{2,1,0:T(8,128)S(1)} %get-tuple-element.27.own_ref), channel_id=1, source_target_pairs={{0,128},{64,192},{128,0},{192,64},{1,129},{65,193},{129,1},{193,65... | collective-permute-start | bytes 786440 | tf_op jit(solution)/shard_map/ppermute | solution.py:500
  42.2 0.1 collective-permute-start.7
  42.3 3.5 %collective-permute-start.6 = (f32[8,16,512]{2,1,0:T(8,128)S(1)}, f32[8,16,512]{2,1,0:T(8,128)S(1)}, u32[]{:S(2)}, u32[]{:S(2)}) collective-permute-start(f32[8,16,512]{2,1,0:T(8,128)S(1)} %get-tuple-element.27.own_ref), channel_id=1, source_target_pairs={{1,2},{2,1},{3,4},{4,3},{5,6},{6,5},{7,8},{8,7},{9,10},{10,9},{11,... | collective-permute-start | bytes 786440 | tf_op jit(solution)/shard_map/ppermute | solution.py:508
  45.9 0.3 collective-permute-start.5
  46.1 0.0 copy-start.1
  46.2 5.0 %shard_map.86.normal_ref = f32[16,8,512]{2,1,0:T(8,128)S(1)} custom-call(f32[16,8,512]{2,1,0:T(8,128)S(1)} %get-tuple-element.28.image_ref, f32[20,8,512]{2,1,0:T(8,128)S(1)} %get-tuple-element.23.maps_ref, s32[16,256]{1,0:T(8,128)S(1)} %get-tuple-element.24.sampling_ref, bf16[4,256,256]{2,1,0:T(8,128)(2,1)S(1)} %get-tuple-element.25.tables_ref), custom_call_target="tpu_custom_call" | custom-call | flops 4026531840 | bytes 524288 | tf_op jit(solution)/shard_map/pallas_call | solution.py:486
  51.1 2.0 %collective-permute-done.9.three_ref = f32[8,16,512]{2,1,0:T(8,128)S(1)} collective-permute-done((f32[8,16,512]{2,1,0:T(8,128)S(1)}, f32[8,16,512]{2,1,0:T(8,128)S(1)}, u32[]{:S(2)}, u32[]{:S(2)}) %collective-permute-start.9) | collective-permute-done | bytes 262176 | tf_op jit(solution)/shard_map/ppermute | solution.py:500
  53.1 0.0 collective-permute-done.8.two_ref
  53.1 0.4 collective-permute-done.7.one_ref
  53.5 0.9 %shard_map.87.field_ref = f32[8,16,512]{2,1,0:T(8,128)S(1)} custom-call(f32[8,128]{1,0:T(8,128)S(1)} %get-tuple-element.21.level_ref, f32[8,16,512]{2,1,0:T(8,128)S(1)} %get-tuple-element.27.own_ref, f32[8,16,512]{2,1,0:T(8,128)S(1)} %collective-permute-done.7.one_ref, f32[8,16,512]{2,1,0:T(8,128)S(1)} %collective-permute-done.8.two_ref, ...), custom_call_target="tpu_custom_call" | custom-call | flops 234881024 | bytes 2347008 | tf_op jit(solution)/shard_map/pallas_call | solution.py:512
  54.3 0.0 collective-permute-done.6.far_ref
  54.4 1.5 %shard_map.88 = f32[16,1,8,512]{3,2,1,0:T(8,128)} custom-call(f32[8,128]{1,0:T(8,128)S(1)} %get-tuple-element.21.level_ref, f32[8,16,512]{2,1,0:T(8,128)S(1)} %get-tuple-element.27.own_ref, f32[8,16,512]{2,1,0:T(8,128)S(1)} %collective-permute-done.5.near_ref, f32[8,16,512]{2,1,0:T(8,128)S(1)} %collective-permute-done.6.far_ref, ...), custom_call_target="tpu_custom_call" | custom-call | flops 1000000 | bytes 3411968 | tf_op jit(solution)/shard_map/pallas_call | solution.py:512
  (7 shorter events, 0.0 us)
Async XLA Ops:
  5.4 15.7 %all-to-all-start = ((f32[16,1,128]{2,1,0:T(1,128)}), f32[16,1,128]{2,1,0:T(1,128)S(1)}, u32[]{:S(2)}, u32[]{:S(2)}) async-start(f32[16,1,128]{2,1,0:T(1,128)} %bitcast.1), calls=%async_computation | async-start | bytes 16384 | tf_op jit(solution)/shard_map/all_to_all | solution.py:481
  13.0 25.3 %collective-permute-start.4 = (f32[8,16,512]{2,1,0:T(8,128)S(1)}, f32[8,16,512]{2,1,0:T(8,128)S(1)}, u32[]{:S(2)}, u32[]{:S(2)}) collective-permute-start(f32[8,16,512]{2,1,0:T(8,128)S(1)} %get-tuple-element.20.refs_1_.own_ref), channel_id=1, source_target_pairs={{1,2},{2,1},{3,4},{4,3},{5,6},{6,5},{7,8},{8,7},{9,10},{10,9},{11,... | collective-permute-start | bytes 786440 | tf_op jit(solution)/shard_map/ppermute | solution.py:508
  17.4 21.0 %collective-permute-start.3 = (f32[8,16,512]{2,1,0:T(8,128)S(1)}, f32[8,16,512]{2,1,0:T(8,128)S(1)}, u32[]{:S(2)}, u32[]{:S(2)}) collective-permute-start(f32[8,16,512]{2,1,0:T(8,128)S(1)} %get-tuple-element.20.refs_1_.own_ref), channel_id=1, source_target_pairs={{0,1},{1,0},{2,3},{3,2},{4,5},{5,4},{6,7},{7,6},{8,9},{9,8},{10,11... | collective-permute-start | bytes 786440 | tf_op jit(solution)/shard_map/ppermute | solution.py:508
  17.5 20.0 %collective-permute-start.2 = (f32[8,16,512]{2,1,0:T(8,128)S(1)}, f32[8,16,512]{2,1,0:T(8,128)S(1)}, u32[]{:S(2)}, u32[]{:S(2)}) collective-permute-start(f32[8,16,512]{2,1,0:T(8,128)S(1)} %get-tuple-element.20.refs_1_.own_ref), channel_id=1, source_target_pairs={{0,192},{64,128},{128,64},{192,0},{1,193},{65,129},{129,65},{193,1... | collective-permute-start | bytes 786440 | tf_op jit(solution)/shard_map/ppermute | solution.py:500
  20.4 17.1 %collective-permute-start.1 = (f32[8,16,512]{2,1,0:T(8,128)S(1)}, f32[8,16,512]{2,1,0:T(8,128)S(1)}, u32[]{:S(2)}, u32[]{:S(2)}) collective-permute-start(f32[8,16,512]{2,1,0:T(8,128)S(1)} %get-tuple-element.20.refs_1_.own_ref), channel_id=1, source_target_pairs={{0,128},{64,192},{128,0},{192,64},{1,129},{65,193},{129,1},{193,65... | collective-permute-start | bytes 786440 | tf_op jit(solution)/shard_map/ppermute | solution.py:500
  21.0 16.5 %collective-permute-start = (f32[8,16,512]{2,1,0:T(8,128)S(1)}, f32[8,16,512]{2,1,0:T(8,128)S(1)}, u32[]{:S(2)}, u32[]{:S(2)}) collective-permute-start(f32[8,16,512]{2,1,0:T(8,128)S(1)} %get-tuple-element.20.refs_1_.own_ref), channel_id=1, source_target_pairs={{0,64},{64,0},{128,192},{192,128},{1,65},{65,1},{129,193},{193,129... | collective-permute-start | bytes 786440 | tf_op jit(solution)/shard_map/ppermute | solution.py:500
  21.8 15.7 %all-to-all-start.1 = ((f32[16,1,128]{2,1,0:T(1,128)}), f32[16,1,128]{2,1,0:T(1,128)S(1)}, u32[]{:S(2)}, u32[]{:S(2)}) async-start(f32[16,1,128]{2,1,0:T(1,128)} %broadcast_in_dim.2), calls=%async_computation.1 | async-start | bytes 16384 | tf_op jit(solution)/shard_map/all_to_all | solution.py:483
  30.6 7.0 %copy-start = (bf16[128,384]{1,0:T(8,128)(2,1)S(1)}, bf16[128,384]{1,0:T(8,128)(2,1)}, u32[]{:S(2)}) copy-start(bf16[128,384]{1,0:T(8,128)(2,1)} %constant.13.clone.refs_5_.fore_ref) | copy-start | bytes 294916
  30.6 7.0 %copy-start.2 = (bf16[32,384]{1,0:T(8,128)(2,1)S(1)}, bf16[32,384]{1,0:T(8,128)(2,1)}, u32[]{:S(2)}) copy-start(bf16[32,384]{1,0:T(8,128)(2,1)} %constant.14.clone.refs_6_.back_ref) | copy-start | bytes 73732
  39.0 14.1 %collective-permute-start.9 = (f32[8,16,512]{2,1,0:T(8,128)S(1)}, f32[8,16,512]{2,1,0:T(8,128)S(1)}, u32[]{:S(2)}, u32[]{:S(2)}) collective-permute-start(f32[8,16,512]{2,1,0:T(8,128)S(1)} %get-tuple-element.27.own_ref), channel_id=1, source_target_pairs={{0,192},{64,128},{128,64},{192,0},{1,193},{65,129},{129,65},{193,1... | collective-permute-start | bytes 786440 | tf_op jit(solution)/shard_map/ppermute | solution.py:500
  41.7 11.4 %collective-permute-start.8 = (f32[8,16,512]{2,1,0:T(8,128)S(1)}, f32[8,16,512]{2,1,0:T(8,128)S(1)}, u32[]{:S(2)}, u32[]{:S(2)}) collective-permute-start(f32[8,16,512]{2,1,0:T(8,128)S(1)} %get-tuple-element.27.own_ref), channel_id=1, source_target_pairs={{0,128},{64,192},{128,0},{192,64},{1,129},{65,193},{129,1},{193,65... | collective-permute-start | bytes 786440 | tf_op jit(solution)/shard_map/ppermute | solution.py:500
  42.2 11.2 %collective-permute-start.7 = (f32[8,16,512]{2,1,0:T(8,128)S(1)}, f32[8,16,512]{2,1,0:T(8,128)S(1)}, u32[]{:S(2)}, u32[]{:S(2)}) collective-permute-start(f32[8,16,512]{2,1,0:T(8,128)S(1)} %get-tuple-element.27.own_ref), channel_id=1, source_target_pairs={{0,64},{64,0},{128,192},{192,128},{1,65},{65,1},{129,193},{193,129... | collective-permute-start | bytes 786440 | tf_op jit(solution)/shard_map/ppermute | solution.py:500
  42.3 12.0 %collective-permute-start.6 = (f32[8,16,512]{2,1,0:T(8,128)S(1)}, f32[8,16,512]{2,1,0:T(8,128)S(1)}, u32[]{:S(2)}, u32[]{:S(2)}) collective-permute-start(f32[8,16,512]{2,1,0:T(8,128)S(1)} %get-tuple-element.27.own_ref), channel_id=1, source_target_pairs={{1,2},{2,1},{3,4},{4,3},{5,6},{6,5},{7,8},{8,7},{9,10},{10,9},{11,... | collective-permute-start | bytes 786440 | tf_op jit(solution)/shard_map/ppermute | solution.py:508
  45.9 8.5 %collective-permute-start.5 = (f32[8,16,512]{2,1,0:T(8,128)S(1)}, f32[8,16,512]{2,1,0:T(8,128)S(1)}, u32[]{:S(2)}, u32[]{:S(2)}) collective-permute-start(f32[8,16,512]{2,1,0:T(8,128)S(1)} %get-tuple-element.27.own_ref), channel_id=1, source_target_pairs={{0,1},{1,0},{2,3},{3,2},{4,5},{5,4},{6,7},{7,6},{8,9},{9,8},{10,11... | collective-permute-start | bytes 786440 | tf_op jit(solution)/shard_map/ppermute | solution.py:508
  46.1 8.2 %copy-start.1 = (bf16[256,256]{1,0:T(8,128)(2,1)S(1)}, bf16[256,256]{1,0:T(8,128)(2,1)}, u32[]{:S(2)}) copy-start(bf16[256,256]{1,0:T(8,128)(2,1)} %constant.16.clone.part_ref) | copy-start | bytes 393220

commit v3 on v2

--- a/solution.py
+++ b/solution.py
@@ -19,7 +19,8 @@
 KEEP = 1.0 / (1.0 + SIGMA)
 TAKE = SIGMA / (1.0 + SIGMA)
 AXES = ("frame", "cuts")
-STEP = 8
+GROUPS = (4, 6, 6)
+NORMAL_STEP = 4
 VMEM_BYTES = 24 * 1024 * 1024
 BF16 = jnp.bfloat16
 F32 = jnp.float32
@@ -131,16 +132,17 @@
 
 def initial_kernel(
     measured_hbm, maps_hbm, sampling_hbm, tables_hbm, part_hbm,
-    image_ref, image_x_ref, energy_ref, parted_ref, tables_ref, sampling_ref,
-    data_ref, maps_ref, part_ref, data_sem, sems,
+    image_ref, image_x_ref, energy_hbm, parted_ref, tables_ref, sampling_ref,
+    data_ref, maps_ref, part_ref, energy_ref, data_sem, sems,
 ):
     frames_here, coils, readout, doubled = data_ref.shape
     half, quarter = doubled // 2, doubled // 4
     rows = coils * readout
-    groups = frames_here // STEP
+    ends = [sum(GROUPS[:i]) for i in range(len(GROUPS) + 1)]
+    groups = len(GROUPS)
 
     def load(group):
-        frames = pl.ds(group * STEP, STEP)
+        frames = pl.ds(ends[group], GROUPS[group])
         return pltpu.make_async_copy(
             measured_hbm.at[frames, 0], data_ref.at[frames], data_sem.at[group]
         )
@@ -151,25 +153,32 @@
         pltpu.make_async_copy(sampling_hbm, sampling_ref, sems.at[2]),
         pltpu.make_async_copy(tables_hbm, tables_ref, sems.at[3]),
     ]
-    for copy in small:
-        copy.start()
-    for group in range(groups):
+    small[2].start()
+    small[3].start()
+    load(0).start()
+    small[0].start()
+    small[1].start()
+    for group in range(1, groups):
         load(group).start()
-    small[0].wait()
-    small[1].wait()
-    maps = maps_ref[...].reshape(rows, doubled)
-    re = moved(maps[:, :half], part_ref[...])
-    im = moved(maps[:, half:], part_ref[...])
-    parted_ref[...] = cat(
-        re[:, :quarter], im[:, :quarter], re[:, quarter:], im[:, quarter:]
-    ).reshape(coils, readout, doubled)
+
+    def part_maps():
+        small[0].wait()
+        small[1].wait()
+        maps = maps_ref[...].reshape(rows, doubled)
+        re = moved(maps[:, :half], part_ref[...])
+        im = moved(maps[:, half:], part_ref[...])
+        parted_ref[...] = cat(
+            re[:, :quarter], im[:, :quarter], re[:, quarter:], im[:, quarter:]
+        ).reshape(coils, readout, doubled)
+
     small[2].wait()
     small[3].wait()
     energy = jnp.zeros((readout, quarter), F32)
     for group in range(groups):
         load(group).wait()
         evens, odds = [], []
-        for frame in range(group * STEP, (group + 1) * STEP):
+        count = GROUPS[group]
+        for frame in range(ends[group], ends[group + 1]):
             data = data_ref[frame].reshape(rows, doubled)
             weight = sampling_ref[frame : frame + 1, :].astype(F32)
             low, high = weight[:, :quarter], weight[:, quarter:]
@@ -180,29 +189,35 @@
             odds.append(cat(re_low - re_high, im_low - im_high))
         evens = product(jnp.concatenate(evens, 0), tables_ref, 0)
         odds = product(jnp.concatenate(odds, 0), tables_ref, 2)
-        evens = evens.reshape(STEP, coils, readout, half)
-        odds = odds.reshape(STEP, coils, readout, half)
-        for index in range(STEP):
+        evens = evens.reshape(count, coils, readout, half)
+        odds = odds.reshape(count, coils, readout, half)
+        if group == 0:
+            part_maps()
+        for index in range(count):
             image = cat(
                 combine_coils(evens[index], parted_ref[:, :, :half]),
                 combine_coils(odds[index], parted_ref[:, :, half:]),
             )
-            image_ref[group * STEP + index] = image
+            image_ref[ends[group] + index] = image
             energy = energy + sum(piece * piece for piece in quarters(image))
     energy_ref[...] = jnp.broadcast_to(jnp.sum(energy), energy_ref.shape)
+    send = pltpu.make_async_copy(energy_ref, energy_hbm, sems.at[4])
+    send.start()
     image_x_ref[...] = jnp.swapaxes(image_ref[...], 0, 1)
-
-
-def normal_kernel(image_ref, maps_ref, sampling_ref, tables_ref, out_ref):
-    frames_here = image_ref.shape[0]
+    send.wait()
+
+
+def normal_kernel(begin, image_ref, maps_ref, sampling_ref, tables_ref, *rest):
+    out_ref = rest[-1]
+    frames_here = out_ref.shape[0]
     coils, readout, doubled = maps_ref.shape
     half, quarter = doubled // 2, doubled // 4
     rows = coils * readout
 
     def lines(group, offset, table):
         pieces = []
-        for index in range(STEP):
-            frame = group * STEP + index
+        for index in range(NORMAL_STEP):
+            frame = begin + group * NORMAL_STEP + index
             re = image_ref[frame, :, offset : offset + quarter][None]
             im = image_ref[frame, :, offset + quarter : offset + half][None]
             map_re = maps_ref[:, :, offset : offset + quarter]
@@ -212,32 +227,38 @@
             )
         return turned_product(jnp.concatenate(pieces, 0), tables_ref, table)
 
-    def step(group, carry):
+    def forth(group):
         from_even = lines(group, 0, 0)
         from_odd = lines(group, half, 2)
         low = from_even + from_odd
         high = from_even - from_odd
         evens, odds = [], []
-        for index in range(STEP):
-            weight = sampling_ref[pl.ds(group * STEP + index, 1), :].astype(F32)
+        for index in range(NORMAL_STEP):
+            frame = begin + group * NORMAL_STEP + index
+            weight = sampling_ref[frame : frame + 1, :].astype(F32)
             weight_low = cat(weight[:, :quarter], weight[:, :quarter])
             weight_high = cat(weight[:, quarter:], weight[:, quarter:])
             kept_low = low[index * rows : (index + 1) * rows] * weight_low
             kept_high = high[index * rows : (index + 1) * rows] * weight_high
             evens.append(kept_low + kept_high)
             odds.append(kept_low - kept_high)
-        evens = product(jnp.concatenate(evens, 0), tables_ref, 0)
-        odds = product(jnp.concatenate(odds, 0), tables_ref, 2)
-        evens = evens.reshape(STEP, coils, readout, half)
-        odds = odds.reshape(STEP, coils, readout, half)
-        for index in range(STEP):
-            out_ref[group * STEP + index] = cat(
+        return jnp.concatenate(evens, 0), jnp.concatenate(odds, 0)
+
+    def back(group, evens, odds):
+        evens = product(evens, tables_ref, 0).reshape(NORMAL_STEP, coils, readout, half)
+        odds = product(odds, tables_ref, 2).reshape(NORMAL_STEP, coils, readout, half)
+        for index in range(NORMAL_STEP):
+            out_ref[group * NORMAL_STEP + index] = cat(
                 combine_coils(evens[index], maps_ref[:, :, :half]),
                 combine_coils(odds[index], maps_ref[:, :, half:]),
             )
-        return carry
-
-    lax.fori_loop(0, frames_here // STEP, step, 0)
+
+    groups = frames_here // NORMAL_STEP
+    held = forth(0)
+    for group in range(groups):
+        later = forth(group + 1) if group + 1 < groups else None
+        back(group, *held)
+        held = later
 
 
 def frequencies(blocks, x, table):
@@ -333,42 +354,45 @@
     return own_ref, jnp.where(even, one, three), two_ref, jnp.where(even, three, one)
 
 
-def time_fields(blocks, level, old, fore_ref, back_ref, field_ref):
-    places = range(field_ref.shape[0])
+def time_duals(duals, level):
     limit = LAM_TIME * cat(level, level)
-    duals = [SIGMA * frequencies(blocks, x, fore_ref[...]) for x in places]
-    if old is not None:
-        duals = [old[x] + dual for x, dual in zip(places, duals)]
-    duals = [clip_time(dual, limit) for dual in duals]
-    for x, dual in zip(places, duals):
-        field_ref[x] = frames_of(dual, back_ref[...])
-    return duals
-
-
-def first_time_kernel(
-    cells, energy_ref, own_ref, one_ref, two_ref, three_ref, fore_ref, back_ref,
-    dual_ref, field_ref, level_ref,
-):
-    rms_level = level(energy_ref, cells)
-    level_ref[...] = jnp.broadcast_to(rms_level, level_ref.shape)
+    return [clip_time(dual, limit) for dual in duals]
+
+
+def summed_kernel(energy_ref, out_ref):
+    out_ref[...] = jnp.broadcast_to(
+        jnp.sum(energy_ref[...], axis=0, keepdims=True), out_ref.shape
+    )
+
+
+def frequency_kernel(own_ref, one_ref, two_ref, three_ref, fore_ref, out_ref):
     blocks = in_turn(own_ref, one_ref, two_ref, three_ref)
-    duals = time_fields(blocks, rms_level, None, fore_ref, back_ref, field_ref)
-    for x, dual in enumerate(duals):
-        dual_ref[x] = dual
+    for x in range(own_ref.shape[0]):
+        out_ref[x] = SIGMA * frequencies(blocks, x, fore_ref[...])
 
 
 def last_time_kernel(
     level_ref, own_ref, one_ref, two_ref, three_ref, dual_ref, fore_ref, back_ref, field_ref
 ):
     blocks = in_turn(own_ref, one_ref, two_ref, three_ref)
-    time_fields(blocks, level_ref[0:1, :], dual_ref, fore_ref, back_ref, field_ref)
-
-
-def first_space_kernel(
-    level_ref, own_ref, near_ref, far_ref, normal_ref, field_ref,
-    base_ref, bar_x_ref, bar_ref, space_ref, space_below_ref,
+    places = range(field_ref.shape[0])
+    duals = [dual_ref[x] + SIGMA * frequencies(blocks, x, fore_ref[...]) for x in places]
+    duals = time_duals(duals, level_ref[0:1, :])
+    for x, dual in enumerate(duals):
+        field_ref[x] = frames_of(dual, back_ref[...])
+
+
+def first_kernel(
+    cells, energy_ref, own_ref, near_ref, far_ref, normal_ref, frequency_ref, back_ref,
+    base_ref, bar_x_ref, bar_ref, dual_ref, level_ref, space_ref, space_below_ref,
 ):
-    limit_space = LAM_SPACE * level_ref[0:1, :]
+    rms_level = level(energy_ref, cells)
+    level_ref[...] = jnp.broadcast_to(rms_level, level_ref.shape)
+    time = time_duals([frequency_ref[x] for x in range(frequency_ref.shape[0])], rms_level)
+    for x, dual in enumerate(time):
+        dual_ref[x] = dual
+    fields = [frames_of(dual, back_ref[...]) for dual in time]
+    limit_space = LAM_SPACE * rms_level
     has_below = (lax.axis_index("cuts") > 0).astype(F32)
     above, below = around(near_ref, far_ref)
     normal = jnp.swapaxes(normal_ref[...], 0, 1)
@@ -384,7 +408,7 @@
             space_below_ref[index, x] = duals_below[index]
         initial = own_ref[x]
         data_part = TAKE * (normal[x] - initial)
-        updated = initial - TAU * (data_part + field_ref[x] + total)
+        updated = initial - TAU * (data_part + fields[x] + total)
         base_ref[x] = updated - TAU * (KEEP * data_part - TAKE * initial)
         bar = 2.0 * updated - initial
         bar_x_ref[x] = bar
@@ -457,7 +481,7 @@
     initial, initial_x, energy, maps, tables, sampling = pl.pallas_call(
         initial_kernel,
         in_specs=[hbm] * 5,
-        out_specs=[vmem] * 6,
+        out_specs=[vmem] * 2 + [pl.BlockSpec(memory_space=pl.ANY)] + [vmem] * 3,
         out_shape=[
             struct(*turned), struct(*plane), struct(len(inner[0]), 128),
             pltpu.VMEM((coils, readout, doubled), F32),
@@ -468,8 +492,9 @@
             pltpu.VMEM((frames_here, coils, readout, doubled), F32),
             pltpu.VMEM((coils, readout, doubled), F32),
             pltpu.VMEM(part.shape, BF16),
-            pltpu.SemaphoreType.DMA((frames_here // STEP,)),
-            pltpu.SemaphoreType.DMA((4,)),
+            pltpu.VMEM((len(inner[0]), 128), F32),
+            pltpu.SemaphoreType.DMA((len(GROUPS),)),
+            pltpu.SemaphoreType.DMA((5,)),
         ],
         compiler_params=params(),
         cost_estimate=cost(6 * rows * doubled * positions, measured.size * 4),
@@ -478,29 +503,27 @@
         for array in (measured, coil_maps, sampling, tables, part)
     ))
 
-    energies = lax.all_to_all(energy, AXES, 0, 0, tiled=True, axis_index_groups=inner)
-    energies = jnp.broadcast_to(jnp.sum(energies, axis=0, keepdims=True), (len(outer[0]), 128))
-    energies = lax.all_to_all(energies, AXES, 0, 0, tiled=True, axis_index_groups=outer)
-
-    def normal(image):
+    def normal(image, begin=0, count=frames_here, after=()):
+        def kernel(*refs):
+            normal_kernel(begin, *refs)
+
         return pl.pallas_call(
-            normal_kernel,
-            in_specs=[vmem] * 4,
+            kernel,
+            in_specs=[vmem] * (4 + len(after)),
             out_specs=vmem,
-            out_shape=struct(*turned),
+            out_shape=struct(count, readout, doubled),
             compiler_params=params(),
-            cost_estimate=cost(12 * rows * doubled * positions, image.size * 8),
+            cost_estimate=cost(12 * rows * doubled * positions * count // frames_here, 1000000),
         )(image, *(
             pltpu.with_memory_space_constraint(array, pltpu.VMEM)
             for array in (maps, sampling, tables)
-        ))
+        ), *after)
+
+    def swapped(image, by):
+        return lax.ppermute(image, "frame", [(index, index ^ by) for index in range(blocks)])
 
     def gathered(image):
-        others = [
-            lax.ppermute(image, "frame", [(index, index ^ by) for index in range(blocks)])
-            for by in range(1, blocks)
-        ]
-        return [image] + others
+        return [image] + [swapped(image, by) for by in range(1, blocks)]
 
     def neighbours(image):
         count = lax.axis_size("cuts")
@@ -518,27 +541,29 @@
             cost_estimate=cost(flops, sum(arg.size * 4 for arg in args)),
         )(*args)
 
+    energies = lax.all_to_all(energy, AXES, 0, 0, tiled=True, axis_index_groups=inner)
+    energies = call(summed_kernel, [energies], pltpu.VMEM((len(outer[0]), 128), F32), 1000)
+    energies = lax.all_to_all(energies, AXES, 0, 0, tiled=True, axis_index_groups=outer)
+
     time_flops = 7 * (2 * frames_all) ** 2 * readout * positions
     dual_shape = struct(readout, 2 * frames_all, positions)
     duals_shape = struct(3, *plane)
 
-    def first_time(*refs):
-        first_time_kernel(cells, *refs)
+    def first(*refs):
+        first_kernel(cells, *refs)
 
     all_blocks = gathered(initial_x)
     pair_near, pair_far = neighbours(initial_x)
     normal_initial = normal(initial)
-    time_dual, field, rms_level = call(
-        first_time,
-        [energies] + all_blocks + [time_fore, time_back],
-        [dual_shape, struct(*plane), struct(8, 128)],
-        time_flops,
-    )
-    base, bar_x, bar, space_dual, space_below = call(
-        first_space_kernel,
-        [rms_level, initial_x, pair_near, pair_far, normal_initial, field],
-        [struct(*plane), struct(*plane), struct(*turned), duals_shape, duals_shape],
-        1000000,
+    frequency = call(frequency_kernel, all_blocks + [time_fore], dual_shape, time_flops // 2)
+    base, bar_x, bar, time_dual, rms_level, space_dual, space_below = call(
+        first,
+        [energies, initial_x, pair_near, pair_far, normal_initial, frequency, time_back],
+        [
+            struct(*plane), struct(*plane), struct(*turned), dual_shape, struct(8, 128),
+            duals_shape, duals_shape,
+        ],
+        time_flops // 2,
     )
     all_blocks = gathered(bar_x)
     pair_near, pair_far = neighbours(bar_x)

time: 56.5 us -> 56.1 us (level)
    unnamed x6 -> x10, local copies, waits for them, and re-layouts: 0.02 us -> 0.98 us
    broadcast_in_dim x1 -> x0, local copies, waits for them, and re-layouts: 0.61 us -> none  [shards(): jnp.broadcast_to(jnp.sum(energies, axis=0, keepdims=True), (len(outer[0])...]
    pallas_call x4 -> x5, Pallas kernels: 3.77 us -> 4.37 us  [call(): pl.pallas_call(kernel, in_specs=[vmem] * len(args), out_specs=jax.tree.ma...]
  transfers between devices with their start and end apart: 12 -> 12, of which waited for: 3 -> 3; matrix products, arithmetic and copies ran while one was open for 1% -> 0% of each run, Pallas kernels for 21% -> 20%
where the time goes in v3:
time: 56.1 us; the launch traced here: 55.7 us
  starting transfers between devices  31.5 us (56%)
  Pallas kernels  19.1 us (34%)
  waiting for transfers between devices  3.94 us (7%)
  local copies, waits for them, and re-layouts  0.98 us (2%)
    pallas_call x2, Pallas kernels, normal(): pl.pallas_call(kernel, in_specs=[vmem] * (4 + len(after)), out_specs=vmem...  9.39 us
    ppermute x4, starting transfers between devices, neighbours(): return [lax.ppermute(image, 'cuts', pair) for pair in pairs]  8.72 us
    all_to_all x1, starting transfers between devices, shards(): lax.all_to_all(energies, AXES, 0, 0, tiled=True, axis_index_groups=outer)  8.24 us
    all_to_all x1, starting transfers between devices, shards(): lax.all_to_all(energy, AXES, 0, 0, tiled=True, axis_index_groups=inner)  7.62 us
    ppermute x6, starting transfers between devices, swapped(): lax.ppermute(image, 'frame', [(index, index ^ by) for index in range(bloc...  6.89 us
    pallas_call x1, Pallas kernels, shards(): pl.pallas_call(initial_kernel, in_specs=[hbm] * 5, out_specs=[vmem] * 2 +...  5.37 us
    pallas_call x5, Pallas kernels, call(): pl.pallas_call(kernel, in_specs=[vmem] * len(args), out_specs=jax.tree.ma...  4.37 us
    ppermute x6, waiting for transfers between devices, swapped(): lax.ppermute(image, 'frame', [(index, index ^ by) for index in range(bloc...  2.24 us
  transfers between devices with their start and end apart: 12, of which 3 were waited for; matrix products, arithmetic and copies ran while one was open for 0% of the time, Pallas kernels for 20%

profile of v3, /device:TPU:1, one launch (start us, length us, event | category | flops | bytes accessed | tf_op | source)
XLA Modules:
  0.0 55.7 jit_solution(6835631313062837626)
XLA Ops:
  0.0 5.4 %shard_map.82 = (f32[16,8,512]{2,1,0:T(8,128)S(1)}, f32[8,16,512]{2,1,0:T(8,128)S(1)}, f32[16,128]{1,0:T(8,128)}, f32[20,8,512]{2,1,0:T(8,128)S(1)}, bf16[4,256,...) custom-call(f32[16,1,20,8,512]{4,3,2,1,0:T(8,128)} %measured_hbm.1, f32[1,20,8,512]{3,2,1,0:T(8,128)} %maps_hbm.1, ...), custom_call_target="tpu_custom_call" | custom-call | flops 2013265920 | bytes 5242880 | tf_op jit(solution)/shard_map/pallas_call | solution.py:481
  5.4 7.6 %all-to-all-start = ((f32[16,1,128]{2,1,0:T(1,128)}), f32[16,1,128]{2,1,0:T(1,128)S(1)}, u32[]{:S(2)}, u32[]{:S(2)}) async-start(f32[16,1,128]{2,1,0:T(1,128)} %bitcast.1), calls=%async_computation | async-start | bytes 16384 | tf_op jit(solution)/shard_map/all_to_all | solution.py:544
  13.0 2.6 %collective-permute-start.4 = (f32[8,16,512]{2,1,0:T(8,128)S(1)}, f32[8,16,512]{2,1,0:T(8,128)S(1)}, u32[]{:S(2)}, u32[]{:S(2)}) collective-permute-start(f32[8,16,512]{2,1,0:T(8,128)S(1)} %get-tuple-element.19.own_ref.refs_1_), channel_id=1, source_target_pairs={{0,192},{64,128},{128,64},{192,0},{1,193},{65,129},{129,65},{193,1... | collective-permute-start | bytes 786440 | tf_op jit(solution)/shard_map/ppermute | solution.py:523
  15.6 0.6 %collective-permute-start.3 = (f32[8,16,512]{2,1,0:T(8,128)S(1)}, f32[8,16,512]{2,1,0:T(8,128)S(1)}, u32[]{:S(2)}, u32[]{:S(2)}) collective-permute-start(f32[8,16,512]{2,1,0:T(8,128)S(1)} %get-tuple-element.19.own_ref.refs_1_), channel_id=1, source_target_pairs={{0,128},{64,192},{128,0},{192,64},{1,129},{65,193},{129,1},{193,65... | collective-permute-start | bytes 786440 | tf_op jit(solution)/shard_map/ppermute | solution.py:523
  16.2 0.2 collective-permute-start.2
  16.4 5.2 %collective-permute-start.1 = (f32[8,16,512]{2,1,0:T(8,128)S(1)}, f32[8,16,512]{2,1,0:T(8,128)S(1)}, u32[]{:S(2)}, u32[]{:S(2)}) collective-permute-start(f32[8,16,512]{2,1,0:T(8,128)S(1)} %get-tuple-element.19.own_ref.refs_1_), channel_id=1, source_target_pairs={{1,2},{2,1},{3,4},{4,3},{5,6},{6,5},{7,8},{8,7},{9,10},{10,9},{11,... | collective-permute-start | bytes 786440 | tf_op jit(solution)/shard_map/ppermute | solution.py:531
  21.6 0.1 collective-permute-start
  21.7 0.0 all-to-all-done
  21.7 0.6 %shard_map.83 = f32[16,128]{1,0:T(8,128)} custom-call(f32[16,128]{1,0:T(8,128)S(1)} %bitcast.9), custom_call_target="tpu_custom_call" | custom-call | flops 1000 | bytes 8192 | tf_op jit(solution)/shard_map/pallas_call | solution.py:535
  22.3 8.2 %all-to-all-start.1 = ((f32[16,1,128]{2,1,0:T(1,128)}), f32[16,1,128]{2,1,0:T(1,128)S(1)}, u32[]{:S(2)}, u32[]{:S(2)}) async-start(f32[16,1,128]{2,1,0:T(1,128)} %bitcast.4), calls=%async_computation.1 | async-start | bytes 16384 | tf_op jit(solution)/shard_map/all_to_all | solution.py:546
  30.5 0.0 copy-start.2
  30.5 4.7 %shard_map.84.refs_4_ = f32[16,8,512]{2,1,0:T(8,128)S(1)} custom-call(f32[16,8,512]{2,1,0:T(8,128)S(1)} %get-tuple-element.20.refs_0_, f32[20,8,512]{2,1,0:T(8,128)S(1)} %get-tuple-element.21.refs_1_, s32[16,256]{1,0:T(8,128)S(1)} %get-tuple-element.22.refs_2_, bf16[4,256,256]{2,1,0:T(8,128)(2,1)S(1)} %get-tuple-element.23.refs_3_), custom_call_target="tpu_custom_call" | custom-call | flops 4026531840 | bytes 1000000 | tf_op jit(solution)/shard_map/pallas_call | solution.py:510
  35.3 0.0 collective-permute-done.4.three_ref
  35.3 0.0 collective-permute-done.3.two_ref
  35.3 0.5 shard_map.85.refs_5_
  35.8 1.7 %all-to-all-done.1 = f32[16,1,128]{2,1,0:T(1,128)S(1)} async-done(((f32[16,1,128]{2,1,0:T(1,128)}), f32[16,1,128]{2,1,0:T(1,128)S(1)}, u32[]{:S(2)}, u32[]{:S(2)}) %all-to-all-start.1) | async-done | bytes 8224 | tf_op jit(solution)/shard_map/all_to_all | solution.py:546
  37.5 0.0 collective-permute-done.1.refs_3_
  37.5 0.0 collective-permute-done.refs_2_
  37.5 0.9 %shard_map.86 = (f32[8,16,512]{2,1,0:T(8,128)S(1)}, f32[8,16,512]{2,1,0:T(8,128)S(1)}, f32[16,8,512]{2,1,0:T(8,128)S(1)}, f32[8,128,256]{2,1,0:T(8,128)S(1)}, f3...) custom-call(f32[16,128]{1,0:T(8,128)S(1)} %bitcast.8, ...), custom_call_target="tpu_custom_call" | custom-call | flops 117440512 | bytes 2154496 | tf_op jit(solution)/shard_map/pallas_call | solution.py:535
  38.4 2.7 %collective-permute-start.9 = (f32[8,16,512]{2,1,0:T(8,128)S(1)}, f32[8,16,512]{2,1,0:T(8,128)S(1)}, u32[]{:S(2)}, u32[]{:S(2)}) collective-permute-start(f32[8,16,512]{2,1,0:T(8,128)S(1)} %get-tuple-element.25.own_ref), channel_id=1, source_target_pairs={{0,192},{64,128},{128,64},{192,0},{1,193},{65,129},{129,65},{193,1... | collective-permute-start | bytes 786440 | tf_op jit(solution)/shard_map/ppermute | solution.py:523
  41.1 0.6 %collective-permute-start.8 = (f32[8,16,512]{2,1,0:T(8,128)S(1)}, f32[8,16,512]{2,1,0:T(8,128)S(1)}, u32[]{:S(2)}, u32[]{:S(2)}) collective-permute-start(f32[8,16,512]{2,1,0:T(8,128)S(1)} %get-tuple-element.25.own_ref), channel_id=1, source_target_pairs={{0,128},{64,192},{128,0},{192,64},{1,129},{65,193},{129,1},{193,65... | collective-permute-start | bytes 786440 | tf_op jit(solution)/shard_map/ppermute | solution.py:523
  41.7 0.3 collective-permute-start.7
  42.0 3.3 %collective-permute-start.6 = (f32[8,16,512]{2,1,0:T(8,128)S(1)}, f32[8,16,512]{2,1,0:T(8,128)S(1)}, u32[]{:S(2)}, u32[]{:S(2)}) collective-permute-start(f32[8,16,512]{2,1,0:T(8,128)S(1)} %get-tuple-element.25.own_ref), channel_id=1, source_target_pairs={{1,2},{2,1},{3,4},{4,3},{5,6},{6,5},{7,8},{8,7},{9,10},{10,9},{11,... | collective-permute-start | bytes 786440 | tf_op jit(solution)/shard_map/ppermute | solution.py:531
  45.3 0.1 collective-permute-start.5
  45.4 1.0 %copy-done.4 = f32[20,8,512]{2,1,0:T(8,128)S(1)} copy-done((f32[20,8,512]{2,1,0:T(8,128)S(1)}, f32[20,8,512]{2,1,0:T(8,128)}, u32[]{:S(2)}) %copy-start.4) | copy-done | bytes 327704
  46.4 4.7 %shard_map.87.normal_ref = f32[16,8,512]{2,1,0:T(8,128)S(1)} custom-call(f32[16,8,512]{2,1,0:T(8,128)S(1)} %get-tuple-element.26.refs_0_, f32[20,8,512]{2,1,0:T(8,128)S(1)} %copy-done.4, s32[16,256]{1,0:T(8,128)S(1)} %get-tuple-element.22.refs_2_, bf16[4,256,256]{2,1,0:T(8,128)(2,1)S(1)} %get-tuple-element.23.refs_3_), custom_call_target="tpu_custom_call" | custom-call | flops 4026531840 | bytes 1000000 | tf_op jit(solution)/shard_map/pallas_call | solution.py:510
  51.1 1.4 %collective-permute-done.9.three_ref = f32[8,16,512]{2,1,0:T(8,128)S(1)} collective-permute-done((f32[8,16,512]{2,1,0:T(8,128)S(1)}, f32[8,16,512]{2,1,0:T(8,128)S(1)}, u32[]{:S(2)}, u32[]{:S(2)}) %collective-permute-start.9) | collective-permute-done | bytes 262176 | tf_op jit(solution)/shard_map/ppermute | solution.py:523
  52.5 0.0 collective-permute-done.8.two_ref
  52.5 0.8 %collective-permute-done.7.one_ref = f32[8,16,512]{2,1,0:T(8,128)S(1)} collective-permute-done((f32[8,16,512]{2,1,0:T(8,128)S(1)}, f32[8,16,512]{2,1,0:T(8,128)S(1)}, u32[]{:S(2)}, u32[]{:S(2)}) %collective-permute-start.7) | collective-permute-done | bytes 262176 | tf_op jit(solution)/shard_map/ppermute | solution.py:523
  53.3 0.8 %shard_map.88.field_ref = f32[8,16,512]{2,1,0:T(8,128)S(1)} custom-call(f32[8,128]{1,0:T(8,128)S(1)} %get-tuple-element.24.level_ref, f32[8,16,512]{2,1,0:T(8,128)S(1)} %get-tuple-element.25.own_ref, f32[8,16,512]{2,1,0:T(8,128)S(1)} %collective-permute-done.7.one_ref, f32[8,16,512]{2,1,0:T(8,128)S(1)} %collective-permute-done.8.two_ref, ...), custom_call_target="tpu_custom_call" | custom-call | flops 234881024 | bytes 2347008 | tf_op jit(solution)/shard_map/pallas_call | solution.py:535
  54.2 0.0 collective-permute-done.5.near_ref
  54.2 1.5 %shard_map.89 = f32[16,1,8,512]{3,2,1,0:T(8,128)} custom-call(f32[8,128]{1,0:T(8,128)S(1)} %get-tuple-element.24.level_ref, f32[8,16,512]{2,1,0:T(8,128)S(1)} %get-tuple-element.25.own_ref, f32[8,16,512]{2,1,0:T(8,128)S(1)} %collective-permute-done.5.near_ref, f32[8,16,512]{2,1,0:T(8,128)S(1)} %collective-permute-done.6.far_ref, ...), custom_call_target="tpu_custom_call" | custom-call | flops 1000000 | bytes 3411968 | tf_op jit(solution)/shard_map/pallas_call | solution.py:535
  (10 shorter events, 0.0 us)
Async XLA Ops:
  5.4 29.9 %copy-start.3 = (f32[20,8,512]{2,1,0:T(8,128)}, f32[20,8,512]{2,1,0:T(8,128)S(1)}, u32[]{:S(2)}) copy-start(f32[20,8,512]{2,1,0:T(8,128)S(1)} %get-tuple-element.21.refs_1_) | copy-start | bytes 983044
  5.4 16.3 %all-to-all-start = ((f32[16,1,128]{2,1,0:T(1,128)}), f32[16,1,128]{2,1,0:T(1,128)S(1)}, u32[]{:S(2)}, u32[]{:S(2)}) async-start(f32[16,1,128]{2,1,0:T(1,128)} %bitcast.1), calls=%async_computation | async-start | bytes 16384 | tf_op jit(solution)/shard_map/all_to_all | solution.py:544
  13.0 22.3 %collective-permute-start.4 = (f32[8,16,512]{2,1,0:T(8,128)S(1)}, f32[8,16,512]{2,1,0:T(8,128)S(1)}, u32[]{:S(2)}, u32[]{:S(2)}) collective-permute-start(f32[8,16,512]{2,1,0:T(8,128)S(1)} %get-tuple-element.19.own_ref.refs_1_), channel_id=1, source_target_pairs={{0,192},{64,128},{128,64},{192,0},{1,193},{65,129},{129,65},{193,1... | collective-permute-start | bytes 786440 | tf_op jit(solution)/shard_map/ppermute | solution.py:523
  15.6 19.7 %collective-permute-start.3 = (f32[8,16,512]{2,1,0:T(8,128)S(1)}, f32[8,16,512]{2,1,0:T(8,128)S(1)}, u32[]{:S(2)}, u32[]{:S(2)}) collective-permute-start(f32[8,16,512]{2,1,0:T(8,128)S(1)} %get-tuple-element.19.own_ref.refs_1_), channel_id=1, source_target_pairs={{0,128},{64,192},{128,0},{192,64},{1,129},{65,193},{129,1},{193,65... | collective-permute-start | bytes 786440 | tf_op jit(solution)/shard_map/ppermute | solution.py:523
  16.2 19.1 %collective-permute-start.2 = (f32[8,16,512]{2,1,0:T(8,128)S(1)}, f32[8,16,512]{2,1,0:T(8,128)S(1)}, u32[]{:S(2)}, u32[]{:S(2)}) collective-permute-start(f32[8,16,512]{2,1,0:T(8,128)S(1)} %get-tuple-element.19.own_ref.refs_1_), channel_id=1, source_target_pairs={{0,64},{64,0},{128,192},{192,128},{1,65},{65,1},{129,193},{193,129... | collective-permute-start | bytes 786440 | tf_op jit(solution)/shard_map/ppermute | solution.py:523
  16.4 21.1 %collective-permute-start.1 = (f32[8,16,512]{2,1,0:T(8,128)S(1)}, f32[8,16,512]{2,1,0:T(8,128)S(1)}, u32[]{:S(2)}, u32[]{:S(2)}) collective-permute-start(f32[8,16,512]{2,1,0:T(8,128)S(1)} %get-tuple-element.19.own_ref.refs_1_), channel_id=1, source_target_pairs={{1,2},{2,1},{3,4},{4,3},{5,6},{6,5},{7,8},{8,7},{9,10},{10,9},{11,... | collective-permute-start | bytes 786440 | tf_op jit(solution)/shard_map/ppermute | solution.py:531
  21.6 15.9 %collective-permute-start = (f32[8,16,512]{2,1,0:T(8,128)S(1)}, f32[8,16,512]{2,1,0:T(8,128)S(1)}, u32[]{:S(2)}, u32[]{:S(2)}) collective-permute-start(f32[8,16,512]{2,1,0:T(8,128)S(1)} %get-tuple-element.19.own_ref.refs_1_), channel_id=1, source_target_pairs={{0,1},{1,0},{2,3},{3,2},{4,5},{5,4},{6,7},{7,6},{8,9},{9,8},{10,11... | collective-permute-start | bytes 786440 | tf_op jit(solution)/shard_map/ppermute | solution.py:531
  22.3 15.2 %all-to-all-start.1 = ((f32[16,1,128]{2,1,0:T(1,128)}), f32[16,1,128]{2,1,0:T(1,128)S(1)}, u32[]{:S(2)}, u32[]{:S(2)}) async-start(f32[16,1,128]{2,1,0:T(1,128)} %bitcast.4), calls=%async_computation.1 | async-start | bytes 16384 | tf_op jit(solution)/shard_map/all_to_all | solution.py:546
  30.5 4.8 %copy-start = (bf16[128,384]{1,0:T(8,128)(2,1)S(1)}, bf16[128,384]{1,0:T(8,128)(2,1)}, u32[]{:S(2)}) copy-start(bf16[128,384]{1,0:T(8,128)(2,1)} %constant.11.clone.fore_ref) | copy-start | bytes 294916
  30.5 6.9 %copy-start.2 = (bf16[32,384]{1,0:T(8,128)(2,1)S(1)}, bf16[32,384]{1,0:T(8,128)(2,1)}, u32[]{:S(2)}) copy-start(bf16[32,384]{1,0:T(8,128)(2,1)} %constant.12.clone.refs_6_.back_ref) | copy-start | bytes 73732
  38.4 14.1 %collective-permute-start.9 = (f32[8,16,512]{2,1,0:T(8,128)S(1)}, f32[8,16,512]{2,1,0:T(8,128)S(1)}, u32[]{:S(2)}, u32[]{:S(2)}) collective-permute-start(f32[8,16,512]{2,1,0:T(8,128)S(1)} %get-tuple-element.25.own_ref), channel_id=1, source_target_pairs={{0,192},{64,128},{128,64},{192,0},{1,193},{65,129},{129,65},{193,1... | collective-permute-start | bytes 786440 | tf_op jit(solution)/shard_map/ppermute | solution.py:523
  41.1 11.4 %collective-permute-start.8 = (f32[8,16,512]{2,1,0:T(8,128)S(1)}, f32[8,16,512]{2,1,0:T(8,128)S(1)}, u32[]{:S(2)}, u32[]{:S(2)}) collective-permute-start(f32[8,16,512]{2,1,0:T(8,128)S(1)} %get-tuple-element.25.own_ref), channel_id=1, source_target_pairs={{0,128},{64,192},{128,0},{192,64},{1,129},{65,193},{129,1},{193,65... | collective-permute-start | bytes 786440 | tf_op jit(solution)/shard_map/ppermute | solution.py:523
  41.7 11.6 %collective-permute-start.7 = (f32[8,16,512]{2,1,0:T(8,128)S(1)}, f32[8,16,512]{2,1,0:T(8,128)S(1)}, u32[]{:S(2)}, u32[]{:S(2)}) collective-permute-start(f32[8,16,512]{2,1,0:T(8,128)S(1)} %get-tuple-element.25.own_ref), channel_id=1, source_target_pairs={{0,64},{64,0},{128,192},{192,128},{1,65},{65,1},{129,193},{193,129... | collective-permute-start | bytes 786440 | tf_op jit(solution)/shard_map/ppermute | solution.py:523
  42.0 12.2 %collective-permute-start.6 = (f32[8,16,512]{2,1,0:T(8,128)S(1)}, f32[8,16,512]{2,1,0:T(8,128)S(1)}, u32[]{:S(2)}, u32[]{:S(2)}) collective-permute-start(f32[8,16,512]{2,1,0:T(8,128)S(1)} %get-tuple-element.25.own_ref), channel_id=1, source_target_pairs={{1,2},{2,1},{3,4},{4,3},{5,6},{6,5},{7,8},{8,7},{9,10},{10,9},{11,... | collective-permute-start | bytes 786440 | tf_op jit(solution)/shard_map/ppermute | solution.py:531
  45.3 8.8 %collective-permute-start.5 = (f32[8,16,512]{2,1,0:T(8,128)S(1)}, f32[8,16,512]{2,1,0:T(8,128)S(1)}, u32[]{:S(2)}, u32[]{:S(2)}) collective-permute-start(f32[8,16,512]{2,1,0:T(8,128)S(1)} %get-tuple-element.25.own_ref), channel_id=1, source_target_pairs={{0,1},{1,0},{2,3},{3,2},{4,5},{5,4},{6,7},{7,6},{8,9},{9,8},{10,11... | collective-permute-start | bytes 786440 | tf_op jit(solution)/shard_map/ppermute | solution.py:531
  45.4 1.0 %copy-start.4 = (f32[20,8,512]{2,1,0:T(8,128)S(1)}, f32[20,8,512]{2,1,0:T(8,128)}, u32[]{:S(2)}) copy-start(f32[20,8,512]{2,1,0:T(8,128)} %copy-done.3) | copy-start | bytes 983044
  46.4 7.8 %copy-start.1 = (bf16[256,256]{1,0:T(8,128)(2,1)S(1)}, bf16[256,256]{1,0:T(8,128)(2,1)}, u32[]{:S(2)}) copy-start(bf16[256,256]{1,0:T(8,128)(2,1)} %constant.14.clone.part_ref) | copy-start | bytes 393220

commit v4 on v3

--- a/solution.py
+++ b/solution.py
@@ -54,12 +54,12 @@
     angles = 2.0 * math.pi / frames_all * (index[:, None] * index[None, :] % frames_all)
     fore = block_table(np.cos(angles), np.sin(angles)) / math.sqrt(frames_all)
     rows = np.concatenate([np.arange(frames_here), frames_all + np.arange(frames_here)])
-    back = fore.T[rows]
     out = []
-    for table in (fore, back):
+    last = frames_all // frames_here - 1
+    for table in (fore, fore.T[rows], fore[:, rows + frames_here], fore[:, rows + last * frames_here]):
         high, low = split_table(table)
         out.append(np.concatenate([high, high, low], 1))
-    return out
+    return out[0], out[1], np.stack(out[2:], 0)
 
 
 def parting_table(positions):
@@ -261,11 +261,16 @@
         held = later
 
 
+def lines_of(block):
+    re_even, im_even, re_odd, im_odd = quarters(block)
+    return cat(re_even, re_odd), cat(im_even, im_odd)
+
+
 def frequencies(blocks, x, table):
-    parts = [quarters(block[x]) for block in blocks]
-    re = jnp.concatenate([cat(part[0], part[2]) for part in parts], 0)
-    im = jnp.concatenate([cat(part[1], part[3]) for part in parts], 0)
-    return left_product(table, jnp.concatenate([re, im], 0))
+    parts = [lines_of(block[x]) for block in blocks]
+    return left_product(
+        table, jnp.concatenate([part[0] for part in parts] + [part[1] for part in parts], 0)
+    )
 
 
 def level(energy_ref, cells):
@@ -369,17 +374,6 @@
     blocks = in_turn(own_ref, one_ref, two_ref, three_ref)
     for x in range(own_ref.shape[0]):
         out_ref[x] = SIGMA * frequencies(blocks, x, fore_ref[...])
-
-
-def last_time_kernel(
-    level_ref, own_ref, one_ref, two_ref, three_ref, dual_ref, fore_ref, back_ref, field_ref
-):
-    blocks = in_turn(own_ref, one_ref, two_ref, three_ref)
-    places = range(field_ref.shape[0])
-    duals = [dual_ref[x] + SIGMA * frequencies(blocks, x, fore_ref[...]) for x in places]
-    duals = time_duals(duals, level_ref[0:1, :])
-    for x, dual in enumerate(duals):
-        field_ref[x] = frames_of(dual, back_ref[...])
 
 
 def first_kernel(
@@ -416,30 +410,45 @@
     bar_ref[...] = jnp.swapaxes(jnp.stack(bars, 0), 0, 1)
 
 
-def last_space_kernel(
-    level_ref, own_ref, near_ref, far_ref, normal_ref, field_ref, base_ref,
-    space_ref, space_below_ref, part_ref,
-    out_ref,
+def middle_kernel(
+    level_ref, near_ref, far_ref, own_ref, two_ref, three_ref, normal_ref, base_ref, dual_ref,
+    space_ref, space_below_ref, fore_ref,
+    partial_ref, out_ref,
 ):
+    absent = jnp.zeros(own_ref.shape, F32)
+    blocks = in_turn(own_ref, absent, two_ref, three_ref)
+    for x in range(own_ref.shape[0]):
+        partial_ref[x] = dual_ref[x] + SIGMA * frequencies(blocks, x, fore_ref[...])
     limit_space = LAM_SPACE * level_ref[0:1, :]
     has_below = (lax.axis_index("cuts") > 0).astype(F32)
     above, below = around(near_ref, far_ref)
     normal = jnp.swapaxes(normal_ref[...], 0, 1)
     rows_before = jnp.zeros(own_ref.shape[1:], F32)
-    images = []
     for x in range(own_ref.shape[0]):
         total, duals, _ = space_part(
             own_ref, above, below, x, rows_before, has_below,
             space_ref, space_below_ref, limit_space,
         )
         rows_before = duals[1]
-        images.append(base_ref[x] - TAU * (TAKE * normal[x] + field_ref[x] + total))
+        out_ref[x] = base_ref[x] - TAU * (TAKE * normal[x] + total)
+
+
+def last_kernel(
+    level_ref, one_ref, partial_ref, base_ref, across_ref, back_ref, part_ref, out_ref
+):
+    places = range(one_ref.shape[0])
+    across = across_ref[lax.axis_index("frame") % 2]
+    duals = [
+        partial_ref[x] + SIGMA * frequencies((one_ref,), x, across) for x in places
+    ]
+    duals = time_duals(duals, level_ref[0:1, :])
+    images = [base_ref[x] - TAU * frames_of(duals[x], back_ref[...]) for x in places]
     image = jnp.concatenate(images, 0)
     re_even, im_even, re_odd, im_odd = quarters(image)
     image = cat(
         moved(cat(re_even, re_odd), part_ref[...]), moved(cat(im_even, im_odd), part_ref[...])
     )
-    out_ref[:, 0] = jnp.swapaxes(image.reshape(own_ref.shape), 0, 1)
+    out_ref[:, 0] = jnp.swapaxes(image.reshape(one_ref.shape), 0, 1)
 
 
 def stages(blocks, cuts):
@@ -469,7 +478,7 @@
     inner, outer = stages(blocks, lax.axis_size("cuts"))
     cells = float(frames_all * slices_all * readout * positions)
     tables = jnp.asarray(line_tables(positions))
-    time_fore, time_back = (jnp.asarray(table) for table in time_tables(frames_all, frames_here))
+    time_fore, time_back, time_across = (jnp.asarray(table) for table in time_tables(frames_all, frames_here))
     parting = parting_table(positions)
     part, unpart = jnp.asarray(parting, BF16), jnp.asarray(parting.T, BF16)
     plane = (readout, frames_here, doubled)
@@ -565,20 +574,23 @@
         ],
         time_flops // 2,
     )
-    all_blocks = gathered(bar_x)
+    one, two, three = gathered(bar_x)[1:]
     pair_near, pair_far = neighbours(bar_x)
     normal_bar = normal(bar)
-    field = call(
-        last_time_kernel,
-        [rms_level] + all_blocks + [time_dual, time_fore, time_back],
-        struct(*plane),
-        time_flops,
+    partial, base = call(
+        middle_kernel,
+        [
+            rms_level, pair_near, pair_far, bar_x, two, three, normal_bar, base, time_dual,
+            space_dual, space_below, time_fore,
+        ],
+        [dual_shape, struct(*plane)],
+        time_flops // 2,
     )
     return call(
-        last_space_kernel,
-        [rms_level, bar_x, pair_near, pair_far, normal_bar, field, base, space_dual, space_below, unpart],
+        last_kernel,
+        [rms_level, one, partial, base, time_across, time_back, unpart],
         struct(frames_here, slices_here, readout, doubled),
-        1000000,
+        time_flops // 2,
     )
 
 

time: 56.1 us -> 55.7 us (level)
  transfers between devices with their start and end apart: 12 -> 12, of which waited for: 3 -> 3; matrix products, arithmetic and copies ran while one was open for 0% -> 0% of each run, Pallas kernels for 20% -> 21%
where the time goes in v4:
time: 55.7 us; the launch traced here: 55.3 us
  starting transfers between devices  31.2 us (56%)
  Pallas kernels  19.4 us (35%)
  waiting for transfers between devices  3.46 us (6%)
  local copies, waits for them, and re-layouts  0.99 us (2%)
    pallas_call x2, Pallas kernels, normal(): pl.pallas_call(kernel, in_specs=[vmem] * (4 + len(after)), out_specs=vmem...  9.39 us
    ppermute x4, starting transfers between devices, neighbours(): return [lax.ppermute(image, 'cuts', pair) for pair in pairs]  8.63 us
    all_to_all x1, starting transfers between devices, shards(): lax.all_to_all(energies, AXES, 0, 0, tiled=True, axis_index_groups=outer)  8.24 us
    all_to_all x1, starting transfers between devices, shards(): lax.all_to_all(energy, AXES, 0, 0, tiled=True, axis_index_groups=inner)  7.6 us
    ppermute x6, starting transfers between devices, swapped(): lax.ppermute(image, 'frame', [(index, index ^ by) for index in range(bloc...  6.77 us
    pallas_call x1, Pallas kernels, shards(): pl.pallas_call(initial_kernel, in_specs=[hbm] * 5, out_specs=[vmem] * 2 +...  5.36 us
    pallas_call x5, Pallas kernels, call(): pl.pallas_call(kernel, in_specs=[vmem] * len(args), out_specs=jax.tree.ma...  4.65 us
    ppermute x6, waiting for transfers between devices, swapped(): lax.ppermute(image, 'frame', [(index, index ^ by) for index in range(bloc...  1.75 us
  transfers between devices with their start and end apart: 12, of which 3 were waited for; matrix products, arithmetic and copies ran while one was open for 0% of the time, Pallas kernels for 21%

profile of v4, /device:TPU:1, one launch (start us, length us, event | category | flops | bytes accessed | tf_op | source)
XLA Modules:
  0.0 55.3 jit_solution(14758504259597632055)
XLA Ops:
  0.0 5.4 %shard_map.91 = (f32[16,8,512]{2,1,0:T(8,128)S(1)}, f32[8,16,512]{2,1,0:T(8,128)S(1)}, f32[16,128]{1,0:T(8,128)}, f32[20,8,512]{2,1,0:T(8,128)S(1)}, bf16[4,256,...) custom-call(f32[16,1,20,8,512]{4,3,2,1,0:T(8,128)} %measured_hbm.1, f32[1,20,8,512]{3,2,1,0:T(8,128)} %maps_hbm.1, ...), custom_call_target="tpu_custom_call" | custom-call | flops 2013265920 | bytes 5242880 | tf_op jit(solution)/shard_map/pallas_call | solution.py:490
  5.4 7.6 %all-to-all-start = ((f32[16,1,128]{2,1,0:T(1,128)}), f32[16,1,128]{2,1,0:T(1,128)S(1)}, u32[]{:S(2)}, u32[]{:S(2)}) async-start(f32[16,1,128]{2,1,0:T(1,128)} %bitcast.1), calls=%async_computation | async-start | bytes 16384 | tf_op jit(solution)/shard_map/all_to_all | solution.py:553
  13.0 2.6 %collective-permute-start.4 = (f32[8,16,512]{2,1,0:T(8,128)S(1)}, f32[8,16,512]{2,1,0:T(8,128)S(1)}, u32[]{:S(2)}, u32[]{:S(2)}) collective-permute-start(f32[8,16,512]{2,1,0:T(8,128)S(1)} %get-tuple-element.21.own_ref.refs_1_), channel_id=1, source_target_pairs={{0,192},{64,128},{128,64},{192,0},{1,193},{65,129},{129,65},{193,1... | collective-permute-start | bytes 786440 | tf_op jit(solution)/shard_map/ppermute | solution.py:532
  15.6 0.6 %collective-permute-start.3 = (f32[8,16,512]{2,1,0:T(8,128)S(1)}, f32[8,16,512]{2,1,0:T(8,128)S(1)}, u32[]{:S(2)}, u32[]{:S(2)}) collective-permute-start(f32[8,16,512]{2,1,0:T(8,128)S(1)} %get-tuple-element.21.own_ref.refs_1_), channel_id=1, source_target_pairs={{0,128},{64,192},{128,0},{192,64},{1,129},{65,193},{129,1},{193,65... | collective-permute-start | bytes 786440 | tf_op jit(solution)/shard_map/ppermute | solution.py:532
  16.1 0.2 collective-permute-start.2
  16.3 5.2 %collective-permute-start.1 = (f32[8,16,512]{2,1,0:T(8,128)S(1)}, f32[8,16,512]{2,1,0:T(8,128)S(1)}, u32[]{:S(2)}, u32[]{:S(2)}) collective-permute-start(f32[8,16,512]{2,1,0:T(8,128)S(1)} %get-tuple-element.21.own_ref.refs_1_), channel_id=1, source_target_pairs={{1,2},{2,1},{3,4},{4,3},{5,6},{6,5},{7,8},{8,7},{9,10},{10,9},{11,... | collective-permute-start | bytes 786440 | tf_op jit(solution)/shard_map/ppermute | solution.py:540
  21.5 0.1 collective-permute-start
  21.6 0.0 all-to-all-done
  21.6 0.6 %shard_map.92 = f32[16,128]{1,0:T(8,128)} custom-call(f32[16,128]{1,0:T(8,128)S(1)} %bitcast.9), custom_call_target="tpu_custom_call" | custom-call | flops 1000 | bytes 8192 | tf_op jit(solution)/shard_map/pallas_call | solution.py:544
  22.2 8.2 %all-to-all-start.1 = ((f32[16,1,128]{2,1,0:T(1,128)}), f32[16,1,128]{2,1,0:T(1,128)S(1)}, u32[]{:S(2)}, u32[]{:S(2)}) async-start(f32[16,1,128]{2,1,0:T(1,128)} %bitcast.4), calls=%async_computation.1 | async-start | bytes 16384 | tf_op jit(solution)/shard_map/all_to_all | solution.py:555
  30.5 0.0 copy-start.2
  30.5 4.7 %shard_map.93.refs_4_ = f32[16,8,512]{2,1,0:T(8,128)S(1)} custom-call(f32[16,8,512]{2,1,0:T(8,128)S(1)} %get-tuple-element.22.refs_0_, f32[20,8,512]{2,1,0:T(8,128)S(1)} %get-tuple-element.23.refs_1_, s32[16,256]{1,0:T(8,128)S(1)} %get-tuple-element.24.refs_2_, bf16[4,256,256]{2,1,0:T(8,128)(2,1)S(1)} %get-tuple-element.25.refs_3_), custom_call_target="tpu_custom_call" | custom-call | flops 4026531840 | bytes 1000000 | tf_op jit(solution)/shard_map/pallas_call | solution.py:519
  35.2 0.0 collective-permute-done.4.three_ref
  35.2 0.0 collective-permute-done.3.two_ref
  35.2 0.0 collective-permute-done.2.one_ref
  35.3 0.5 shard_map.94.refs_5_
  35.7 1.7 %all-to-all-done.1 = f32[16,1,128]{2,1,0:T(1,128)S(1)} async-done(((f32[16,1,128]{2,1,0:T(1,128)}), f32[16,1,128]{2,1,0:T(1,128)S(1)}, u32[]{:S(2)}, u32[]{:S(2)}) %all-to-all-start.1) | async-done | bytes 8224 | tf_op jit(solution)/shard_map/all_to_all | solution.py:555
  37.4 0.0 collective-permute-done.1.refs_3_
  37.4 0.0 collective-permute-done.refs_2_
  37.4 1.0 %shard_map.95 = (f32[8,16,512]{2,1,0:T(8,128)S(1)}, f32[8,16,512]{2,1,0:T(8,128)S(1)}, f32[16,8,512]{2,1,0:T(8,128)S(1)}, f32[8,128,256]{2,1,0:T(8,128)S(1)}, f3...) custom-call(f32[16,128]{1,0:T(8,128)S(1)} %bitcast.8, ...), custom_call_target="tpu_custom_call" | custom-call | flops 117440512 | bytes 2154496 | tf_op jit(solution)/shard_map/pallas_call | solution.py:544
  38.4 2.7 %collective-permute-start.9 = (f32[8,16,512]{2,1,0:T(8,128)S(1)}, f32[8,16,512]{2,1,0:T(8,128)S(1)}, u32[]{:S(2)}, u32[]{:S(2)}) collective-permute-start(f32[8,16,512]{2,1,0:T(8,128)S(1)} %get-tuple-element.27.own_ref), channel_id=1, source_target_pairs={{0,192},{64,128},{128,64},{192,0},{1,193},{65,129},{129,65},{193,1... | collective-permute-start | bytes 786440 | tf_op jit(solution)/shard_map/ppermute | solution.py:532
  41.1 0.6 %collective-permute-start.8 = (f32[8,16,512]{2,1,0:T(8,128)S(1)}, f32[8,16,512]{2,1,0:T(8,128)S(1)}, u32[]{:S(2)}, u32[]{:S(2)}) collective-permute-start(f32[8,16,512]{2,1,0:T(8,128)S(1)} %get-tuple-element.27.own_ref), channel_id=1, source_target_pairs={{0,128},{64,192},{128,0},{192,64},{1,129},{65,193},{129,1},{193,65... | collective-permute-start | bytes 786440 | tf_op jit(solution)/shard_map/ppermute | solution.py:532
  41.7 3.3 %collective-permute-start.7 = (f32[8,16,512]{2,1,0:T(8,128)S(1)}, f32[8,16,512]{2,1,0:T(8,128)S(1)}, u32[]{:S(2)}, u32[]{:S(2)}) collective-permute-start(f32[8,16,512]{2,1,0:T(8,128)S(1)} %get-tuple-element.27.own_ref), channel_id=1, source_target_pairs={{1,2},{2,1},{3,4},{4,3},{5,6},{6,5},{7,8},{8,7},{9,10},{10,9},{11,... | collective-permute-start | bytes 786440 | tf_op jit(solution)/shard_map/ppermute | solution.py:540
  45.0 0.1 collective-permute-start.6
  45.1 0.1 collective-permute-start.5
  45.2 1.0 %copy-done.5 = f32[20,8,512]{2,1,0:T(8,128)S(1)} copy-done((f32[20,8,512]{2,1,0:T(8,128)S(1)}, f32[20,8,512]{2,1,0:T(8,128)}, u32[]{:S(2)}) %copy-start.5) | copy-done | bytes 327704
  46.2 4.7 %shard_map.96.normal_ref = f32[16,8,512]{2,1,0:T(8,128)S(1)} custom-call(f32[16,8,512]{2,1,0:T(8,128)S(1)} %get-tuple-element.28.refs_0_, f32[20,8,512]{2,1,0:T(8,128)S(1)} %copy-done.5, s32[16,256]{1,0:T(8,128)S(1)} %get-tuple-element.24.refs_2_, bf16[4,256,256]{2,1,0:T(8,128)(2,1)S(1)} %get-tuple-element.25.refs_3_), custom_call_target="tpu_custom_call" | custom-call | flops 4026531840 | bytes 1000000 | tf_op jit(solution)/shard_map/pallas_call | solution.py:519
  50.9 1.6 %collective-permute-done.9.three_ref = f32[8,16,512]{2,1,0:T(8,128)S(1)} collective-permute-done((f32[8,16,512]{2,1,0:T(8,128)S(1)}, f32[8,16,512]{2,1,0:T(8,128)S(1)}, u32[]{:S(2)}, u32[]{:S(2)}) %collective-permute-start.9) | collective-permute-done | bytes 262176 | tf_op jit(solution)/shard_map/ppermute | solution.py:532
  52.5 0.0 collective-permute-done.8.two_ref
  52.5 0.9 %shard_map.97 = (f32[8,128,256]{2,1,0:T(8,128)S(1)}, f32[8,16,512]{2,1,0:T(8,128)S(1)}) custom-call(f32[8,128]{1,0:T(8,128)S(1)} %get-tuple-element.26.level_ref, f32[8,16,512]{2,1,0:T(8,128)S(1)} %collective-permute-done.6.near_ref, f32[8,16,512]{2,1,0:T(8,128)S(1)} %collective-permute-done.7.far_ref, f32[8,16,512]{2,1,0:T(8,128)S(1)} %get-tuple-element.27.own_ref, ...), custom_call_target="tpu_custom_call" | custom-call | flops 117440512 | bytes 4657152 | tf_op jit(solution)/shard_map/pallas_call | solution.py:544
  53.4 0.1 collective-permute-done.5.one_ref
  53.5 1.7 %shard_map.98 = f32[16,1,8,512]{3,2,1,0:T(8,128)} custom-call(f32[8,128]{1,0:T(8,128)S(1)} %get-tuple-element.26.level_ref, f32[8,16,512]{2,1,0:T(8,128)S(1)} %collective-permute-done.5.one_ref, f32[8,128,256]{2,1,0:T(8,128)S(1)} %get-tuple-element.33.partial_ref, f32[8,16,512]{2,1,0:T(8,128)S(1)} %get-tuple-element.34.base_ref, ...), custom_call_target="tpu_custom_call" | custom-call | flops 117440512 | bytes 1986560 | tf_op jit(solution)/shard_map/pallas_call | solution.py:544
  (12 shorter events, 0.0 us)
Async XLA Ops:
  5.4 29.8 %copy-start.4 = (f32[20,8,512]{2,1,0:T(8,128)}, f32[20,8,512]{2,1,0:T(8,128)S(1)}, u32[]{:S(2)}) copy-start(f32[20,8,512]{2,1,0:T(8,128)S(1)} %get-tuple-element.23.refs_1_) | copy-start | bytes 983044
  5.4 16.2 %all-to-all-start = ((f32[16,1,128]{2,1,0:T(1,128)}), f32[16,1,128]{2,1,0:T(1,128)S(1)}, u32[]{:S(2)}, u32[]{:S(2)}) async-start(f32[16,1,128]{2,1,0:T(1,128)} %bitcast.1), calls=%async_computation | async-start | bytes 16384 | tf_op jit(solution)/shard_map/all_to_all | solution.py:553
  13.0 22.2 %collective-permute-start.4 = (f32[8,16,512]{2,1,0:T(8,128)S(1)}, f32[8,16,512]{2,1,0:T(8,128)S(1)}, u32[]{:S(2)}, u32[]{:S(2)}) collective-permute-start(f32[8,16,512]{2,1,0:T(8,128)S(1)} %get-tuple-element.21.own_ref.refs_1_), channel_id=1, source_target_pairs={{0,192},{64,128},{128,64},{192,0},{1,193},{65,129},{129,65},{193,1... | collective-permute-start | bytes 786440 | tf_op jit(solution)/shard_map/ppermute | solution.py:532
  15.6 19.7 %collective-permute-start.3 = (f32[8,16,512]{2,1,0:T(8,128)S(1)}, f32[8,16,512]{2,1,0:T(8,128)S(1)}, u32[]{:S(2)}, u32[]{:S(2)}) collective-permute-start(f32[8,16,512]{2,1,0:T(8,128)S(1)} %get-tuple-element.21.own_ref.refs_1_), channel_id=1, source_target_pairs={{0,128},{64,192},{128,0},{192,64},{1,129},{65,193},{129,1},{193,65... | collective-permute-start | bytes 786440 | tf_op jit(solution)/shard_map/ppermute | solution.py:532
  16.1 19.1 %collective-permute-start.2 = (f32[8,16,512]{2,1,0:T(8,128)S(1)}, f32[8,16,512]{2,1,0:T(8,128)S(1)}, u32[]{:S(2)}, u32[]{:S(2)}) collective-permute-start(f32[8,16,512]{2,1,0:T(8,128)S(1)} %get-tuple-element.21.own_ref.refs_1_), channel_id=1, source_target_pairs={{0,64},{64,0},{128,192},{192,128},{1,65},{65,1},{129,193},{193,129... | collective-permute-start | bytes 786440 | tf_op jit(solution)/shard_map/ppermute | solution.py:532
  16.3 21.1 %collective-permute-start.1 = (f32[8,16,512]{2,1,0:T(8,128)S(1)}, f32[8,16,512]{2,1,0:T(8,128)S(1)}, u32[]{:S(2)}, u32[]{:S(2)}) collective-permute-start(f32[8,16,512]{2,1,0:T(8,128)S(1)} %get-tuple-element.21.own_ref.refs_1_), channel_id=1, source_target_pairs={{1,2},{2,1},{3,4},{4,3},{5,6},{6,5},{7,8},{8,7},{9,10},{10,9},{11,... | collective-permute-start | bytes 786440 | tf_op jit(solution)/shard_map/ppermute | solution.py:540
  21.5 15.9 %collective-permute-start = (f32[8,16,512]{2,1,0:T(8,128)S(1)}, f32[8,16,512]{2,1,0:T(8,128)S(1)}, u32[]{:S(2)}, u32[]{:S(2)}) collective-permute-start(f32[8,16,512]{2,1,0:T(8,128)S(1)} %get-tuple-element.21.own_ref.refs_1_), channel_id=1, source_target_pairs={{0,1},{1,0},{2,3},{3,2},{4,5},{5,4},{6,7},{7,6},{8,9},{9,8},{10,11... | collective-permute-start | bytes 786440 | tf_op jit(solution)/shard_map/ppermute | solution.py:540
  22.2 15.2 %all-to-all-start.1 = ((f32[16,1,128]{2,1,0:T(1,128)}), f32[16,1,128]{2,1,0:T(1,128)S(1)}, u32[]{:S(2)}, u32[]{:S(2)}) async-start(f32[16,1,128]{2,1,0:T(1,128)} %bitcast.4), calls=%async_computation.1 | async-start | bytes 16384 | tf_op jit(solution)/shard_map/all_to_all | solution.py:555
  30.5 4.8 %copy-start = (bf16[128,384]{1,0:T(8,128)(2,1)S(1)}, bf16[128,384]{1,0:T(8,128)(2,1)}, u32[]{:S(2)}) copy-start(bf16[128,384]{1,0:T(8,128)(2,1)} %constant.13.clone.fore_ref) | copy-start | bytes 294916
  30.5 6.9 %copy-start.2 = (bf16[32,384]{1,0:T(8,128)(2,1)S(1)}, bf16[32,384]{1,0:T(8,128)(2,1)}, u32[]{:S(2)}) copy-start(bf16[32,384]{1,0:T(8,128)(2,1)} %constant.14.clone.refs_6_.back_ref) | copy-start | bytes 73732
  38.4 14.1 %collective-permute-start.9 = (f32[8,16,512]{2,1,0:T(8,128)S(1)}, f32[8,16,512]{2,1,0:T(8,128)S(1)}, u32[]{:S(2)}, u32[]{:S(2)}) collective-permute-start(f32[8,16,512]{2,1,0:T(8,128)S(1)} %get-tuple-element.27.own_ref), channel_id=1, source_target_pairs={{0,192},{64,128},{128,64},{192,0},{1,193},{65,129},{129,65},{193,1... | collective-permute-start | bytes 786440 | tf_op jit(solution)/shard_map/ppermute | solution.py:532
  41.1 11.4 %collective-permute-start.8 = (f32[8,16,512]{2,1,0:T(8,128)S(1)}, f32[8,16,512]{2,1,0:T(8,128)S(1)}, u32[]{:S(2)}, u32[]{:S(2)}) collective-permute-start(f32[8,16,512]{2,1,0:T(8,128)S(1)} %get-tuple-element.27.own_ref), channel_id=1, source_target_pairs={{0,128},{64,192},{128,0},{192,64},{1,129},{65,193},{129,1},{193,65... | collective-permute-start | bytes 786440 | tf_op jit(solution)/shard_map/ppermute | solution.py:532
  41.7 10.8 %collective-permute-start.7 = (f32[8,16,512]{2,1,0:T(8,128)S(1)}, f32[8,16,512]{2,1,0:T(8,128)S(1)}, u32[]{:S(2)}, u32[]{:S(2)}) collective-permute-start(f32[8,16,512]{2,1,0:T(8,128)S(1)} %get-tuple-element.27.own_ref), channel_id=1, source_target_pairs={{1,2},{2,1},{3,4},{4,3},{5,6},{6,5},{7,8},{8,7},{9,10},{10,9},{11,... | collective-permute-start | bytes 786440 | tf_op jit(solution)/shard_map/ppermute | solution.py:540
  45.0 7.5 %collective-permute-start.6 = (f32[8,16,512]{2,1,0:T(8,128)S(1)}, f32[8,16,512]{2,1,0:T(8,128)S(1)}, u32[]{:S(2)}, u32[]{:S(2)}) collective-permute-start(f32[8,16,512]{2,1,0:T(8,128)S(1)} %get-tuple-element.27.own_ref), channel_id=1, source_target_pairs={{0,1},{1,0},{2,3},{3,2},{4,5},{5,4},{6,7},{7,6},{8,9},{9,8},{10,11... | collective-permute-start | bytes 786440 | tf_op jit(solution)/shard_map/ppermute | solution.py:540
  45.1 8.5 %collective-permute-start.5 = (f32[8,16,512]{2,1,0:T(8,128)S(1)}, f32[8,16,512]{2,1,0:T(8,128)S(1)}, u32[]{:S(2)}, u32[]{:S(2)}) collective-permute-start(f32[8,16,512]{2,1,0:T(8,128)S(1)} %get-tuple-element.27.own_ref), channel_id=1, source_target_pairs={{0,64},{64,0},{128,192},{192,128},{1,65},{65,1},{129,193},{193,129... | collective-permute-start | bytes 786440 | tf_op jit(solution)/shard_map/ppermute | solution.py:532
  45.2 1.0 %copy-start.5 = (f32[20,8,512]{2,1,0:T(8,128)S(1)}, f32[20,8,512]{2,1,0:T(8,128)}, u32[]{:S(2)}) copy-start(f32[20,8,512]{2,1,0:T(8,128)} %copy-done.4) | copy-start | bytes 983044
  46.2 7.4 %copy-start.1 = (bf16[256,256]{1,0:T(8,128)(2,1)S(1)}, bf16[256,256]{1,0:T(8,128)(2,1)}, u32[]{:S(2)}) copy-start(bf16[256,256]{1,0:T(8,128)(2,1)} %constant.17.clone.part_ref) | copy-start | bytes 393220
  46.2 7.4 %copy-start.3 = (bf16[2,128,96]{2,1,0:T(8,128)(2,1)S(1)}, bf16[2,128,96]{2,1,0:T(8,128)(2,1)}, u32[]{:S(2)}) copy-start(bf16[2,128,96]{2,1,0:T(8,128)(2,1)} %constant.15.clone.across_ref) | copy-start | bytes 147460

commit v5 on v4

--- a/solution.py
+++ b/solution.py
@@ -411,7 +411,7 @@
 
 
 def middle_kernel(
-    level_ref, near_ref, far_ref, own_ref, two_ref, three_ref, normal_ref, base_ref, dual_ref,
+    level_ref, near_ref, far_ref, own_ref, three_ref, two_ref, normal_ref, base_ref, dual_ref,
     space_ref, space_below_ref, fore_ref,
     partial_ref, out_ref,
 ):
@@ -580,7 +580,7 @@
     partial, base = call(
         middle_kernel,
         [
-            rms_level, pair_near, pair_far, bar_x, two, three, normal_bar, base, time_dual,
+            rms_level, pair_near, pair_far, bar_x, three, two, normal_bar, base, time_dual,
             space_dual, space_below, time_fore,
         ],
         [dual_shape, struct(*plane)],

time: 55.7 us -> 56.8 us (1.020)
  waiting for transfers between devices: 3.46 us -> 4.09 us
  starting transfers between devices: 31.2 us -> 31.8 us
    ppermute x6, waiting for transfers between devices: 1.75 us -> 2.38 us  [swapped(): lax.ppermute(image, 'frame', [(index, index ^ by) for index in range(bloc...]
  transfers between devices with their start and end apart: 12 -> 12, of which waited for: 3 -> 2; matrix products, arithmetic and copies ran while one was open for 0% -> 0% of each run, Pallas kernels for 21% -> 20%
where the time goes in v5:
time: 56.8 us; the launch traced here: 56.5 us
  starting transfers between devices  31.8 us (56%)
  Pallas kernels  19.4 us (34%)
  waiting for transfers between devices  4.09 us (7%)
  local copies, waits for them, and re-layouts  0.99 us (2%)
    pallas_call x2, Pallas kernels, normal(): pl.pallas_call(kernel, in_specs=[vmem] * (4 + len(after)), out_specs=vmem...  9.39 us
    ppermute x4, starting transfers between devices, neighbours(): return [lax.ppermute(image, 'cuts', pair) for pair in pairs]  8.63 us
    all_to_all x1, starting transfers between devices, shards(): lax.all_to_all(energies, AXES, 0, 0, tiled=True, axis_index_groups=outer)  8.24 us
    all_to_all x1, starting transfers between devices, shards(): lax.all_to_all(energy, AXES, 0, 0, tiled=True, axis_index_groups=inner)  7.6 us
    ppermute x6, starting transfers between devices, swapped(): lax.ppermute(image, 'frame', [(index, index ^ by) for index in range(bloc...  7.33 us
    pallas_call x1, Pallas kernels, shards(): pl.pallas_call(initial_kernel, in_specs=[hbm] * 5, out_specs=[vmem] * 2 +...  5.36 us
    pallas_call x5, Pallas kernels, call(): pl.pallas_call(kernel, in_specs=[vmem] * len(args), out_specs=jax.tree.ma...  4.62 us
    ppermute x6, waiting for transfers between devices, swapped(): lax.ppermute(image, 'frame', [(index, index ^ by) for index in range(bloc...  2.38 us
  transfers between devices with their start and end apart: 12, of which 2 were waited for; matrix products, arithmetic and copies ran while one was open for 0% of the time, Pallas kernels for 20%

profile of v5, /device:TPU:1, one launch (start us, length us, event | category | flops | bytes accessed | tf_op | source)
XLA Modules:
  0.0 56.5 jit_solution(4807504733582892566)
XLA Ops:
  0.0 5.4 %shard_map.91 = (f32[16,8,512]{2,1,0:T(8,128)S(1)}, f32[8,16,512]{2,1,0:T(8,128)S(1)}, f32[16,128]{1,0:T(8,128)}, f32[20,8,512]{2,1,0:T(8,128)S(1)}, bf16[4,256,...) custom-call(f32[16,1,20,8,512]{4,3,2,1,0:T(8,128)} %measured_hbm.1, f32[1,20,8,512]{3,2,1,0:T(8,128)} %maps_hbm.1, ...), custom_call_target="tpu_custom_call" | custom-call | flops 2013265920 | bytes 5242880 | tf_op jit(solution)/shard_map/pallas_call | solution.py:490
  5.4 7.6 %all-to-all-start = ((f32[16,1,128]{2,1,0:T(1,128)}), f32[16,1,128]{2,1,0:T(1,128)S(1)}, u32[]{:S(2)}, u32[]{:S(2)}) async-start(f32[16,1,128]{2,1,0:T(1,128)} %bitcast.1), calls=%async_computation | async-start | bytes 16384 | tf_op jit(solution)/shard_map/all_to_all | solution.py:553
  13.0 2.6 %collective-permute-start.4 = (f32[8,16,512]{2,1,0:T(8,128)S(1)}, f32[8,16,512]{2,1,0:T(8,128)S(1)}, u32[]{:S(2)}, u32[]{:S(2)}) collective-permute-start(f32[8,16,512]{2,1,0:T(8,128)S(1)} %get-tuple-element.21.own_ref.refs_1_), channel_id=1, source_target_pairs={{0,192},{64,128},{128,64},{192,0},{1,193},{65,129},{129,65},{193,1... | collective-permute-start | bytes 786440 | tf_op jit(solution)/shard_map/ppermute | solution.py:532
  15.6 0.6 %collective-permute-start.3 = (f32[8,16,512]{2,1,0:T(8,128)S(1)}, f32[8,16,512]{2,1,0:T(8,128)S(1)}, u32[]{:S(2)}, u32[]{:S(2)}) collective-permute-start(f32[8,16,512]{2,1,0:T(8,128)S(1)} %get-tuple-element.21.own_ref.refs_1_), channel_id=1, source_target_pairs={{0,128},{64,192},{128,0},{192,64},{1,129},{65,193},{129,1},{193,65... | collective-permute-start | bytes 786440 | tf_op jit(solution)/shard_map/ppermute | solution.py:532
  16.1 0.2 collective-permute-start.2
  16.3 5.2 %collective-permute-start.1 = (f32[8,16,512]{2,1,0:T(8,128)S(1)}, f32[8,16,512]{2,1,0:T(8,128)S(1)}, u32[]{:S(2)}, u32[]{:S(2)}) collective-permute-start(f32[8,16,512]{2,1,0:T(8,128)S(1)} %get-tuple-element.21.own_ref.refs_1_), channel_id=1, source_target_pairs={{1,2},{2,1},{3,4},{4,3},{5,6},{6,5},{7,8},{8,7},{9,10},{10,9},{11,... | collective-permute-start | bytes 786440 | tf_op jit(solution)/shard_map/ppermute | solution.py:540
  21.5 0.1 collective-permute-start
  21.6 0.0 all-to-all-done
  21.6 0.6 %shard_map.92 = f32[16,128]{1,0:T(8,128)} custom-call(f32[16,128]{1,0:T(8,128)S(1)} %bitcast.9), custom_call_target="tpu_custom_call" | custom-call | flops 1000 | bytes 8192 | tf_op jit(solution)/shard_map/pallas_call | solution.py:544
  22.2 8.2 %all-to-all-start.1 = ((f32[16,1,128]{2,1,0:T(1,128)}), f32[16,1,128]{2,1,0:T(1,128)S(1)}, u32[]{:S(2)}, u32[]{:S(2)}) async-start(f32[16,1,128]{2,1,0:T(1,128)} %bitcast.4), calls=%async_computation.1 | async-start | bytes 16384 | tf_op jit(solution)/shard_map/all_to_all | solution.py:555
  30.5 0.0 copy-start.2
  30.5 4.7 %shard_map.93.refs_4_ = f32[16,8,512]{2,1,0:T(8,128)S(1)} custom-call(f32[16,8,512]{2,1,0:T(8,128)S(1)} %get-tuple-element.22.refs_0_, f32[20,8,512]{2,1,0:T(8,128)S(1)} %get-tuple-element.23.refs_1_, s32[16,256]{1,0:T(8,128)S(1)} %get-tuple-element.24.refs_2_, bf16[4,256,256]{2,1,0:T(8,128)(2,1)S(1)} %get-tuple-element.25.refs_3_), custom_call_target="tpu_custom_call" | custom-call | flops 4026531840 | bytes 1000000 | tf_op jit(solution)/shard_map/pallas_call | solution.py:519
  35.2 0.0 collective-permute-done.4.three_ref
  35.2 0.0 collective-permute-done.3.two_ref
  35.2 0.0 collective-permute-done.2.one_ref
  35.3 0.5 shard_map.94.refs_5_
  35.7 1.7 %all-to-all-done.1 = f32[16,1,128]{2,1,0:T(1,128)S(1)} async-done(((f32[16,1,128]{2,1,0:T(1,128)}), f32[16,1,128]{2,1,0:T(1,128)S(1)}, u32[]{:S(2)}, u32[]{:S(2)}) %all-to-all-start.1) | async-done | bytes 8224 | tf_op jit(solution)/shard_map/all_to_all | solution.py:555
  37.4 1.0 %shard_map.95 = (f32[8,16,512]{2,1,0:T(8,128)S(1)}, f32[8,16,512]{2,1,0:T(8,128)S(1)}, f32[16,8,512]{2,1,0:T(8,128)S(1)}, f32[8,128,256]{2,1,0:T(8,128)S(1)}, f3...) custom-call(f32[16,128]{1,0:T(8,128)S(1)} %bitcast.8, ...), custom_call_target="tpu_custom_call" | custom-call | flops 117440512 | bytes 2154496 | tf_op jit(solution)/shard_map/pallas_call | solution.py:544
  38.4 3.0 %collective-permute-start.9 = (f32[8,16,512]{2,1,0:T(8,128)S(1)}, f32[8,16,512]{2,1,0:T(8,128)S(1)}, u32[]{:S(2)}, u32[]{:S(2)}) collective-permute-start(f32[8,16,512]{2,1,0:T(8,128)S(1)} %get-tuple-element.27.own_ref), channel_id=1, source_target_pairs={{0,128},{64,192},{128,0},{192,64},{1,129},{65,193},{129,1},{193,65... | collective-permute-start | bytes 786440 | tf_op jit(solution)/shard_map/ppermute | solution.py:532
  41.4 0.9 %collective-permute-start.8 = (f32[8,16,512]{2,1,0:T(8,128)S(1)}, f32[8,16,512]{2,1,0:T(8,128)S(1)}, u32[]{:S(2)}, u32[]{:S(2)}) collective-permute-start(f32[8,16,512]{2,1,0:T(8,128)S(1)} %get-tuple-element.27.own_ref), channel_id=1, source_target_pairs={{0,192},{64,128},{128,64},{192,0},{1,193},{65,129},{129,65},{193,1... | collective-permute-start | bytes 786440 | tf_op jit(solution)/shard_map/ppermute | solution.py:532
  42.3 3.3 %collective-permute-start.7 = (f32[8,16,512]{2,1,0:T(8,128)S(1)}, f32[8,16,512]{2,1,0:T(8,128)S(1)}, u32[]{:S(2)}, u32[]{:S(2)}) collective-permute-start(f32[8,16,512]{2,1,0:T(8,128)S(1)} %get-tuple-element.27.own_ref), channel_id=1, source_target_pairs={{1,2},{2,1},{3,4},{4,3},{5,6},{6,5},{7,8},{8,7},{9,10},{10,9},{11,... | collective-permute-start | bytes 786440 | tf_op jit(solution)/shard_map/ppermute | solution.py:540
  45.6 0.1 collective-permute-start.6
  45.7 0.1 collective-permute-start.5
  45.8 1.0 %copy-done.5 = f32[20,8,512]{2,1,0:T(8,128)S(1)} copy-done((f32[20,8,512]{2,1,0:T(8,128)S(1)}, f32[20,8,512]{2,1,0:T(8,128)}, u32[]{:S(2)}) %copy-start.5) | copy-done | bytes 327704
  46.8 4.7 %shard_map.96.normal_ref = f32[16,8,512]{2,1,0:T(8,128)S(1)} custom-call(f32[16,8,512]{2,1,0:T(8,128)S(1)} %get-tuple-element.28.refs_0_, f32[20,8,512]{2,1,0:T(8,128)S(1)} %copy-done.5, s32[16,256]{1,0:T(8,128)S(1)} %get-tuple-element.24.refs_2_, bf16[4,256,256]{2,1,0:T(8,128)(2,1)S(1)} %get-tuple-element.25.refs_3_), custom_call_target="tpu_custom_call" | custom-call | flops 4026531840 | bytes 1000000 | tf_op jit(solution)/shard_map/pallas_call | solution.py:519
  51.5 0.0 collective-permute-done.9.two_ref
  51.5 2.4 %collective-permute-done.8.three_ref = f32[8,16,512]{2,1,0:T(8,128)S(1)} collective-permute-done((f32[8,16,512]{2,1,0:T(8,128)S(1)}, f32[8,16,512]{2,1,0:T(8,128)S(1)}, u32[]{:S(2)}, u32[]{:S(2)}) %collective-permute-start.8) | collective-permute-done | bytes 262176 | tf_op jit(solution)/shard_map/ppermute | solution.py:532
  53.8 0.0 collective-permute-done.7.far_ref
  53.8 0.0 collective-permute-done.6.near_ref
  53.8 0.9 %shard_map.97 = (f32[8,128,256]{2,1,0:T(8,128)S(1)}, f32[8,16,512]{2,1,0:T(8,128)S(1)}) custom-call(f32[8,128]{1,0:T(8,128)S(1)} %get-tuple-element.26.level_ref, f32[8,16,512]{2,1,0:T(8,128)S(1)} %collective-permute-done.6.near_ref, f32[8,16,512]{2,1,0:T(8,128)S(1)} %collective-permute-done.7.far_ref, f32[8,16,512]{2,1,0:T(8,128)S(1)} %get-tuple-element.27.own_ref, ...), custom_call_target="tpu_custom_call" | custom-call | flops 117440512 | bytes 4657152 | tf_op jit(solution)/shard_map/pallas_call | solution.py:544
  54.7 0.0 collective-permute-done.5.one_ref
  54.8 1.7 %shard_map.98 = f32[16,1,8,512]{3,2,1,0:T(8,128)} custom-call(f32[8,128]{1,0:T(8,128)S(1)} %get-tuple-element.26.level_ref, f32[8,16,512]{2,1,0:T(8,128)S(1)} %collective-permute-done.5.one_ref, f32[8,128,256]{2,1,0:T(8,128)S(1)} %get-tuple-element.33.partial_ref, f32[8,16,512]{2,1,0:T(8,128)S(1)} %get-tuple-element.34.base_ref, ...), custom_call_target="tpu_custom_call" | custom-call | flops 117440512 | bytes 1986560 | tf_op jit(solution)/shard_map/pallas_call | solution.py:544
  (12 shorter events, 0.0 us)
Async XLA Ops:
  5.4 29.8 %copy-start.4 = (f32[20,8,512]{2,1,0:T(8,128)}, f32[20,8,512]{2,1,0:T(8,128)S(1)}, u32[]{:S(2)}) copy-start(f32[20,8,512]{2,1,0:T(8,128)S(1)} %get-tuple-element.23.refs_1_) | copy-start | bytes 983044
  5.4 16.2 %all-to-all-start = ((f32[16,1,128]{2,1,0:T(1,128)}), f32[16,1,128]{2,1,0:T(1,128)S(1)}, u32[]{:S(2)}, u32[]{:S(2)}) async-start(f32[16,1,128]{2,1,0:T(1,128)} %bitcast.1), calls=%async_computation | async-start | bytes 16384 | tf_op jit(solution)/shard_map/all_to_all | solution.py:553
  13.0 22.2 %collective-permute-start.4 = (f32[8,16,512]{2,1,0:T(8,128)S(1)}, f32[8,16,512]{2,1,0:T(8,128)S(1)}, u32[]{:S(2)}, u32[]{:S(2)}) collective-permute-start(f32[8,16,512]{2,1,0:T(8,128)S(1)} %get-tuple-element.21.own_ref.refs_1_), channel_id=1, source_target_pairs={{0,192},{64,128},{128,64},{192,0},{1,193},{65,129},{129,65},{193,1... | collective-permute-start | bytes 786440 | tf_op jit(solution)/shard_map/ppermute | solution.py:532
  15.6 19.7 %collective-permute-start.3 = (f32[8,16,512]{2,1,0:T(8,128)S(1)}, f32[8,16,512]{2,1,0:T(8,128)S(1)}, u32[]{:S(2)}, u32[]{:S(2)}) collective-permute-start(f32[8,16,512]{2,1,0:T(8,128)S(1)} %get-tuple-element.21.own_ref.refs_1_), channel_id=1, source_target_pairs={{0,128},{64,192},{128,0},{192,64},{1,129},{65,193},{129,1},{193,65... | collective-permute-start | bytes 786440 | tf_op jit(solution)/shard_map/ppermute | solution.py:532
  16.1 19.1 %collective-permute-start.2 = (f32[8,16,512]{2,1,0:T(8,128)S(1)}, f32[8,16,512]{2,1,0:T(8,128)S(1)}, u32[]{:S(2)}, u32[]{:S(2)}) collective-permute-start(f32[8,16,512]{2,1,0:T(8,128)S(1)} %get-tuple-element.21.own_ref.refs_1_), channel_id=1, source_target_pairs={{0,64},{64,0},{128,192},{192,128},{1,65},{65,1},{129,193},{193,129... | collective-permute-start | bytes 786440 | tf_op jit(solution)/shard_map/ppermute | solution.py:532
  16.3 21.1 %collective-permute-start.1 = (f32[8,16,512]{2,1,0:T(8,128)S(1)}, f32[8,16,512]{2,1,0:T(8,128)S(1)}, u32[]{:S(2)}, u32[]{:S(2)}) collective-permute-start(f32[8,16,512]{2,1,0:T(8,128)S(1)} %get-tuple-element.21.own_ref.refs_1_), channel_id=1, source_target_pairs={{1,2},{2,1},{3,4},{4,3},{5,6},{6,5},{7,8},{8,7},{9,10},{10,9},{11,... | collective-permute-start | bytes 786440 | tf_op jit(solution)/shard_map/ppermute | solution.py:540
  21.5 15.9 %collective-permute-start = (f32[8,16,512]{2,1,0:T(8,128)S(1)}, f32[8,16,512]{2,1,0:T(8,128)S(1)}, u32[]{:S(2)}, u32[]{:S(2)}) collective-permute-start(f32[8,16,512]{2,1,0:T(8,128)S(1)} %get-tuple-element.21.own_ref.refs_1_), channel_id=1, source_target_pairs={{0,1},{1,0},{2,3},{3,2},{4,5},{5,4},{6,7},{7,6},{8,9},{9,8},{10,11... | collective-permute-start | bytes 786440 | tf_op jit(solution)/shard_map/ppermute | solution.py:540
  22.2 15.2 %all-to-all-start.1 = ((f32[16,1,128]{2,1,0:T(1,128)}), f32[16,1,128]{2,1,0:T(1,128)S(1)}, u32[]{:S(2)}, u32[]{:S(2)}) async-start(f32[16,1,128]{2,1,0:T(1,128)} %bitcast.4), calls=%async_computation.1 | async-start | bytes 16384 | tf_op jit(solution)/shard_map/all_to_all | solution.py:555
  30.5 4.8 %copy-start = (bf16[128,384]{1,0:T(8,128)(2,1)S(1)}, bf16[128,384]{1,0:T(8,128)(2,1)}, u32[]{:S(2)}) copy-start(bf16[128,384]{1,0:T(8,128)(2,1)} %constant.13.clone.fore_ref) | copy-start | bytes 294916
  30.5 6.9 %copy-start.2 = (bf16[32,384]{1,0:T(8,128)(2,1)S(1)}, bf16[32,384]{1,0:T(8,128)(2,1)}, u32[]{:S(2)}) copy-start(bf16[32,384]{1,0:T(8,128)(2,1)} %constant.14.clone.refs_6_.back_ref) | copy-start | bytes 73732
  38.4 13.1 %collective-permute-start.9 = (f32[8,16,512]{2,1,0:T(8,128)S(1)}, f32[8,16,512]{2,1,0:T(8,128)S(1)}, u32[]{:S(2)}, u32[]{:S(2)}) collective-permute-start(f32[8,16,512]{2,1,0:T(8,128)S(1)} %get-tuple-element.27.own_ref), channel_id=1, source_target_pairs={{0,128},{64,192},{128,0},{192,64},{1,129},{65,193},{129,1},{193,65... | collective-permute-start | bytes 786440 | tf_op jit(solution)/shard_map/ppermute | solution.py:532
  41.4 12.4 %collective-permute-start.8 = (f32[8,16,512]{2,1,0:T(8,128)S(1)}, f32[8,16,512]{2,1,0:T(8,128)S(1)}, u32[]{:S(2)}, u32[]{:S(2)}) collective-permute-start(f32[8,16,512]{2,1,0:T(8,128)S(1)} %get-tuple-element.27.own_ref), channel_id=1, source_target_pairs={{0,192},{64,128},{128,64},{192,0},{1,193},{65,129},{129,65},{193,1... | collective-permute-start | bytes 786440 | tf_op jit(solution)/shard_map/ppermute | solution.py:532
  42.3 11.5 %collective-permute-start.7 = (f32[8,16,512]{2,1,0:T(8,128)S(1)}, f32[8,16,512]{2,1,0:T(8,128)S(1)}, u32[]{:S(2)}, u32[]{:S(2)}) collective-permute-start(f32[8,16,512]{2,1,0:T(8,128)S(1)} %get-tuple-element.27.own_ref), channel_id=1, source_target_pairs={{1,2},{2,1},{3,4},{4,3},{5,6},{6,5},{7,8},{8,7},{9,10},{10,9},{11,... | collective-permute-start | bytes 786440 | tf_op jit(solution)/shard_map/ppermute | solution.py:540
  45.6 8.3 %collective-permute-start.6 = (f32[8,16,512]{2,1,0:T(8,128)S(1)}, f32[8,16,512]{2,1,0:T(8,128)S(1)}, u32[]{:S(2)}, u32[]{:S(2)}) collective-permute-start(f32[8,16,512]{2,1,0:T(8,128)S(1)} %get-tuple-element.27.own_ref), channel_id=1, source_target_pairs={{0,1},{1,0},{2,3},{3,2},{4,5},{5,4},{6,7},{7,6},{8,9},{9,8},{10,11... | collective-permute-start | bytes 786440 | tf_op jit(solution)/shard_map/ppermute | solution.py:540
  45.7 9.1 %collective-permute-start.5 = (f32[8,16,512]{2,1,0:T(8,128)S(1)}, f32[8,16,512]{2,1,0:T(8,128)S(1)}, u32[]{:S(2)}, u32[]{:S(2)}) collective-permute-start(f32[8,16,512]{2,1,0:T(8,128)S(1)} %get-tuple-element.27.own_ref), channel_id=1, source_target_pairs={{0,64},{64,0},{128,192},{192,128},{1,65},{65,1},{129,193},{193,129... | collective-permute-start | bytes 786440 | tf_op jit(solution)/shard_map/ppermute | solution.py:532
  45.8 1.0 %copy-start.5 = (f32[20,8,512]{2,1,0:T(8,128)S(1)}, f32[20,8,512]{2,1,0:T(8,128)}, u32[]{:S(2)}) copy-start(f32[20,8,512]{2,1,0:T(8,128)} %copy-done.4) | copy-start | bytes 983044
  46.7 8.0 %copy-start.1 = (bf16[256,256]{1,0:T(8,128)(2,1)S(1)}, bf16[256,256]{1,0:T(8,128)(2,1)}, u32[]{:S(2)}) copy-start(bf16[256,256]{1,0:T(8,128)(2,1)} %constant.17.clone.part_ref) | copy-start | bytes 393220
  46.7 8.0 %copy-start.3 = (bf16[2,128,96]{2,1,0:T(8,128)(2,1)S(1)}, bf16[2,128,96]{2,1,0:T(8,128)(2,1)}, u32[]{:S(2)}) copy-start(bf16[2,128,96]{2,1,0:T(8,128)(2,1)} %constant.15.clone.across_ref) | copy-start | bytes 147460
